TPU v7x, 32 devices: a whole 2x2x4 slice. The times are simulated.
32 devices in a mesh: groups: 2 (over y), replica: 4 (over x, core), trow: 4 (over z).
Axes of the slice: x: 2, y: 2, z: 4, core: 2. Of those that a mesh axis runs over, the one named last changes fastest.
Arguments:
- hidden: bfloat16 [5120, 8192], P(('groups', 'replica'), 'trow'), parts along dimension 0, may hold values from -36 to 36, as said below
- w_query: bfloat16 [8192, 4096], P('replica', 'trow'), as said below
- w_keyval: bfloat16 [8192, 8, 256], P('replica', 'trow'), as said below
- seg_lengths: int32 [8, 2], P(('groups', 'replica')), parts along dimension 0, may hold values from 128 to 512, as said below
- home_pos: int32 [5120], P('groups'), parts along dimension 0, may hold values from 0 to 2559, as said below
Outputs:
- attended: bfloat16 [5120, 4096], P(('groups', 'replica'), 'trow'), parts along dimension 0
There are 2 independent parts, one for each index of `groups`. A program takes and returns all parts, laid end to end along the dimension named above; an argument that names none is the same for every part. Nothing has to cross between parts.
Inputs may be any that keep to these rules, and one draw needn't show every extreme that they name: `hidden`: Floats. `w_query`: floats scaled by the inverse square root of 8192. `w_keyval`: floats scaled by the inverse square root of 8192. `seg_lengths`: each replica's 2 lengths sum to exactly 640; some replica has a segment of 512 tokens. `home_pos`: A permutation of the 2560 rows; the rows of each replica go in equal numbers to the home rows of every replica.
All inputs are finite; a program needn't handle non-finite values.
Results may differ from a plain program's by a relative error of at most 0.0068.
Values may be sent and summed in bfloat16 or wider, within the bound.
No kernel may reach another device: no remote copies, remote signals or barrier semaphores. Data moves between devices by JAX's collectives and lax.ppermute only.
A program may use at most 128 MiB of HBM per device.

v0:
```python
import math

import jax
import jax.numpy as jnp
from jax import lax
from jax.sharding import PartitionSpec as P

rope_base = 500000.0


def segment_layout(lengths_row, count):
    seg_ends = jnp.cumsum(lengths_row)
    seg_starts = seg_ends - lengths_row
    row_index = jnp.arange(count, dtype=jnp.int32)
    segment = jnp.sum((row_index[:, None] >= seg_ends[None, :]).astype(jnp.int32), axis=1)
    picked = segment[:, None] == jnp.arange(lengths_row.shape[0], dtype=jnp.int32)[None, :]
    seg_first = jnp.sum(jnp.where(picked, seg_starts[None, :], 0), axis=1)
    return (segment, row_index - seg_first)


def rotate(vectors, position):
    half_dim = vectors.shape[-1] // 2
    exponent = jnp.arange(half_dim, dtype=jnp.float32) * (2.0 / vectors.shape[-1])
    frequency = jnp.power(jnp.float32(rope_base), -exponent)
    angle = position.astype(jnp.float32)[:, None] * frequency[None, :]
    cosine = jnp.cos(angle)[:, None, :]
    sine = jnp.sin(angle)[:, None, :]
    first_half = vectors[..., :half_dim]
    second_half = vectors[..., half_dim:]
    return jnp.concatenate(
        [first_half * cosine - second_half * sine, second_half * cosine + first_half * sine],
        axis=-1,
    )


def attend(query, keys, values, segment, count):
    head_dim = keys.shape[2]
    grouped = query.reshape(count, keys.shape[1], -1, head_dim)
    scores = jnp.einsum(
        "qkgd,skd->kgqs", grouped, keys, preferred_element_type=jnp.float32
    ) / math.sqrt(head_dim)
    row_index = jnp.arange(count, dtype=jnp.int32)
    allowed = (segment[:, None] == segment[None, :]) & (row_index[None, :] <= row_index[:, None])
    scores = jnp.where(allowed[None, None], scores, -jnp.inf)
    peak = jnp.max(scores, axis=-1, keepdims=True)
    weights = jnp.exp(scores - peak)
    probs = (weights / jnp.sum(weights, axis=-1, keepdims=True)).astype(jnp.bfloat16)
    mixed = jnp.einsum("kgqs,skd->qkgd", probs, values, preferred_element_type=jnp.float32)
    return mixed.reshape(count, -1).astype(jnp.bfloat16)


def local(hidden, w_query, w_keyval, seg_lengths, home_pos):
    tok_rows = hidden.shape[0]
    kv_heads = w_keyval.shape[1]
    head_dim = w_keyval.shape[2] // 2
    query_cols = w_query.shape[1]
    keyval_cols = kv_heads * 2 * head_dim
    features = lax.all_gather(hidden, "trow", axis=1, tiled=True)
    pieces = (
        lax.all_gather(w_query, "replica", axis=0, tiled=True),
        lax.all_gather(w_keyval, "replica", axis=0, tiled=True),
    )
    width = pieces[0].shape[0]
    query_raw = jnp.dot(features, pieces[0], preferred_element_type=jnp.float32)
    keyval_raw = jnp.dot(
        features, pieces[1].reshape(width, keyval_cols), preferred_element_type=jnp.float32
    )
    segment, position = segment_layout(seg_lengths[0], tok_rows)
    query = rotate(query_raw.reshape(tok_rows, -1, head_dim), position).astype(jnp.bfloat16)
    keyval = keyval_raw.reshape(tok_rows, kv_heads, 2 * head_dim)
    keys = rotate(keyval[..., :head_dim], position).astype(jnp.bfloat16)
    values = keyval[..., head_dim:].astype(jnp.bfloat16)
    mixed = attend(query, keys, values, segment, tok_rows)
    replicas = lax.axis_size("replica")
    my_replica = lax.axis_index("replica")
    per_pair = tok_rows // replicas
    home_table = home_pos.reshape(replicas, tok_rows)
    owner_rep = home_table // tok_rows
    send_order = jnp.argsort(owner_rep, axis=1, stable=True)
    my_order = lax.dynamic_index_in_dim(send_order, my_replica, 0, keepdims=False)
    outgoing = jnp.take(mixed, my_order, axis=0).reshape(replicas, per_pair, query_cols)
    incoming = lax.all_to_all(outgoing, "replica", split_axis=0, concat_axis=0, tiled=True)
    sorted_home = jnp.take_along_axis(home_table, send_order, axis=1)
    targets = (
        lax.dynamic_slice_in_dim(sorted_home, my_replica * per_pair, per_pair, 1)
        - my_replica * tok_rows
    )
    result = jnp.zeros((tok_rows, query_cols), jnp.bfloat16)
    return result.at[targets.reshape(-1)].set(incoming.reshape(-1, query_cols))


def solution(mesh):
    placed = (
        P(("groups", "replica"), "trow"),
        P("replica", "trow"),
        P("replica", "trow", None),
        P(("groups", "replica"), None),
        P("groups"),
    )
    return jax.shard_map(
        local,
        mesh=mesh,
        in_specs=placed,
        out_specs=P(("groups", "replica"), "trow"),
        check_vma=False,
    )
```

profile of v0, /device:TPU:0, one launch (start us, length us, event | category | flops | bytes accessed | tf_op | source)
XLA Modules:
  0.0 440.7 jit_solution(7326843695819779241)
XLA Ops:
  7.4 0.0 sort.19.cloned.1.call-start
  7.4 0.7 reshape.214
  8.1 0.6 add_select_fusion
  8.7 0.6 iota.37
  9.3 0.0 sort.19.cloned.1.call-update
  9.3 0.0 all-gather.6.cloned.1.call-start
  9.4 0.5 all-gather.6.cloned.1.call-update
  9.9 0.0 all-gather.4.cloned.1.call-start
  10.0 0.5 all-gather.4.cloned.1.call-update
  10.5 0.0 copy-start.2
  10.5 0.0 all-gather.8.cloned.1.call-start
  10.6 0.5 all-gather.8.cloned.1.call-update
  11.1 0.1 copy-done.2
  11.2 0.2 reduce-window.4
  11.3 0.1 fusion.19
  11.4 0.1 fusion.20
  11.5 0.6 multiply_cosine_fusion
  12.2 0.2 copy.31
  12.4 0.2 copy.32
  12.5 0.3 fusion.9
  12.8 0.7 sort.19.cloned.1.call-done
  13.5 0.7 dynamic-slice_reduce_fusion
  14.2 0.1 squeeze.7
  14.3 0.7 fusion.23
  15.0 57.2 %all-gather.6.cloned.1.call-done = bf16[8192,2,256]{2,1,0:T(2,128)(2,1)} async-done(((bf16[2048,2,256]{2,1,0:T(2,128)(2,1)}), bf16[8192,2,256]{2,1,0:T(2,128)(2,1)}) %all-gather.6.cloned.1.call-update) | async-done | bytes 8388624 | tf_op jit(solution)/shard_map/all_gather | solution.py:61
  72.2 21.5 %copy.41 = bf16[8192,2,256]{0,2,1:T(8,128)(2,1)} copy(bf16[8192,2,256]{2,1,0:T(2,128)(2,1)} %all-gather.6.cloned.1.call-done) | data formatting | bytes 16777216 | tf_op jit(solution)/shard_map/reshape | solution.py:66
  93.7 163.7 %all-gather.4.cloned.1.call-done = bf16[640,8192]{1,0:T(8,128)(2,1)} async-done(((bf16[640,2048]{1,0:T(8,128)(2,1)}), bf16[640,8192]{1,0:T(8,128)(2,1)}) %all-gather.4.cloned.1.call-update) | async-done | bytes 10485776 | tf_op jit(solution)/shard_map/all_gather | solution.py:58
  257.4 16.0 %fusion.1 = f32[640,2,256]{0,2,1:T(8,128)S(1)} fusion(bf16[640,8192]{1,0:T(8,128)(2,1)} %all-gather.4.cloned.1.call-done, bf16[8192,2,256]{0,2,1:T(8,128)(2,1)} %copy.41), kind=kOutput, calls=%fused_computation.7 | convolution fusion | flops 5368709120 | bytes 20185088 | tf_op jit(solution)/shard_map/dot_general | solution.py:65
  273.5 0.0 copy-start
  273.5 1.0 copy-done
  274.5 0.1 subtract_convert_fusion.1
  274.6 88.2 %all-gather.8.cloned.1.call-done = bf16[8192,1024]{1,0:T(8,128)(2,1)} async-done(((bf16[2048,1024]{1,0:T(8,128)(2,1)}), bf16[8192,1024]{1,0:T(8,128)(2,1)}) %all-gather.8.cloned.1.call-update) | async-done | bytes 16777232 | tf_op jit(solution)/shard_map/all_gather | solution.py:60
  362.9 16.1 %convolution_bitcast_fusion = f32[80,8,8,128]{3,1,2,0:T(8,128)S(1)} fusion(bf16[640,8192]{1,0:T(8,128)(2,1)} %all-gather.4.cloned.1.call-done, bf16[8192,1024]{1,0:T(8,128)(2,1)} %all-gather.8.cloned.1.call-done), kind=kOutput, calls=%fused_computation.17 | convolution fusion | flops 10737418240 | bytes 29884416 | tf_op jit(solution)/shard_map/dot_general | solution.py:64
  379.0 0.6 copy.44
  379.6 1.1 subtract_convert_fusion
  380.7 0.2 copy.33
  380.9 0.2 copy.34
  381.0 8.4 %fusion.31 = (f32[2,4,640]{2,1,0:T(4,128)S(1)}, f32[2,4,640,640]{2,3,1,0:T(8,128)}) fusion(pred[640,640]{0,1:T(8,128)(4,1)S(1)} %fusion.9, bf16[640,2,64]{0,2,1:T(8,128)(2,1)S(1)} %get-tuple-element.10, bf16[640,2,64]{0,2,1:T(8,128)(2,1)S(1)} %get-tuple-element.9, bf16[640,2,4,64]{3,0,2,1:T(8,128)(2,1)S(1)} %bitcast.71, bf16[640,2,4,64]{3,0,2,1:T(8,128)(2,1)S(1)} %bitcast.70), kind=kOutput, calls=%fused_computation.62 | convolution fusion | flops 855245440 | bytes 15175680 | tf_op jit(solution)/shard_map/sub | solution.py:46
  389.4 6.2 %fusion.10 = bf16[2,128,4,640]{3,1,2,0:T(8,128)(2,1)S(1)} fusion(f32[2,4,640,640]{2,3,1,0:T(8,128)} %get-tuple-element.14, f32[2,4,640]{2,1,0:T(4,128)S(1)} %get-tuple-element.13, f32[640,2,256]{0,2,1:T(8,128)} %copy-done), kind=kOutput, calls=%fused_computation.20 | convolution fusion | flops 846069760 | bytes 14766080 | tf_op jit(solution)/shard_map/kgqs,skd->qkgd/dot_general | solution.py:48
  395.6 0.7 copy.37
  396.2 2.8 gather_fusion
  399.1 1.2 broadcast_select_fusion
  400.3 0.0 copy-start.1
  400.3 3.7 all-to-all-start
  404.0 0.0 copy-done.1
  404.1 22.0 %gather_fusion.1 = s32[2560]{0:T(1024)S(1)} fusion(s32[4,640]{1,0:T(4,128)S(1)} %reshape.214, s32[2560]{0:T(1024)S(1)} %reshape.230), kind=kCustom, calls=%fused_computation.1 | custom fusion | bytes 40960 | tf_op jit(solution)/shard_map/jit(take_along_axis)/gather | solution.py:83
  426.1 0.1 fusion.21
  426.1 0.1 reshape.216
  426.3 0.0 all-to-all-done
  426.3 6.8 %scatter_custom_fusion = bf16[640,1024]{1,0:T(8,128)(2,1)} fusion(s32[640]{0:T(1024)S(1)} %fusion.22, bf16[640,1024]{1,0:T(8,128)(2,1)S(1)} %bitcast.69, bf16[]{:T(256)} %constant.34.clone.1), kind=kCustom, calls=%fused_computation.25 | custom fusion | bytes 1310722 | tf_op jit(solution)/shard_map/scatter | solution.py:89
  (10 shorter events, 0.1 us)
Async XLA Ops:
  7.4 6.1 %sort.19.cloned.1.call-start = ((), (), s32[]{:S(2)}) async-start(), calls=%async_computation.4 | async-start | bytes 61472 | tf_op jit(solution)/shard_map/jit(argsort)/sort | solution.py:79
  9.3 62.9 %all-gather.6.cloned.1.call-start = ((), (), s32[]{:S(2)}) async-start(), calls=%async_computation.2 | async-start | bytes 10485760 | tf_op jit(solution)/shard_map/all_gather | solution.py:61
  9.9 247.5 %all-gather.4.cloned.1.call-start = ((), (), s32[]{:S(2)}) async-start(), calls=%async_computation.1 | async-start | bytes 13107200 | tf_op jit(solution)/shard_map/all_gather | solution.py:58
  10.5 0.7 copy-start.2
  10.5 352.3 %all-gather.8.cloned.1.call-start = ((), (), s32[]{:S(2)}) async-start(), calls=%async_computation.3 | async-start | bytes 20971520 | tf_op jit(solution)/shard_map/all_gather | solution.py:60
  273.5 1.1 copy-start
  400.3 3.7 copy-start.1
  400.3 25.9 %all-to-all-start = ((bf16[4,160,1024]{2,1,0:T(8,128)(2,1)}), bf16[4,160,1024]{2,1,0:T(8,128)(2,1)S(1)}, u32[]{:S(2)}, u32[]{:S(2)}) async-start(bf16[4,160,1024]{2,1,0:T(8,128)(2,1)} %broadcast_select_fusion), calls=%async_computation | async-start | bytes 2621440 | tf_op jit(solution)/shard_map/all_to_all | solution.py:82
Sparse Core Ops, SparseCore 0:
  10.6 2.5 sort.21.cloned.1.call-done
  (1 shorter events, 0.0 us)
Sparse Core Ops, SparseCore 1:
  11.4 60.8 all-gather.5
  73.7 183.7 all-gather.3
  258.9 103.9 all-gather.7
where the time goes:
time: 442 us; the launch traced here: 441 us
  waiting for transfers between devices  311 us (70%)
  local copies, waits for them, and re-layouts  59.1 us (13%)
  matrix products  46.7 us (11%)
  between operations  15.2 us (3%)
  other arithmetic  5.15 us (1%)
    all_gather x1, waiting for transfers between devices, local(): features = lax.all_gather(hidden, 'trow', axis=1, tiled=True)  164 us
    all_gather x1, waiting for transfers between devices, local(): lax.all_gather(w_query, 'replica', axis=0, tiled=True)  88.2 us
    all_gather x1, waiting for transfers between devices, local(): lax.all_gather(w_keyval, 'replica', axis=0, tiled=True)  57.2 us
    gather x3, local copies, waits for them, and re-layouts, local(): sorted_home = jnp.take_along_axis(home_table, send_order, axis=1)  22 us
    reshape x1, local copies, waits for them, and re-layouts, local(): pieces[1].reshape(width, keyval_cols)  21.5 us
    dot_general x1, matrix products, local(): query_raw = jnp.dot(features, pieces[0], preferred_element_type=jnp.float32)  16.1 us
    dot_general x1, matrix products, local(): jnp.dot(features, pieces[1].reshape(width, keyval_cols), preferred_elemen...  16 us
  transfers between devices with their start and end apart: 4, of which 3 were waited for; matrix products, arithmetic and copies ran while one was open for 14% of the time, Pallas kernels for 0%

commit v1 on v0

v1 whole, which is shorter than its diff:
```python
import functools
import math

import jax
import jax.numpy as jnp
from jax import lax
from jax.experimental import pallas as pl
from jax.experimental.pallas import tpu as pltpu
from jax.sharding import PartitionSpec as P

rope_base = 500000.0
BF16 = jnp.bfloat16
F32 = jnp.float32
VMEM_BYTES = 56 * 1024 * 1024


def row_tables(lengths_row, count, head_dim):
    seg_ends = jnp.cumsum(lengths_row)
    seg_starts = seg_ends - lengths_row
    row_index = jnp.arange(count, dtype=jnp.int32)
    segment = jnp.sum((row_index[:, None] >= seg_ends[None, :]).astype(jnp.int32), axis=1)
    picked = segment[:, None] == jnp.arange(lengths_row.shape[0], dtype=jnp.int32)[None, :]
    seg_first = jnp.sum(jnp.where(picked, seg_starts[None, :], 0), axis=1)
    position = row_index - seg_first
    half_dim = head_dim // 2
    exponent = jnp.arange(half_dim, dtype=F32) * (2.0 / head_dim)
    frequency = jnp.power(F32(rope_base), -exponent)
    angle = position.astype(F32)[:, None] * frequency[None, :]
    cosine, sine = jnp.cos(angle), jnp.sin(angle)
    return (
        seg_first.astype(jnp.int32)[:, None],
        jnp.concatenate([cosine, cosine], axis=1),
        jnp.concatenate([-sine, sine], axis=1),
    )


def route_tables(home_pos, replicas, tok_rows, me):
    per_pair = tok_rows // replicas
    table = home_pos.reshape(replicas, tok_rows)
    owner = table // tok_rows
    kinds = jnp.arange(replicas, dtype=jnp.int32)
    onehot = owner[:, :, None] == kinds[None, None, :]
    row = jnp.arange(tok_rows, dtype=jnp.int32)
    earlier = (row[None, :] < row[:, None]).astype(BF16)
    counts = jnp.einsum("ij,sjo->sio", earlier, onehot.astype(BF16), preferred_element_type=F32)
    rank = jnp.sum(jnp.where(onehot, counts, 0.0), axis=2).astype(jnp.int32)
    my_owner = lax.dynamic_index_in_dim(owner, me, 0, keepdims=False)
    my_rank = lax.dynamic_index_in_dim(rank, me, 0, keepdims=False)
    slot = (my_owner ^ me) * per_pair + my_rank
    place = (kinds[:, None] ^ me) * per_pair + rank
    target = (table - me * tok_rows).reshape(-1)
    hit = target[None, :] == row[:, None]
    source = jnp.sum(jnp.where(hit, place.reshape(-1)[None, :], 0), axis=1)
    return slot.astype(jnp.int32)[None, :], source.astype(jnp.int32)[:, None]


def block_cols(q_cols, kv_cols):
    return math.gcd(512, q_cols, kv_cols)


def fetch(picks, step, wq, wkv, buf, sem, q_cols, block, slot):
    width = buf.shape[2]
    q_blocks = q_cols // width
    refs, first = (wq, block * width) if block < q_blocks else (wkv, (block - q_blocks) * width)

    def start():
        for j, ref in enumerate(refs):
            @pl.when(picks[step] == j)
            def _():
                pltpu.make_async_copy(ref.at[:, pl.ds(first, width)], buf.at[slot], sem.at[slot]).start()

    def wait():
        pltpu.make_async_copy(refs[0].at[:, pl.ds(first, width)], buf.at[slot], sem.at[slot]).wait()

    return start, wait


def project_kernel(steps, shards, q_cols, all_cols, picks, *refs):
    hidden, refs = refs[:steps], refs[steps:]
    wq, refs = refs[:shards], refs[shards:]
    wkv, refs = refs[:shards], refs[shards:]
    out, buf, sem = refs
    width = buf.shape[2]
    blocks = all_cols // width
    todo = [(block, step) for block in range(blocks) for step in range(steps)]
    copies = [
        fetch(picks, step, wq, wkv, buf, sem, q_cols, block, i % 3) for i, (block, step) in enumerate(todo)
    ]
    copies[0][0]()
    if len(todo) > 1:
        copies[1][0]()
    for i, (block, step) in enumerate(todo):
        if i + 2 < len(todo):
            copies[i + 2][0]()
        copies[i][1]()
        part = jnp.dot(hidden[step][...], buf[i % 3], preferred_element_type=F32)
        span = slice(block * width, (block + 1) * width)
        if step == 0:
            out[:, span] = part
        else:
            out[:, span] += part


def project(picks, hidden, wq, wkv):
    rows, depth = hidden[0].shape
    q_cols, kv_cols = wq[0].shape[1], wkv[0].shape[1]
    steps, shards = len(hidden), len(wq)
    vmem = pl.BlockSpec(memory_space=pltpu.VMEM)
    hbm = pl.BlockSpec(memory_space=pl.ANY)
    return pl.pallas_call(
        functools.partial(project_kernel, steps, shards, q_cols, q_cols + kv_cols),
        out_shape=jax.ShapeDtypeStruct((rows, q_cols + kv_cols), F32),
        in_specs=[pl.BlockSpec(memory_space=pltpu.SMEM)] + [vmem] * steps + [hbm] * (2 * shards),
        out_specs=vmem,
        scratch_shapes=[pltpu.VMEM((3, depth, block_cols(q_cols, kv_cols)), BF16), pltpu.SemaphoreType.DMA((3,))],
        compiler_params=pltpu.CompilerParams(vmem_limit_bytes=VMEM_BYTES),
        cost_estimate=pl.CostEstimate(
            flops=2 * rows * depth * steps * (q_cols + kv_cols), bytes_accessed=30_000_000, transcendentals=0
        ),
        name="project",
    )(picks, *hidden, *wq, *wkv)


def attend_kernel(shards, earlier, last, heads, kv_heads, head_dim, picks, *refs):
    part, refs = refs[0], refs[1:]
    wq, refs = refs[:shards], refs[shards:]
    wkv, refs = refs[:shards], refs[shards:]
    raw_in, cos_ref, sin_ref, first_ref, refs = *refs[:4], refs[4:]
    if earlier:
        kv_before, refs = refs[0], refs[1:]
    if last:
        mixed_before, slot_ref, refs = *refs[:2], refs[2:]
        out_refs, refs = refs[:-4], refs[-4:]
    else:
        kv_out, mixed_ref, refs = *refs[:2], refs[2:]
    buf, sem, raw, kv_all = refs[:4]
    rows = part.shape[0]
    q_cols = heads * head_dim
    all_cols = q_cols + 2 * kv_heads * head_dim
    group = heads // kv_heads
    width = buf.shape[2]
    blocks = all_cols // width
    copies = [fetch(picks, 0, wq, wkv, buf, sem, q_cols, block, block) for block in range(blocks)]
    for start, _ in copies:
        start()
    if earlier:
        kv_all[0:earlier] = kv_before[...]
    cos, sin = cos_ref[...], sin_ref[...]

    def rotated(first):
        u = raw[:, first : first + head_dim]
        return u * cos + pltpu.roll(u, head_dim // 2, 1) * sin

    for block, (_, wait) in enumerate(copies):
        wait()
        span = slice(block * width, (block + 1) * width)
        raw[:, span] = raw_in[:, span] + jnp.dot(part[...], buf[block], preferred_element_type=F32)
    here = slice(earlier, earlier + rows)
    for g in range(kv_heads):
        first = q_cols + 2 * g * head_dim
        kv_all[here, 2 * g * head_dim : (2 * g + 1) * head_dim] = rotated(first).astype(BF16)
        kv_all[here, (2 * g + 1) * head_dim : (2 * g + 2) * head_dim] = raw[
            :, first + head_dim : first + 2 * head_dim
        ].astype(BF16)
    if not last:
        kv_out[...] = kv_all[here]
    step = 256 if rows % 256 == 0 else rows
    scale = math.log2(math.e) / math.sqrt(head_dim)
    pieces = []
    for top in range(0, rows, step):
        span = earlier + top + step
        row_index = earlier + top + lax.broadcasted_iota(jnp.int32, (step, span), 0)
        key_index = lax.broadcasted_iota(jnp.int32, (step, span), 1)
        allowed = (key_index <= row_index) & (key_index >= first_ref[top : top + step])
        for h in range(heads):
            g = h // group
            u = raw[top : top + step, h * head_dim : (h + 1) * head_dim]
            q = u * cos[top : top + step] + pltpu.roll(u, head_dim // 2, 1) * sin[top : top + step]
            keys = kv_all[0:span, 2 * g * head_dim : (2 * g + 1) * head_dim]
            values = kv_all[0:span, (2 * g + 1) * head_dim : (2 * g + 2) * head_dim]
            scores = lax.dot_general(
                q.astype(BF16), keys, (((1,), (1,)), ((), ())), preferred_element_type=F32
            )
            scores = jnp.where(allowed, scores * scale, -jnp.inf)
            weights = jnp.exp2(scores - jnp.max(scores, axis=1, keepdims=True))
            total = jnp.sum(weights, axis=1, keepdims=True)
            mixed = jnp.dot(weights.astype(BF16), values, preferred_element_type=F32) / total
            if last:
                pieces.append(mixed.astype(BF16))
            else:
                mixed_ref[top : top + step, h * head_dim : (h + 1) * head_dim] = mixed.astype(BF16)
    if last:
        count = earlier + rows
        per = count // len(out_refs)
        for j, out in enumerate(out_refs):
            slots = j * per + lax.broadcasted_iota(jnp.int32, (per, count), 0)
            onehot = (slots == slot_ref[...]).astype(BF16)
            old = jnp.dot(onehot[:, :earlier], mixed_before[...], preferred_element_type=F32)
            for h in range(heads):
                span = slice(h * head_dim, (h + 1) * head_dim)
                new = jnp.dot(onehot[:, earlier:], pieces[h], preferred_element_type=F32)
                out[:, span] = (old[:, span] + new).astype(BF16)


def attend(picks, part, wq, wkv, raw, tables, earlier, head_dim, kv_before=None, mixed_before=None, slot=None, replicas=0):
    rows, depth = part.shape
    shards = len(wq)
    q_cols, kv_cols = wq[0].shape[1], wkv[0].shape[1]
    heads, kv_heads = q_cols // head_dim, kv_cols // (2 * head_dim)
    last = slot is not None
    count = earlier + rows
    vmem = pl.BlockSpec(memory_space=pltpu.VMEM)
    hbm = pl.BlockSpec(memory_space=pl.ANY)
    args = [part, *wq, *wkv, raw, tables[1], tables[2], tables[0]]
    specs = [vmem] + [hbm] * (2 * shards) + [vmem] * 4
    if earlier:
        args.append(kv_before)
        specs.append(vmem)
    if last:
        args += [mixed_before, slot]
        specs += [vmem] * 2
        outs = [jax.ShapeDtypeStruct((count // replicas, q_cols), BF16)] * replicas
    else:
        outs = [
            jax.ShapeDtypeStruct((rows, kv_cols), BF16),
            jax.ShapeDtypeStruct((rows, q_cols), BF16),
        ]
    width = block_cols(q_cols, kv_cols)
    blocks = (q_cols + kv_cols) // width
    return pl.pallas_call(
        functools.partial(attend_kernel, shards, earlier, last, heads, kv_heads, head_dim),
        out_shape=outs,
        in_specs=[pl.BlockSpec(memory_space=pltpu.SMEM)] + specs,
        out_specs=[vmem] * len(outs),
        scratch_shapes=[
            pltpu.VMEM((blocks, depth, width), BF16),
            pltpu.SemaphoreType.DMA((blocks,)),
            pltpu.VMEM((rows, q_cols + kv_cols), F32),
            pltpu.VMEM((count, kv_cols), BF16),
        ],
        compiler_params=pltpu.CompilerParams(vmem_limit_bytes=VMEM_BYTES),
        cost_estimate=pl.CostEstimate(
            flops=2 * rows * depth * (q_cols + kv_cols) + 4 * rows * count * q_cols,
            bytes_accessed=15_000_000,
            transcendentals=heads * rows * count,
        ),
        name="attend_last" if last else "attend_first",
    )(picks, *args)


def place_kernel(source_ref, *refs):
    blocks, out = refs[:-1], refs[-1]
    per = blocks[0].shape[0]
    rows = out.shape[0]
    total = None
    for j, block in enumerate(blocks):
        slots = j * per + lax.broadcasted_iota(jnp.int32, (rows, per), 1)
        onehot = (slots == source_ref[...]).astype(BF16)
        part = jnp.dot(onehot, block[...], preferred_element_type=F32)
        total = part if total is None else total + part
    out[...] = total.astype(BF16)


def place(source, blocks):
    vmem = pl.BlockSpec(memory_space=pltpu.VMEM)
    rows, cols = source.shape[0], blocks[0].shape[1]
    return pl.pallas_call(
        place_kernel,
        out_shape=jax.ShapeDtypeStruct((rows, cols), BF16),
        in_specs=[vmem] * (1 + len(blocks)),
        out_specs=vmem,
        compiler_params=pltpu.CompilerParams(vmem_limit_bytes=VMEM_BYTES),
        cost_estimate=pl.CostEstimate(flops=2 * rows * rows * cols, bytes_accessed=4 * rows * cols, transcendentals=0),
        name="place",
    )(source, *blocks)


def local(hidden, w_query, w_keyval, seg_lengths, home_pos):
    tok_rows, depth = hidden.shape
    w_rows = w_query.shape[0]
    head_dim = w_keyval.shape[2] // 2
    replicas, columns = lax.axis_size("replica"), lax.axis_size("trow")
    me, my_col = lax.axis_index("replica"), lax.axis_index("trow")
    flat_keyval = w_keyval.reshape(w_rows, -1)

    def swap(block, j):
        return lax.ppermute(block, "replica", [(i, i ^ j) for i in range(replicas)])

    ring = [(i, (i + 1) % columns) for i in range(columns)]
    cut = tok_rows * 4 // 5
    hiddens = [hidden]
    for _ in range(columns - 2):
        hiddens.append(lax.ppermute(hiddens[-1], "trow", ring))
    first_part = lax.ppermute(hiddens[-1][:cut], "trow", ring)
    last_part = lax.ppermute(hiddens[-1][cut:], "trow", ring)
    shard_of = [lax.rem(my_col - k + columns, columns) for k in range(columns)]
    if replicas == columns and replicas == 4:
        wq = [w_query, swap(w_query, 1), swap(w_query, 2)]
        wkv = [flat_keyval, swap(flat_keyval, 1), swap(flat_keyval, 2)]
        wq.append(swap(wq[2], 1))
        wkv.append(swap(wkv[2], 1))
        picks = [s ^ me for s in shard_of]
    else:
        all_q = lax.all_gather(w_query, "replica", axis=0, tiled=True)
        all_kv = lax.all_gather(flat_keyval, "replica", axis=0, tiled=True)
        wq = [all_q[s * depth : (s + 1) * depth] for s in range(columns)]
        wkv = [all_kv[s * depth : (s + 1) * depth] for s in range(columns)]
        picks = shard_of
    picks = jnp.stack(picks).astype(jnp.int32)

    seg_first, cosine, sine = row_tables(seg_lengths[0], tok_rows, head_dim)
    slot, source = route_tables(home_pos, replicas, tok_rows, me)
    raw = project(picks[:-1], hiddens, wq, wkv)
    kv_first, mixed_first = attend(
        picks[-1:], first_part, wq, wkv, raw[:cut], (seg_first[:cut], cosine[:cut], sine[:cut]), 0, head_dim
    )
    outgoing = attend(
        picks[-1:], last_part, wq, wkv, raw[cut:], (seg_first[cut:], cosine[cut:], sine[cut:]), cut, head_dim,
        kv_before=kv_first, mixed_before=mixed_first, slot=slot, replicas=replicas,
    )
    incoming = [outgoing[0]] + [swap(outgoing[j], j) for j in range(1, replicas)]
    return place(source, incoming)


def solution(mesh):
    placed = (
        P(("groups", "replica"), "trow"),
        P("replica", "trow"),
        P("replica", "trow", None),
        P(("groups", "replica"), None),
        P("groups"),
    )
    return jax.shard_map(
        local,
        mesh=mesh,
        in_specs=placed,
        out_specs=P(("groups", "replica"), "trow"),
        check_vma=False,
    )
```

time: 442 us -> 258 us (0.58)
  waiting for transfers between devices: 311 us -> 176 us
  Pallas kernels: 0 us -> 48.1 us
  matrix products: 46.7 us -> 0.31 us
  local copies, waits for them, and re-layouts: 59.1 us -> 16.2 us
  between operations: 15.2 us -> 0.19 us
  starting transfers between devices: 3.8 us -> 10.9 us
    all_gather x3 -> x0, waiting for transfers between devices: 309 us -> none  [the longest x1 164 us: local(): features = lax.all_gather(hidden, 'trow', axis=1, tiled=True)]
    ppermute x0 -> x13, waiting for transfers between devices: none -> 176 us  [the longest x9 143 us: swap(): return lax.ppermute(block, 'replica', [(i, i ^ j) for i in range(replicas)])]
    pallas_call x0 -> x4, Pallas kernels: none -> 48.1 us  [the longest x2 24.3 us: attend(): pl.pallas_call(functools.partial(attend_kernel, shards, earlier, last, he...]
    dot_general x3 -> x1, matrix products: 38.3 us -> 0.31 us  [route_tables(): jnp.einsum('ij,sjo->sio', earlier, onehot.astype(BF16), preferred_element...]
    gather x4 -> x0, local copies, waits for them, and re-layouts: 24.8 us -> none  [the longest x3 22 us: local(): sorted_home = jnp.take_along_axis(home_table, send_order, axis=1)]
    reshape x3 -> x0, local copies, waits for them, and re-layouts: 22.3 us -> none  [the longest x1 21.5 us: local(): pieces[1].reshape(width, keyval_cols)]
    slice x0 -> x8, local copies, waits for them, and re-layouts: none -> 11.7 us  [the longest x1 3.76 us: local(): raw[:cut]]
    ppermute x0 -> x13, starting transfers between devices: none -> 10.9 us  [the longest x9 5.71 us: swap(): return lax.ppermute(block, 'replica', [(i, i ^ j) for i in range(replicas)])]
  transfers between devices with their start and end apart: 4 -> 13, of which waited for: 3 -> 6; matrix products, arithmetic and copies ran while one was open for 14% -> 8% of each run, Pallas kernels for 0% -> 13%
where the time goes in v1:
time: 258 us; the launch traced here: 257 us
  waiting for transfers between devices  176 us (68%)
  Pallas kernels  48.1 us (19%)
  local copies, waits for them, and re-layouts  16.2 us (6%)
  starting transfers between devices  10.9 us (4%)
  other arithmetic  5.46 us (2%)
    ppermute x9, waiting for transfers between devices, swap(): return lax.ppermute(block, 'replica', [(i, i ^ j) for i in range(replicas)])  143 us
    pallas_call x2, Pallas kernels, attend(): pl.pallas_call(functools.partial(attend_kernel, shards, earlier, last, he...  24.3 us
    pallas_call x1, Pallas kernels, project(): pl.pallas_call(functools.partial(project_kernel, steps, shards, q_cols, q...  19.8 us
    ppermute x2, waiting for transfers between devices, local(): hiddens.append(lax.ppermute(hiddens[-1], 'trow', ring))  17.2 us
    ppermute x1, waiting for transfers between devices, local(): first_part = lax.ppermute(hiddens[-1][:cut], 'trow', ring)  16.5 us
    ppermute x9, starting transfers between devices, swap(): return lax.ppermute(block, 'replica', [(i, i ^ j) for i in range(replicas)])  5.71 us
  transfers between devices with their start and end apart: 13, of which 6 were waited for; matrix products, arithmetic and copies ran while one was open for 8% of the time, Pallas kernels for 13%

profile of v1, /device:TPU:0, one launch (start us, length us, event | category | flops | bytes accessed | tf_op | source)
XLA Modules:
  0.0 257.3 jit_solution(2089045038601686837)
XLA Ops:
  0.0 0.0 copy-start.2
  0.0 0.0 copy-start.6
  0.0 2.9 %collective-permute-start.4 = (bf16[2048,1024]{1,0:T(8,128)(2,1)}, bf16[2048,1024]{1,0:T(8,128)(2,1)}, u32[]{:S(2)}, u32[]{:S(2)}) collective-permute-start(bf16[2048,1024]{1,0:T(8,128)(2,1)} %refs_1_.3), channel_id=1, source_target_pairs={{0,8},{4,12},{8,0},{12,4},{1,9},{5,13},{9,1},{13,5},{2,10},{6,14},... | collective-permute-start | bytes 12582920 | tf_op jit(solution)/shard_map/ppermute | solution.py:287
  2.9 1.6 collective-permute-start
  4.5 2.0 copy.13
  6.6 0.0 copy-start
  6.6 0.6 collective-permute-start.7
  7.2 0.0 collective-permute-start.3
  7.2 87.5 %collective-permute-done.4.refs_5_.refs_3_ = bf16[2048,1024]{1,0:T(8,128)(2,1)} collective-permute-done((bf16[2048,1024]{1,0:T(8,128)(2,1)}, bf16[2048,1024]{1,0:T(8,128)(2,1)}, u32[]{:S(2)}, u32[]{:S(2)}) %collective-permute-start.4) | collective-permute-done | bytes 4194336 | tf_op jit(solution)/shard_map/ppermute | solution.py:287
  94.7 0.0 collective-permute-start.5
  94.7 0.0 collective-permute-done.refs_1_
  94.7 2.1 collective-permute-start.1
  96.8 0.2 collective-permute-start.6
  97.0 0.0 copy-done.2
  97.1 41.7 %collective-permute-done.7.refs_9_.refs_7_ = bf16[2048,512]{1,0:T(8,128)(2,1)} collective-permute-done((bf16[2048,512]{1,0:T(8,128)(2,1)S(1)}, bf16[2048,512]{1,0:T(8,128)(2,1)}, u32[]{:S(2)}, u32[]{:S(2)}) %collective-permute-start.7) | collective-permute-done | bytes 2097184 | tf_op jit(solution)/shard_map/ppermute | solution.py:287
  138.8 0.0 collective-permute-start.8
  138.8 0.0 copy-done.6
  138.8 0.2 reduce-window.4
  139.0 0.1 fusion.15
  139.1 0.1 fusion.16
  139.2 0.3 fusion.9
  139.5 17.2 %collective-permute-done.1.refs_2_ = bf16[640,2048]{1,0:T(8,128)(2,1)} collective-permute-done((bf16[640,2048]{1,0:T(8,128)(2,1)}, bf16[640,2048]{1,0:T(8,128)(2,1)}, u32[]{:S(2)}, u32[]{:S(2)}) %collective-permute-start.1) | collective-permute-done | bytes 2621472 | tf_op jit(solution)/shard_map/ppermute | solution.py:293
  156.7 3.1 %slice.50 = bf16[512,2048]{1,0:T(8,128)(2,1)} slice(bf16[640,2048]{1,0:T(8,128)(2,1)} %collective-permute-done.1.refs_2_), slice={[0:512], [0:2048]} | slice | bytes 4194304 | tf_op jit(solution)/shard_map/slice | solution.py:294
  159.8 0.0 collective-permute-start.9
  159.9 0.7 copy.11.refs_12_
  160.6 0.9 copy.10.refs_12_
  161.4 0.0 copy-done
  161.5 0.6 pad_add_fusion.picks
  162.1 0.6 dynamic-slice_add_fusion.refs_15_
  162.7 1.2 fusion.12
  163.9 0.8 pad_maximum_fusion.2
  164.7 1.0 pad_maximum_fusion
  165.7 1.1 slice.48
  166.8 0.0 collective-permute-done.6.refs_8_.refs_6_
  166.8 1.5 collective-permute-start.2
  168.3 0.0 collective-permute-done.3.refs_4_.refs_2_
  168.3 0.0 collective-permute-done.8.refs_10_.refs_8_
  168.3 0.0 collective-permute-done.5.refs_6_.refs_4_
  168.3 19.8 %project.1 = f32[640,1536]{1,0:T(8,128)} custom-call(s32[3]{0:T(128)} %pad_add_fusion.picks, bf16[640,2048]{1,0:T(8,128)(2,1)} %refs_0_.1, bf16[640,2048]{1,0:T(8,128)(2,1)} %collective-permute-done.refs_1_, bf16[640,2048]{1,0:T(8,128)(2,1)} %collective-permute-done.1.refs_2_, bf16[2048,1024]{1,0:T(8,128)(2,1)} %refs_1_.3, ...), custom_call_target="tpu_custom_call" | custom-call | flops 12079595520 | bytes 30000000 | tf_op jit(solution)/shard_map/project/pallas_call | solution.py:110
  188.1 2.1 slice.49.refs_9_
  190.2 3.8 %slice.51.refs_9_ = f32[512,1536]{1,0:T(8,128)} slice(f32[640,1536]{1,0:T(8,128)} %project.1), slice={[0:512], [0:1536]} | slice | bytes 6291456 | tf_op jit(solution)/shard_map/slice | solution.py:315
  194.0 16.5 %collective-permute-done.9.refs_0_ = bf16[512,2048]{1,0:T(8,128)(2,1)} collective-permute-done((bf16[512,2048]{1,0:T(8,128)(2,1)}, bf16[512,2048]{1,0:T(8,128)(2,1)}, u32[]{:S(2)}, u32[]{:S(2)}) %collective-permute-start.9) | collective-permute-done | bytes 2097184 | tf_op jit(solution)/shard_map/ppermute | solution.py:294
  210.4 14.5 %attend_first.1 = (bf16[512,512]{1,0:T(8,128)(2,1)}, bf16[512,1024]{1,0:T(8,128)(2,1)}) custom-call(s32[1]{0:T(128)} %bitcast.2.picks, bf16[512,2048]{1,0:T(8,128)(2,1)} %collective-permute-done.9.refs_0_, bf16[2048,1024]{1,0:T(8,128)(2,1)} %refs_1_.3, bf16[2048,1024]{1,0:T(8,128)(2,1)} %collective-permute-done.3.refs_4_.refs_2_, ...), custom_call_target="tpu_custom_call" | custom-call | flops 4294967296 | bytes 15000000 | tf_op jit(solution)/shard_map/attend_first/pallas_call | solution.py:230
  224.9 0.0 collective-permute-done.2.refs_0_
  225.0 0.0 copy-start.1
  225.0 0.8 copy-done.1
  225.8 9.8 %attend_last.1 = (bf16[160,1024]{1,0:T(8,128)(2,1)}, bf16[160,1024]{1,0:T(8,128)(2,1)}, bf16[160,1024]{1,0:T(8,128)(2,1)}, bf16[160,1024]{1,0:T(8,128)(2,1)}) custom-call(s32[1]{0:T(128)} %bitcast.2.picks, bf16[128,2048]{1,0:T(8,128)(2,1)} %copy-done.1, bf16[2048,1024]{1,0:T(8,128)(2,1)} %refs_1_.3, ...), custom_call_target="tpu_custom_call" | custom-call | flops 1140850688 | bytes 15000000 | tf_op jit(solution)/shard_map/attend_last/pallas_call | solution.py:230
  235.6 0.1 collective-permute-start.10
  235.7 1.6 collective-permute-start.11
  237.3 0.3 collective-permute-start.12
  237.6 0.1 broadcast_add_fusion
  237.6 0.7 select_reduce_fusion
  238.4 0.9 broadcast_in_dim.55.source_ref
  239.3 0.0 collective-permute-done.10.refs_1_
  239.3 0.0 copy-start.3
  239.3 7.2 %collective-permute-done.11.refs_2_ = bf16[160,1024]{1,0:T(8,128)(2,1)S(1)} collective-permute-done((bf16[160,1024]{1,0:T(8,128)(2,1)}, bf16[160,1024]{1,0:T(8,128)(2,1)S(1)}, u32[]{:S(2)}, u32[]{:S(2)}) %collective-permute-start.11) | collective-permute-done | bytes 327712 | tf_op jit(solution)/shard_map/ppermute | solution.py:287
  246.5 0.0 copy-start.4
  246.5 6.1 %collective-permute-done.12.refs_3_ = bf16[160,1024]{1,0:T(8,128)(2,1)S(1)} collective-permute-done((bf16[160,1024]{1,0:T(8,128)(2,1)}, bf16[160,1024]{1,0:T(8,128)(2,1)S(1)}, u32[]{:S(2)}, u32[]{:S(2)}) %collective-permute-start.12) | collective-permute-done | bytes 327712 | tf_op jit(solution)/shard_map/ppermute | solution.py:287
  252.6 0.0 copy-start.5
  252.6 0.0 copy-done.3
  252.6 0.0 copy-done.4
  252.6 0.7 copy-done.5
  253.3 4.0 %place.1 = bf16[640,1024]{1,0:T(8,128)(2,1)} custom-call(s32[640,1]{1,0:T(8,128)} %broadcast_in_dim.55.source_ref, bf16[160,1024]{1,0:T(8,128)(2,1)} %get-tuple-element.13.refs_0_, bf16[160,1024]{1,0:T(8,128)(2,1)} %copy-done.3, bf16[160,1024]{1,0:T(8,128)(2,1)} %copy-done.4, bf16[160,1024]{1,0:T(8,128)(2,1)} %copy-done.5), custom_call_target="tpu_custom_call" | custom-call | flops 838860800 | bytes 2621440 | tf_op jit(solution)/shard_map/place/pallas_call | solution.py:267
  (13 shorter events, 0.1 us)
Async XLA Ops:
  0.0 97.0 %copy-start.2 = (s32[2560]{0:T(1024)S(1)}, s32[2560]{0:T(1024)}, u32[]{:S(2)}) copy-start(s32[2560]{0:T(1024)} %param.9) | copy-start | bytes 30724
  0.0 138.8 %copy-start.6 = (s32[1,2]{1,0:T(1,128)S(1)}, s32[1,2]{1,0:T(1,128)}, u32[]{:S(2)}) copy-start(s32[1,2]{1,0:T(1,128)} %param.8) | copy-start | bytes 28
  0.0 94.7 %collective-permute-start.4 = (bf16[2048,1024]{1,0:T(8,128)(2,1)}, bf16[2048,1024]{1,0:T(8,128)(2,1)}, u32[]{:S(2)}, u32[]{:S(2)}) collective-permute-start(bf16[2048,1024]{1,0:T(8,128)(2,1)} %refs_1_.3), channel_id=1, source_target_pairs={{0,8},{4,12},{8,0},{12,4},{1,9},{5,13},{9,1},{13,5},{2,10},{6,14},... | collective-permute-start | bytes 12582920 | tf_op jit(solution)/shard_map/ppermute | solution.py:287
  2.9 91.7 %collective-permute-start = (bf16[640,2048]{1,0:T(8,128)(2,1)}, bf16[640,2048]{1,0:T(8,128)(2,1)}, u32[]{:S(2)}, u32[]{:S(2)}) collective-permute-start(bf16[640,2048]{1,0:T(8,128)(2,1)} %refs_0_.1), channel_id=1, source_target_pairs={{0,1},{1,2},{2,3},{3,0},{4,5},{5,6},{6,7},{7,4},{8,9},{9,10},{10,1... | collective-permute-start | bytes 7864328 | tf_op jit(solution)/shard_map/ppermute | solution.py:293
  6.6 154.9 %copy-start = (bf16[256,8,2,256]{3,1,2,0:T(8,128)(2,1)}, bf16[256,8,2,256]{3,1,2,0:T(8,128)(2,1)S(1)}, u32[]{:S(2)}) copy-start(bf16[256,8,2,256]{3,1,2,0:T(8,128)(2,1)S(1)} %copy.13) | copy-start | bytes 6291460
  6.6 132.2 %collective-permute-start.7 = (bf16[2048,512]{1,0:T(8,128)(2,1)S(1)}, bf16[2048,512]{1,0:T(8,128)(2,1)}, u32[]{:S(2)}, u32[]{:S(2)}) collective-permute-start(bf16[2048,512]{1,0:T(8,128)(2,1)S(1)} %bitcast.32), channel_id=1, source_target_pairs={{0,8},{4,12},{8,0},{12,4},{1,9},{5,13},{9,1},{13,5},{2,10},{6,14},... | collective-permute-start | bytes 6291464 | tf_op jit(solution)/shard_map/ppermute | solution.py:287
  7.2 161.1 %collective-permute-start.3 = (bf16[2048,1024]{1,0:T(8,128)(2,1)}, bf16[2048,1024]{1,0:T(8,128)(2,1)}, u32[]{:S(2)}, u32[]{:S(2)}) collective-permute-start(bf16[2048,1024]{1,0:T(8,128)(2,1)} %refs_1_.3), channel_id=1, source_target_pairs={{0,4},{4,0},{8,12},{12,8},{1,5},{5,1},{9,13},{13,9},{2,6},{6,2},{1... | collective-permute-start | bytes 12582920 | tf_op jit(solution)/shard_map/ppermute | solution.py:287
  94.7 73.7 %collective-permute-start.5 = (bf16[2048,1024]{1,0:T(8,128)(2,1)}, bf16[2048,1024]{1,0:T(8,128)(2,1)}, u32[]{:S(2)}, u32[]{:S(2)}) collective-permute-start(bf16[2048,1024]{1,0:T(8,128)(2,1)} %collective-permute-done.4.refs_5_.refs_3_), channel_id=1, source_target_pairs={{0,4},{4,0},{8,12},{12,8},{1,5},{5,1},{9,13},{13,9},{2,6},{6,2},{1... | collective-permute-start | bytes 12582920 | tf_op jit(solution)/shard_map/ppermute | solution.py:287
  94.7 62.0 %collective-permute-start.1 = (bf16[640,2048]{1,0:T(8,128)(2,1)}, bf16[640,2048]{1,0:T(8,128)(2,1)}, u32[]{:S(2)}, u32[]{:S(2)}) collective-permute-start(bf16[640,2048]{1,0:T(8,128)(2,1)} %collective-permute-done.refs_1_), channel_id=1, source_target_pairs={{0,1},{1,2},{2,3},{3,0},{4,5},{5,6},{6,7},{7,4},{8,9},{9,10},{10,1... | collective-permute-start | bytes 7864328 | tf_op jit(solution)/shard_map/ppermute | solution.py:293
  96.8 70.0 %collective-permute-start.6 = (bf16[2048,512]{1,0:T(8,128)(2,1)S(1)}, bf16[2048,512]{1,0:T(8,128)(2,1)}, u32[]{:S(2)}, u32[]{:S(2)}) collective-permute-start(bf16[2048,512]{1,0:T(8,128)(2,1)S(1)} %bitcast.33), channel_id=1, source_target_pairs={{0,4},{4,0},{8,12},{12,8},{1,5},{5,1},{9,13},{13,9},{2,6},{6,2},{1... | collective-permute-start | bytes 6291464 | tf_op jit(solution)/shard_map/ppermute | solution.py:287
  138.8 29.6 %collective-permute-start.8 = (bf16[2048,512]{1,0:T(8,128)(2,1)}, bf16[2048,512]{1,0:T(8,128)(2,1)}, u32[]{:S(2)}, u32[]{:S(2)}) collective-permute-start(bf16[2048,512]{1,0:T(8,128)(2,1)} %collective-permute-done.7.refs_9_.refs_7_), channel_id=1, source_target_pairs={{0,4},{4,0},{8,12},{12,8},{1,5},{5,1},{9,13},{13,9},{2,6},{6,2},{1... | collective-permute-start | bytes 6291464 | tf_op jit(solution)/shard_map/ppermute | solution.py:287
  159.8 50.6 %collective-permute-start.9 = (bf16[512,2048]{1,0:T(8,128)(2,1)}, bf16[512,2048]{1,0:T(8,128)(2,1)}, u32[]{:S(2)}, u32[]{:S(2)}) collective-permute-start(bf16[512,2048]{1,0:T(8,128)(2,1)} %slice.50), channel_id=1, source_target_pairs={{0,1},{1,2},{2,3},{3,0},{4,5},{5,6},{6,7},{7,4},{8,9},{9,10},{10,1... | collective-permute-start | bytes 6291464 | tf_op jit(solution)/shard_map/ppermute | solution.py:294
  166.8 58.1 %collective-permute-start.2 = (bf16[128,2048]{1,0:T(8,128)(2,1)S(1)}, bf16[128,2048]{1,0:T(8,128)(2,1)S(1)}, u32[]{:S(2)}, u32[]{:S(2)}) collective-permute-start(bf16[128,2048]{1,0:T(8,128)(2,1)S(1)} %slice.48), channel_id=1, source_target_pairs={{0,1},{1,2},{2,3},{3,0},{4,5},{5,6},{6,7},{7,4},{8,9},{9,10},{10,1... | collective-permute-start | bytes 1572872 | tf_op jit(solution)/shard_map/ppermute | solution.py:295
  225.0 0.8 copy-start.1
  235.6 3.7 %collective-permute-start.10 = (bf16[160,1024]{1,0:T(8,128)(2,1)}, bf16[160,1024]{1,0:T(8,128)(2,1)S(1)}, u32[]{:S(2)}, u32[]{:S(2)}) collective-permute-start(bf16[160,1024]{1,0:T(8,128)(2,1)} %get-tuple-element.14), channel_id=1, source_target_pairs={{0,4},{4,0},{8,12},{12,8},{1,5},{5,1},{9,13},{13,9},{2,6},{6,2},{1... | collective-permute-start | bytes 983048 | tf_op jit(solution)/shard_map/ppermute | solution.py:287
  235.7 10.8 %collective-permute-start.11 = (bf16[160,1024]{1,0:T(8,128)(2,1)}, bf16[160,1024]{1,0:T(8,128)(2,1)S(1)}, u32[]{:S(2)}, u32[]{:S(2)}) collective-permute-start(bf16[160,1024]{1,0:T(8,128)(2,1)} %get-tuple-element.15), channel_id=1, source_target_pairs={{0,8},{4,12},{8,0},{12,4},{1,9},{5,13},{9,1},{13,5},{2,10},{6,14},... | collective-permute-start | bytes 983048 | tf_op jit(solution)/shard_map/ppermute | solution.py:287
  237.3 15.3 %collective-permute-start.12 = (bf16[160,1024]{1,0:T(8,128)(2,1)}, bf16[160,1024]{1,0:T(8,128)(2,1)S(1)}, u32[]{:S(2)}, u32[]{:S(2)}) collective-permute-start(bf16[160,1024]{1,0:T(8,128)(2,1)} %get-tuple-element.16), channel_id=1, source_target_pairs={{0,12},{4,8},{8,4},{12,0},{1,13},{5,9},{9,5},{13,1},{2,14},{6,10},... | collective-permute-start | bytes 983048 | tf_op jit(solution)/shard_map/ppermute | solution.py:287
  239.3 13.3 %copy-start.3 = (bf16[160,1024]{1,0:T(8,128)(2,1)}, bf16[160,1024]{1,0:T(8,128)(2,1)S(1)}, u32[]{:S(2)}) copy-start(bf16[160,1024]{1,0:T(8,128)(2,1)S(1)} %collective-permute-done.10.refs_1_) | copy-start | bytes 983044
  246.5 6.1 %copy-start.4 = (bf16[160,1024]{1,0:T(8,128)(2,1)}, bf16[160,1024]{1,0:T(8,128)(2,1)S(1)}, u32[]{:S(2)}) copy-start(bf16[160,1024]{1,0:T(8,128)(2,1)S(1)} %collective-permute-done.11.refs_2_) | copy-start | bytes 983044
  252.6 0.7 copy-start.5

commit v2 on v0

v2 whole, which is shorter than its diff:
```python
import functools
import math

import jax
import jax.numpy as jnp
from jax import lax
from jax.experimental import pallas as pl
from jax.experimental.pallas import tpu as pltpu
from jax.sharding import PartitionSpec as P

rope_base = 500000.0
BF16 = jnp.bfloat16
F32 = jnp.float32
VMEM_BYTES = 56 * 1024 * 1024
ROW_CHUNKS = (320, 192, 128)
VMEM = pl.BlockSpec(memory_space=pltpu.VMEM)
SMEM = pl.BlockSpec(memory_space=pltpu.SMEM)
HBM = pl.BlockSpec(memory_space=pl.ANY)


def row_tables(lengths_row, count, head_dim):
    seg_ends = jnp.cumsum(lengths_row)
    seg_starts = seg_ends - lengths_row
    row_index = jnp.arange(count, dtype=jnp.int32)
    segment = jnp.sum((row_index[:, None] >= seg_ends[None, :]).astype(jnp.int32), axis=1)
    picked = segment[:, None] == jnp.arange(lengths_row.shape[0], dtype=jnp.int32)[None, :]
    seg_first = jnp.sum(jnp.where(picked, seg_starts[None, :], 0), axis=1)
    position = row_index - seg_first
    half_dim = head_dim // 2
    exponent = jnp.arange(half_dim, dtype=F32) * (2.0 / head_dim)
    frequency = jnp.power(F32(rope_base), -exponent)
    angle = position.astype(F32)[:, None] * frequency[None, :]
    cosine, sine = jnp.cos(angle), jnp.sin(angle)
    return (
        seg_first.astype(jnp.int32)[:, None],
        jnp.concatenate([cosine, cosine], axis=1),
        jnp.concatenate([-sine, sine], axis=1),
    )


def home_sources(home_pos, tok_rows, me):
    target = home_pos - me * tok_rows
    hit = target[None, :] == jnp.arange(tok_rows, dtype=jnp.int32)[:, None]
    packed = jnp.arange(home_pos.shape[0], dtype=jnp.int32)
    return jnp.sum(jnp.where(hit, packed[None, :], 0), axis=1).astype(jnp.int32)[:, None]


class Weights:
    def __init__(self, query, keyval):
        self.query, self.keyval = query, keyval
        self.depth = keyval[0].shape[0]
        self.q_cols, self.kv_cols = query[0][0].shape[1], keyval[0].shape[1]
        self.all_cols = self.q_cols + self.kv_cols
        self.width = math.gcd(512, self.q_cols, self.kv_cols)
        self.blocks = self.all_cols // self.width

    def arrays(self):
        return [piece for pieces in self.query for piece in pieces] + self.keyval

    def refs(self, flat):
        flat = list(flat)
        query = [[flat.pop(0) for _ in pieces] for pieces in self.query]
        return query, flat

    def fetch(self, refs, pick, which, block, buf, sem):
        query, keyval = refs
        q_blocks = self.q_cols // self.width
        is_query = block < q_blocks
        span = pl.ds((block if is_query else block - q_blocks) * self.width, self.width)

        def start():
            for j in range(len(keyval)):
                pieces = query[j] if is_query else [keyval[j]]

                @pl.when(pick == j)
                def _(pieces=pieces):
                    if len(pieces) == 1:
                        pltpu.make_async_copy(pieces[0].at[:, span], buf, sem).start()
                    else:
                        half = self.depth // 2
                        for order in range(2):
                            @pl.when(which == order)
                            def _(order=order):
                                for n, piece in enumerate(pieces):
                                    rows = pl.ds((n ^ order) * half, half)
                                    pltpu.make_async_copy(piece.at[:, span], buf.at[rows], sem).start()

        def wait():
            whole = query[0][0] if is_query else keyval[0]
            pltpu.make_async_copy(whole.at[:, span], buf, sem).wait()

        return start, wait


def project_kernel(w, steps, chunks, ctrl, *refs):
    hidden, refs = refs[:steps], refs[steps:]
    count = len(w.arrays())
    w_refs, refs = w.refs(refs[:count]), refs[count:]
    outs, (held, buf, sem, h_sem) = refs[: len(chunks)], refs[len(chunks) :]
    which = ctrl[steps + 1]
    loads = [pltpu.make_async_copy(hidden[s], held.at[s], h_sem.at[s]) for s in range(steps)]
    todo = [(block, step) for block in range(w.blocks) for step in range(steps)]
    slots = buf.shape[0]
    copies = [
        w.fetch(w_refs, ctrl[step], which, block, buf.at[i % slots], sem.at[i % slots])
        for i, (block, step) in enumerate(todo)
    ]
    loads[0].start()
    for i in range(min(slots - 1, len(todo))):
        copies[i][0]()
        if i + 1 < steps:
            loads[i + 1].start()
    for s in range(min(slots, len(todo) + 1), steps):
        loads[s].start()
    for i, (block, step) in enumerate(todo):
        if i + slots - 1 < len(todo):
            copies[i + slots - 1][0]()
        if block == 0:
            loads[step].wait()
        copies[i][1]()
        span = slice(block * w.width, (block + 1) * w.width)
        first = 0
        for out, rows in zip(outs, chunks):
            part = jnp.dot(held[step, first : first + rows], buf[i % slots], preferred_element_type=F32)
            if step == 0:
                out[:, span] = part
            else:
                out[:, span] += part
            first += rows


def project(ctrl, hidden, w, chunks):
    rows, depth = hidden[0].shape
    steps = len(hidden)
    return pl.pallas_call(
        functools.partial(project_kernel, w, steps, chunks),
        out_shape=[jax.ShapeDtypeStruct((r, w.all_cols), F32) for r in chunks],
        in_specs=[SMEM] + [HBM] * (steps + len(w.arrays())),
        out_specs=[VMEM] * len(chunks),
        scratch_shapes=[
            pltpu.VMEM((steps, rows, depth), BF16),
            pltpu.VMEM((4, depth, w.width), BF16),
            pltpu.SemaphoreType.DMA((4,)),
            pltpu.SemaphoreType.DMA((steps,)),
        ],
        compiler_params=pltpu.CompilerParams(vmem_limit_bytes=VMEM_BYTES),
        cost_estimate=pl.CostEstimate(
            flops=2 * rows * depth * steps * w.all_cols, bytes_accessed=30_000_000, transcendentals=0
        ),
        name="project",
    )(ctrl, *hidden, *w.arrays())


def attend_kernel(w, last_step, heads, head_dim, before, ctrl, part, *refs):
    count = len(w.arrays())
    w_refs, refs = w.refs(refs[:count]), refs[count:]
    raw_in, cos_ref, sin_ref, first_ref, refs = *refs[:4], refs[4:]
    kv_before, refs = refs[: len(before)], refs[len(before) :]
    kv_out, mixed_ref, buf, sem, raw, kv_all = refs
    rows, earlier = part.shape[0], sum(before)
    kv_heads = w.kv_cols // (2 * head_dim)
    group = heads // kv_heads
    copies = [
        w.fetch(w_refs, ctrl[last_step], ctrl[last_step + 1], block, buf.at[block], sem.at[block])
        for block in range(w.blocks)
    ]
    for start, _ in copies[::-1]:
        start()
    top = 0
    for ref, n in zip(kv_before, before):
        kv_all[top : top + n] = ref[...]
        top += n
    cos, sin = cos_ref[...], sin_ref[...]

    def rotated(first):
        u = raw[:, first : first + head_dim]
        return (u * cos + pltpu.roll(u, head_dim // 2, 1) * sin).astype(BF16)

    for block in range(w.blocks)[::-1]:
        copies[block][1]()
        span = slice(block * w.width, (block + 1) * w.width)
        raw[:, span] = raw_in[:, span] + jnp.dot(part[...], buf[block], preferred_element_type=F32)
    here = slice(earlier, earlier + rows)
    for g in range(kv_heads):
        first = w.q_cols + 2 * g * head_dim
        kv_all[here, 2 * g * head_dim : (2 * g + 1) * head_dim] = rotated(first)
        kv_all[here, (2 * g + 1) * head_dim : (2 * g + 2) * head_dim] = raw[
            :, first + head_dim : first + 2 * head_dim
        ].astype(BF16)
    kv_out[...] = kv_all[here]
    span = earlier + rows
    row_index = earlier + lax.broadcasted_iota(jnp.int32, (rows, span), 0)
    key_index = lax.broadcasted_iota(jnp.int32, (rows, span), 1)
    allowed = (key_index <= row_index) & (key_index >= first_ref[...])
    scale = math.log2(math.e) / math.sqrt(head_dim)
    for h in range(heads):
        g = h // group
        keys = kv_all[0:span, 2 * g * head_dim : (2 * g + 1) * head_dim]
        values = kv_all[0:span, (2 * g + 1) * head_dim : (2 * g + 2) * head_dim]
        scores = lax.dot_general(
            rotated(h * head_dim), keys, (((1,), (1,)), ((), ())), preferred_element_type=F32
        )
        scores = jnp.where(allowed, scores * scale, -jnp.inf)
        weights = jnp.exp2(scores - jnp.max(scores, axis=1, keepdims=True))
        total = jnp.sum(weights, axis=1, keepdims=True)
        mixed = jnp.dot(weights.astype(BF16), values, preferred_element_type=F32) / total
        mixed_ref[:, h * head_dim : (h + 1) * head_dim] = mixed.astype(BF16)


def attend(ctrl, last_step, part, w, raw, tables, kv_before, head_dim):
    rows, depth = part.shape
    heads = w.q_cols // head_dim
    before = [a.shape[0] for a in kv_before]
    count = sum(before) + rows
    return pl.pallas_call(
        functools.partial(attend_kernel, w, last_step, heads, head_dim, before),
        out_shape=[
            jax.ShapeDtypeStruct((rows, w.kv_cols), BF16),
            jax.ShapeDtypeStruct((rows, w.q_cols), BF16),
        ],
        in_specs=[SMEM, VMEM] + [HBM] * len(w.arrays()) + [VMEM] * (4 + len(before)),
        out_specs=[VMEM] * 2,
        scratch_shapes=[
            pltpu.VMEM((w.blocks, depth, w.width), BF16),
            pltpu.SemaphoreType.DMA((w.blocks,)),
            pltpu.VMEM((rows, w.all_cols), F32),
            pltpu.VMEM((count, w.kv_cols), BF16),
        ],
        compiler_params=pltpu.CompilerParams(vmem_limit_bytes=VMEM_BYTES),
        cost_estimate=pl.CostEstimate(
            flops=2 * rows * depth * w.all_cols + 4 * rows * count * w.q_cols,
            bytes_accessed=15_000_000,
            transcendentals=heads * rows * count,
        ),
        name="attend",
    )(ctrl, part, *w.arrays(), raw, tables[1], tables[2], tables[0], *kv_before)


def place_kernel(tops, tok_rows, more, me_ref, source_ref, *refs):
    blocks, out = refs[: len(refs) - 1 - more], refs[-1]
    rows = out.shape[0]
    peers = len(blocks) // len(tops)
    me = me_ref[0]
    total = None
    for n, block in enumerate(blocks):
        chunk, j = divmod(n, peers)
        base = (me ^ j) * tok_rows + tops[chunk]
        index = lax.broadcasted_iota(jnp.int32, (rows, block.shape[0]), 1)
        onehot = (index == source_ref[...] - base).astype(BF16)
        part = jnp.dot(onehot, block[...], preferred_element_type=F32)
        total = part if total is None else total + part
    if more:
        total = total + refs[len(blocks)][...].astype(F32)
    out[...] = total.astype(BF16)


def place(me, source, blocks, tops, tok_rows, before=None):
    rows, cols = source.shape[0], blocks[0].shape[1]
    more = [] if before is None else [before]
    return pl.pallas_call(
        functools.partial(place_kernel, tops, tok_rows, len(more)),
        out_shape=jax.ShapeDtypeStruct((rows, cols), BF16),
        in_specs=[SMEM] + [VMEM] * (1 + len(blocks) + len(more)),
        out_specs=VMEM,
        compiler_params=pltpu.CompilerParams(vmem_limit_bytes=VMEM_BYTES),
        cost_estimate=pl.CostEstimate(
            flops=2 * rows * cols * sum(b.shape[0] for b in blocks),
            bytes_accessed=8 * rows * cols,
            transcendentals=0,
        ),
        name="place",
    )(me, source, *blocks, *more)


def local(hidden, w_query, w_keyval, seg_lengths, home_pos):
    tok_rows = hidden.shape[0]
    w_rows = w_query.shape[0]
    head_dim = w_keyval.shape[2] // 2
    replicas, columns = lax.axis_size("replica"), lax.axis_size("trow")
    me, my_col, my_group = lax.axis_index("replica"), lax.axis_index("trow"), lax.axis_index("groups")
    flat_keyval = w_keyval.reshape(w_rows, -1)
    total = sum(ROW_CHUNKS)
    chunks = [tok_rows * c // total for c in ROW_CHUNKS]
    tops = [sum(chunks[:n]) for n in range(len(chunks))]

    def swap(block, j):
        return lax.ppermute(block, "replica", [(i, i ^ j) for i in range(replicas)])

    def on(block):
        return lax.ppermute(block, "trow", [(i, (i + 1) % columns) for i in range(columns)])

    small = replicas == 4 and columns == 4
    if small:
        half = w_rows // 2
        h1 = on(hidden)
        mine = swap(lax.dynamic_slice_in_dim(w_query, my_group * half, half, 0), 2)
        query_1, keyval_1 = swap(w_query, 1), swap(flat_keyval, 1)
        h1, mine, keyval_later = lax.optimization_barrier((h1, mine, flat_keyval))
        h2 = on(h1)
        other = lax.ppermute(mine, "groups", [(0, 1), (1, 0)])
        keyval_2 = swap(keyval_later, 2)
        mine_3 = swap(mine, 1)
        h2, other, keyval_2 = lax.optimization_barrier((h2, other, keyval_2))
        hiddens = [hidden, h1, h2]
        parts = [on(h2[top : top + rows]) for top, rows in zip(tops, chunks)]
        weights = Weights(
            [[w_query], [query_1], [mine, other], [mine_3, swap(other, 1)]],
            [flat_keyval, keyval_1, keyval_2, swap(keyval_2, 1)],
        )
    else:
        hiddens = [hidden]
        for _ in range(columns - 2):
            hiddens.append(on(hiddens[-1]))
        parts = [on(hiddens[-1][top : top + rows]) for top, rows in zip(tops, chunks)]
        depth = hidden.shape[1]
        all_q = lax.all_gather(w_query, "replica", axis=0, tiled=True)
        all_kv = lax.all_gather(flat_keyval, "replica", axis=0, tiled=True)
        spans = [slice(s * depth, (s + 1) * depth) for s in range(columns)]
        weights = Weights([[all_q[s]] for s in spans], [all_kv[s] for s in spans])
    shard_of = [lax.rem(my_col - k + columns, columns) for k in range(columns)]
    picks = [s ^ me for s in shard_of] if small else shard_of
    ctrl = jnp.stack(picks + [my_group]).astype(jnp.int32)

    seg_first, cosine, sine = row_tables(seg_lengths[0], tok_rows, head_dim)
    source = home_sources(home_pos, tok_rows, me)
    me_array = me.astype(jnp.int32)[None]
    raws = project(ctrl, hiddens, weights, chunks)
    kv, mixed = [], []
    for part, raw, top, rows in zip(parts, raws, tops, chunks):
        tables = [t[top : top + rows] for t in (seg_first, cosine, sine)]
        kv_new, mixed_new = attend(ctrl, columns - 1, part, weights, raw, tables, kv, head_dim)
        kv, mixed = kv + [kv_new], mixed + [mixed_new]
    blocks = []
    for n, block in enumerate(mixed):
        if small:
            across = swap(block, 2)
            there = across
            if n + 1 < len(mixed):
                there, _ = lax.optimization_barrier((across, mixed[n + 1]))
            blocks.append([block, swap(block, 1), there, swap(there, 1)])
        else:
            blocks.append([block] + [swap(block, j) for j in range(1, replicas)])
    source_late, _ = lax.optimization_barrier((source, mixed[-1]))
    placed = place(me_array, source_late, sum(blocks[:-1], []), tops[:-1], tok_rows)
    return place(me_array, source_late, blocks[-1], tops[-1:], tok_rows, placed)


def solution(mesh):
    placed = (
        P(("groups", "replica"), "trow"),
        P("replica", "trow"),
        P("replica", "trow", None),
        P(("groups", "replica"), None),
        P("groups"),
    )
    return jax.shard_map(
        local,
        mesh=mesh,
        in_specs=placed,
        out_specs=P(("groups", "replica"), "trow"),
        check_vma=False,
    )
```

time: 442 us -> 224 us (0.51)
  waiting for transfers between devices: 311 us -> 131 us
  Pallas kernels: 0 us -> 57.7 us
  matrix products: 46.7 us -> 0 us
  local copies, waits for them, and re-layouts: 59.1 us -> 15.9 us
  between operations: 15.2 us -> 0.22 us
  starting transfers between devices: 3.8 us -> 13.6 us
    all_gather x3 -> x0, waiting for transfers between devices: 309 us -> none  [the longest x1 164 us: local(): features = lax.all_gather(hidden, 'trow', axis=1, tiled=True)]
    ppermute x0 -> x22, waiting for transfers between devices: none -> 131 us  [the longest x16 53.9 us: swap(): return lax.ppermute(block, 'replica', [(i, i ^ j) for i in range(replicas)])]
    pallas_call x0 -> x6, Pallas kernels: none -> 57.7 us  [the longest x3 26.5 us: attend(): pl.pallas_call(functools.partial(attend_kernel, w, last_step, heads, head...]
    dot_general x3 -> x0, matrix products: 38.3 us -> none  [the longest x1 16.1 us: local(): query_raw = jnp.dot(features, pieces[0], preferred_element_type=jnp.float32)]
    gather x4 -> x0, local copies, waits for them, and re-layouts: 24.8 us -> none  [the longest x3 22 us: local(): sorted_home = jnp.take_along_axis(home_table, send_order, axis=1)]
    reshape x3 -> x0, local copies, waits for them, and re-layouts: 22.3 us -> none  [the longest x1 21.5 us: local(): pieces[1].reshape(width, keyval_cols)]
    ppermute x0 -> x22, starting transfers between devices: none -> 13.6 us  [the longest x16 8.72 us: swap(): return lax.ppermute(block, 'replica', [(i, i ^ j) for i in range(replicas)])]
    sub x1 -> x0, matrix products: 8.36 us -> none  [attend(): weights = jnp.exp(scores - peak)]
  transfers between devices with their start and end apart: 4 -> 22, of which waited for: 3 -> 8; matrix products, arithmetic and copies ran while one was open for 14% -> 8% of each run, Pallas kernels for 0% -> 24%
where the time goes in v2:
time: 224 us; the launch traced here: 223 us
  waiting for transfers between devices  131 us (58%)
  Pallas kernels  57.7 us (26%)
  local copies, waits for them, and re-layouts  15.9 us (7%)
  starting transfers between devices  13.6 us (6%)
  other arithmetic  4.78 us (2%)
    ppermute x16, waiting for transfers between devices, swap(): return lax.ppermute(block, 'replica', [(i, i ^ j) for i in range(replicas)])  53.9 us
    ppermute x1, waiting for transfers between devices, local(): other = lax.ppermute(mine, 'groups', [(0, 1), (1, 0)])  43.6 us
    ppermute x5, waiting for transfers between devices, on(): lax.ppermute(block, 'trow', [(i, (i + 1) % columns) for i in range(column...  33.8 us
    pallas_call x3, Pallas kernels, attend(): pl.pallas_call(functools.partial(attend_kernel, w, last_step, heads, head...  26.5 us
    pallas_call x1, Pallas kernels, project(): pl.pallas_call(functools.partial(project_kernel, w, steps, chunks), out_s...  19.2 us
    pallas_call x2, Pallas kernels, place(): pl.pallas_call(functools.partial(place_kernel, tops, tok_rows, len(more))...  12 us
    ppermute x16, starting transfers between devices, swap(): return lax.ppermute(block, 'replica', [(i, i ^ j) for i in range(replicas)])  8.72 us
    slice x3, local copies, waits for them, and re-layouts, local(): parts = [on(h2[top:top + rows]) for top, rows in zip(tops, chunks)]  5.7 us
  transfers between devices with their start and end apart: 22, of which 8 were waited for; matrix products, arithmetic and copies ran while one was open for 8% of the time, Pallas kernels for 24%

profile of v2, /device:TPU:0, one launch (start us, length us, event | category | flops | bytes accessed | tf_op | source)
XLA Modules:
  0.0 223.5 jit_solution(98957485959242232)
XLA Ops:
  0.0 3.0 %collective-permute-start = (bf16[640,2048]{1,0:T(8,128)(2,1)}, bf16[640,2048]{1,0:T(8,128)(2,1)}, u32[]{:S(2)}, u32[]{:S(2)}) collective-permute-start(bf16[640,2048]{1,0:T(8,128)(2,1)} %refs_0_.4), channel_id=1, source_target_pairs={{0,1},{1,2},{2,3},{3,0},{4,5},{5,6},{6,7},{7,4},{8,9},{9,10},{10,1... | collective-permute-start | bytes 7864328 | tf_op jit(solution)/shard_map/ppermute | solution.py:290
  3.0 1.9 constant_dynamic-slice_fusion
  4.9 1.6 collective-permute-start.1
  6.5 0.5 copy.17
  7.0 45.2 %collective-permute-done.1.refs_5_.refs_2_ = bf16[1024,1024]{1,0:T(8,128)(2,1)} collective-permute-done((bf16[1024,1024]{1,0:T(8,128)(2,1)S(1)}, bf16[1024,1024]{1,0:T(8,128)(2,1)}, u32[]{:S(2)}, u32[]{:S(2)}) %collective-permute-start.1) | collective-permute-done | bytes 2097184 | tf_op jit(solution)/shard_map/ppermute | solution.py:287
  52.2 10.0 %collective-permute-done.refs_1_ = bf16[640,2048]{1,0:T(8,128)(2,1)} collective-permute-done((bf16[640,2048]{1,0:T(8,128)(2,1)}, bf16[640,2048]{1,0:T(8,128)(2,1)}, u32[]{:S(2)}, u32[]{:S(2)}) %collective-permute-start) | collective-permute-done | bytes 2621472 | tf_op jit(solution)/shard_map/ppermute | solution.py:290
  62.2 0.0 collective-permute-start.2
  62.2 1.5 collective-permute-start.3
  63.8 1.5 collective-permute-start.4
  65.2 0.0 collective-permute-start.6
  65.2 0.5 collective-permute-start.9
  65.8 43.6 %collective-permute-done.3.refs_6_.refs_3_ = bf16[1024,1024]{1,0:T(8,128)(2,1)} collective-permute-done((bf16[1024,1024]{1,0:T(8,128)(2,1)}, bf16[1024,1024]{1,0:T(8,128)(2,1)}, u32[]{:S(2)}, u32[]{:S(2)}) %collective-permute-start.3) | collective-permute-done | bytes 2097184 | tf_op jit(solution)/shard_map/ppermute | solution.py:300
  109.4 0.0 collective-permute-start.7
  109.4 0.8 collective-permute-done.4.refs_11_.refs_8_
  110.1 12.2 %collective-permute-done.2.refs_2_ = bf16[640,2048]{1,0:T(8,128)(2,1)} collective-permute-done((bf16[640,2048]{1,0:T(8,128)(2,1)}, bf16[640,2048]{1,0:T(8,128)(2,1)}, u32[]{:S(2)}, u32[]{:S(2)}) %collective-permute-start.2) | collective-permute-done | bytes 2621472 | tf_op jit(solution)/shard_map/ppermute | solution.py:290
  122.4 0.0 collective-permute-start.10
  122.4 0.5 collective-permute-start.8
  122.9 0.2 reduce-window.4
  123.1 0.1 fusion.3
  123.2 0.1 fusion.4
  123.3 2.5 %slice.50 = bf16[320,2048]{1,0:T(8,128)(2,1)} slice(bf16[640,2048]{1,0:T(8,128)(2,1)} %collective-permute-done.2.refs_2_), slice={[0:320], [0:2048]} | slice | bytes 2621440 | tf_op jit(solution)/shard_map/slice | solution.py:305
  125.8 0.0 collective-permute-done.9.refs_10_.refs_7_
  125.8 1.2 fusion.2
  127.1 0.8 slice.60.refs_13_
  127.8 0.6 stack.23.ctrl
  128.5 0.9 fusion
  129.4 2.1 slice.55
  131.5 0.0 collective-permute-done.6.refs_4_.refs_1_
  131.5 0.0 collective-permute-start.12
  131.5 0.0 collective-permute-done.7.refs_7_.refs_4_
  131.5 0.0 collective-permute-done.8.refs_8_.refs_5_
  131.5 19.2 %project.1 = (f32[320,1536]{1,0:T(8,128)}, f32[192,1536]{1,0:T(8,128)}, f32[128,1536]{1,0:T(8,128)}) custom-call(s32[5]{0:T(128)} %stack.23.ctrl, bf16[640,2048]{1,0:T(8,128)(2,1)} %refs_0_.4, bf16[640,2048]{1,0:T(8,128)(2,1)} %collective-permute-done.refs_1_, bf16[640,2048]{1,0:T(8,128)(2,1)} %collective-permute-done.2.refs_2_, bf16[2048,1024]{1,0:T(8,128)(2,1)} %refs_0_.7, ...), custom_call_target="tpu_custom_call" | custom-call | flops 12079595520 | bytes 30000000 | tf_op jit(solution)/shard_map/project/pallas_call | solution.py:135
  150.8 8.8 %collective-permute-done.11.part = bf16[320,2048]{1,0:T(8,128)(2,1)} collective-permute-done((bf16[320,2048]{1,0:T(8,128)(2,1)}, bf16[320,2048]{1,0:T(8,128)(2,1)}, u32[]{:S(2)}, u32[]{:S(2)}) %collective-permute-start.11) | collective-permute-done | bytes 1310752 | tf_op jit(solution)/shard_map/ppermute | solution.py:290
  159.6 9.7 %attend.3 = (bf16[320,512]{1,0:T(8,128)(2,1)}, bf16[320,1024]{1,0:T(8,128)(2,1)}) custom-call(s32[5]{0:T(128)} %stack.23.ctrl, bf16[320,2048]{1,0:T(8,128)(2,1)} %collective-permute-done.11.part, bf16[2048,1024]{1,0:T(8,128)(2,1)} %refs_0_.7, bf16[2048,1024]{1,0:T(8,128)(2,1)} %collective-permute-done.6.refs_4_.refs_1_, ...), custom_call_target="tpu_custom_call" | custom-call | flops 2432696320 | bytes 15000000 | tf_op jit(solution)/shard_map/attend/pallas_call | solution.py:215
  169.2 1.3 collective-permute-start.17
  170.6 1.1 slice.45
  171.6 0.3 collective-permute-start.5
  171.9 0.8 pad_maximum_fusion
  172.7 0.1 slice.58
  172.8 0.8 copy.13.refs_13_
  173.6 2.7 %collective-permute-done.12.part = bf16[192,2048]{1,0:T(8,128)(2,1)S(1)} collective-permute-done((bf16[192,2048]{1,0:T(8,128)(2,1)}, bf16[192,2048]{1,0:T(8,128)(2,1)S(1)}, u32[]{:S(2)}, u32[]{:S(2)}) %collective-permute-start.12) | collective-permute-done | bytes 786464 | tf_op jit(solution)/shard_map/ppermute | solution.py:290
  176.3 0.9 copy-done.2
  177.2 8.5 %attend.4 = (bf16[192,512]{1,0:T(8,128)(2,1)}, bf16[192,1024]{1,0:T(8,128)(2,1)}) custom-call(s32[5]{0:T(128)} %stack.23.ctrl, bf16[192,2048]{1,0:T(8,128)(2,1)} %copy-done.2, bf16[2048,1024]{1,0:T(8,128)(2,1)} %refs_0_.7, bf16[2048,1024]{1,0:T(8,128)(2,1)} %collective-permute-done.6.refs_4_.refs_1_, ...), custom_call_target="tpu_custom_call" | custom-call | flops 1610612736 | bytes 15000000 | tf_op jit(solution)/shard_map/attend/pallas_call | solution.py:215
  185.7 1.2 collective-permute-start.20
  187.0 0.5 collective-permute-start.16
  187.5 0.0 collective-permute-done.17.refs_2_
  187.5 0.0 collective-permute-start.18
  187.5 0.7 pad_maximum_fusion.2
  188.2 0.7 copy.14.refs_13_
  189.0 0.0 collective-permute-done.5.part
  189.0 0.8 copy-done.3
  189.8 8.3 %attend.5 = (bf16[128,512]{1,0:T(8,128)(2,1)}, bf16[128,1024]{1,0:T(8,128)(2,1)}) custom-call(s32[5]{0:T(128)} %stack.23.ctrl, bf16[128,2048]{1,0:T(8,128)(2,1)} %copy-done.3, bf16[2048,1024]{1,0:T(8,128)(2,1)} %refs_0_.7, bf16[2048,1024]{1,0:T(8,128)(2,1)} %collective-permute-done.6.refs_4_.refs_1_, ...), custom_call_target="tpu_custom_call" | custom-call | flops 1140850688 | bytes 15000000 | tf_op jit(solution)/shard_map/attend/pallas_call | solution.py:215
  198.1 0.8 collective-permute-start.14
  199.0 0.2 collective-permute-start.21
  199.2 7.9 %collective-permute-done.14.refs_2_ = bf16[128,1024]{1,0:T(8,128)(2,1)S(1)} collective-permute-done((bf16[128,1024]{1,0:T(8,128)(2,1)}, bf16[128,1024]{1,0:T(8,128)(2,1)S(1)}, u32[]{:S(2)}, u32[]{:S(2)}) %collective-permute-start.14) | collective-permute-done | bytes 262176 | tf_op jit(solution)/shard_map/ppermute | solution.py:287
  207.1 0.0 collective-permute-start.13
  207.1 0.5 collective-permute-start.15
  207.6 0.8 select_reduce_fusion
  208.4 0.9 copy.16.source_ref
  209.3 0.7 copy-done.9
  210.1 7.6 %place.2.refs_4_ = bf16[640,1024]{1,0:T(8,128)(2,1)} custom-call(s32[1]{0:T(128)} %bitcast.me_ref, s32[640,1]{1,0:T(8,128)} %copy.16.source_ref, bf16[320,1024]{1,0:T(8,128)(2,1)} %get-tuple-element.35.refs_0_, bf16[320,1024]{1,0:T(8,128)(2,1)} %collective-permute-done.16.refs_1_, bf16[320,1024]{1,0:T(8,128)(2,1)} %collective-permute-done.17.refs_2_, ...), custom_call_target="tpu_custom_call" | custom-call | flops 2684354560 | bytes 5242880 | tf_op jit(solution)/shard_map/place/pallas_call | solution.py:260
  217.7 0.7 copy-done.5
  218.4 0.7 copy-done.6
  219.1 4.4 %place.3 = bf16[640,1024]{1,0:T(8,128)(2,1)} custom-call(s32[1]{0:T(128)} %bitcast.me_ref, s32[640,1]{1,0:T(8,128)} %copy.16.source_ref, bf16[128,1024]{1,0:T(8,128)(2,1)} %get-tuple-element.33.refs_0_, bf16[128,1024]{1,0:T(8,128)(2,1)} %copy-done.5, bf16[128,1024]{1,0:T(8,128)(2,1)} %copy-done.4, bf16[128,1024]{1,0:T(8,128)(2,1)} %copy-done.6, ...), custom_call_target="tpu_custom_call" | custom-call | flops 671088640 | bytes 5242880 | tf_op jit(solution)/shard_map/place/pallas_call | solution.py:260
  (34 shorter events, 0.1 us)
Async XLA Ops:
  0.0 62.2 %collective-permute-start = (bf16[640,2048]{1,0:T(8,128)(2,1)}, bf16[640,2048]{1,0:T(8,128)(2,1)}, u32[]{:S(2)}, u32[]{:S(2)}) collective-permute-start(bf16[640,2048]{1,0:T(8,128)(2,1)} %refs_0_.4), channel_id=1, source_target_pairs={{0,1},{1,2},{2,3},{3,0},{4,5},{5,6},{6,7},{7,4},{8,9},{9,10},{10,1... | collective-permute-start | bytes 7864328 | tf_op jit(solution)/shard_map/ppermute | solution.py:290
  3.0 3.5 %copy-start.1 = (bf16[2048,2,256]{2,1,0:T(2,128)(2,1)S(1)}, bf16[2048,2,256]{2,1,0:T(2,128)(2,1)}, u32[]{:S(2)}) copy-start(bf16[2048,2,256]{2,1,0:T(2,128)(2,1)} %param.7) | copy-start | bytes 6291460
  4.9 47.3 %collective-permute-start.1 = (bf16[1024,1024]{1,0:T(8,128)(2,1)S(1)}, bf16[1024,1024]{1,0:T(8,128)(2,1)}, u32[]{:S(2)}, u32[]{:S(2)}) collective-permute-start(bf16[1024,1024]{1,0:T(8,128)(2,1)S(1)} %constant_dynamic-slice_fusion), channel_id=1, source_target_pairs={{0,8},{4,12},{8,0},{12,4},{1,9},{5,13},{9,1},{13,5},{2,10},{6,14},... | collective-permute-start | bytes 6291464 | tf_op jit(solution)/shard_map/ppermute | solution.py:287
  6.5 116.4 %copy-start.10 = (s32[1,2]{1,0:T(1,128)S(1)}, s32[1,2]{1,0:T(1,128)}, u32[]{:S(2)}) copy-start(s32[1,2]{1,0:T(1,128)} %param.8) | copy-start | bytes 28
  7.0 122.3 %copy-start = (bf16[256,8,2,256]{3,1,2,0:T(8,128)(2,1)}, bf16[256,8,2,256]{3,1,2,0:T(8,128)(2,1)S(1)}, u32[]{:S(2)}) copy-start(bf16[256,8,2,256]{3,1,2,0:T(8,128)(2,1)S(1)} %copy.17) | copy-start | bytes 6291460
  62.2 60.2 %collective-permute-start.2 = (bf16[640,2048]{1,0:T(8,128)(2,1)}, bf16[640,2048]{1,0:T(8,128)(2,1)}, u32[]{:S(2)}, u32[]{:S(2)}) collective-permute-start(bf16[640,2048]{1,0:T(8,128)(2,1)} %collective-permute-done.refs_1_), channel_id=1, source_target_pairs={{0,1},{1,2},{2,3},{3,0},{4,5},{5,6},{6,7},{7,4},{8,9},{9,10},{10,1... | collective-permute-start | bytes 7864328 | tf_op jit(solution)/shard_map/ppermute | solution.py:290
  62.2 47.1 %collective-permute-start.3 = (bf16[1024,1024]{1,0:T(8,128)(2,1)}, bf16[1024,1024]{1,0:T(8,128)(2,1)}, u32[]{:S(2)}, u32[]{:S(2)}) collective-permute-start(bf16[1024,1024]{1,0:T(8,128)(2,1)} %collective-permute-done.1.refs_5_.refs_2_), channel_id=1, source_target_pairs={{0,16},{16,0},{1,17},{17,1},{2,18},{18,2},{3,19},{19,3},{4,20},{20... | collective-permute-start | bytes 6291464 | tf_op jit(solution)/shard_map/ppermute | solution.py:300
  63.8 46.4 %collective-permute-start.4 = (bf16[2048,512]{1,0:T(8,128)(2,1)S(1)}, bf16[2048,512]{1,0:T(8,128)(2,1)}, u32[]{:S(2)}, u32[]{:S(2)}) collective-permute-start(bf16[2048,512]{1,0:T(8,128)(2,1)S(1)} %bitcast.19), channel_id=1, source_target_pairs={{0,8},{4,12},{8,0},{12,4},{1,9},{5,13},{9,1},{13,5},{2,10},{6,14},... | collective-permute-start | bytes 6291464 | tf_op jit(solution)/shard_map/ppermute | solution.py:287
  65.2 66.2 %collective-permute-start.6 = (bf16[2048,1024]{1,0:T(8,128)(2,1)}, bf16[2048,1024]{1,0:T(8,128)(2,1)}, u32[]{:S(2)}, u32[]{:S(2)}) collective-permute-start(bf16[2048,1024]{1,0:T(8,128)(2,1)} %refs_0_.7), channel_id=1, source_target_pairs={{0,4},{4,0},{8,12},{12,8},{1,5},{5,1},{9,13},{13,9},{2,6},{6,2},{1... | collective-permute-start | bytes 12582920 | tf_op jit(solution)/shard_map/ppermute | solution.py:287
  65.2 60.6 %collective-permute-start.9 = (bf16[2048,512]{1,0:T(8,128)(2,1)S(1)}, bf16[2048,512]{1,0:T(8,128)(2,1)}, u32[]{:S(2)}, u32[]{:S(2)}) collective-permute-start(bf16[2048,512]{1,0:T(8,128)(2,1)S(1)} %bitcast.20), channel_id=1, source_target_pairs={{0,4},{4,0},{8,12},{12,8},{1,5},{5,1},{9,13},{13,9},{2,6},{6,2},{1... | collective-permute-start | bytes 6291464 | tf_op jit(solution)/shard_map/ppermute | solution.py:287
  109.4 22.1 %collective-permute-start.7 = (bf16[1024,1024]{1,0:T(8,128)(2,1)}, bf16[1024,1024]{1,0:T(8,128)(2,1)}, u32[]{:S(2)}, u32[]{:S(2)}) collective-permute-start(bf16[1024,1024]{1,0:T(8,128)(2,1)} %collective-permute-done.1.refs_5_.refs_2_), channel_id=1, source_target_pairs={{0,4},{4,0},{8,12},{12,8},{1,5},{5,1},{9,13},{13,9},{2,6},{6,2},{1... | collective-permute-start | bytes 6291464 | tf_op jit(solution)/shard_map/ppermute | solution.py:287
  122.4 9.1 %collective-permute-start.10 = (bf16[2048,512]{1,0:T(8,128)(2,1)}, bf16[2048,512]{1,0:T(8,128)(2,1)}, u32[]{:S(2)}, u32[]{:S(2)}) collective-permute-start(bf16[2048,512]{1,0:T(8,128)(2,1)} %collective-permute-done.4.refs_11_.refs_8_), channel_id=1, source_target_pairs={{0,4},{4,0},{8,12},{12,8},{1,5},{5,1},{9,13},{13,9},{2,6},{6,2},{1... | collective-permute-start | bytes 6291464 | tf_op jit(solution)/shard_map/ppermute | solution.py:287
  122.4 9.1 %collective-permute-start.8 = (bf16[1024,1024]{1,0:T(8,128)(2,1)}, bf16[1024,1024]{1,0:T(8,128)(2,1)}, u32[]{:S(2)}, u32[]{:S(2)}) collective-permute-start(bf16[1024,1024]{1,0:T(8,128)(2,1)} %collective-permute-done.3.refs_6_.refs_3_), channel_id=1, source_target_pairs={{0,4},{4,0},{8,12},{12,8},{1,5},{5,1},{9,13},{13,9},{2,6},{6,2},{1... | collective-permute-start | bytes 6291464 | tf_op jit(solution)/shard_map/ppermute | solution.py:287
  125.8 33.8 %collective-permute-start.11 = (bf16[320,2048]{1,0:T(8,128)(2,1)}, bf16[320,2048]{1,0:T(8,128)(2,1)}, u32[]{:S(2)}, u32[]{:S(2)}) collective-permute-start(bf16[320,2048]{1,0:T(8,128)(2,1)} %slice.50), channel_id=1, source_target_pairs={{0,1},{1,2},{2,3},{3,0},{4,5},{5,6},{6,7},{7,4},{8,9},{9,10},{10,1... | collective-permute-start | bytes 3932168 | tf_op jit(solution)/shard_map/ppermute | solution.py:290
  131.5 44.8 %collective-permute-start.12 = (bf16[192,2048]{1,0:T(8,128)(2,1)}, bf16[192,2048]{1,0:T(8,128)(2,1)S(1)}, u32[]{:S(2)}, u32[]{:S(2)}) collective-permute-start(bf16[192,2048]{1,0:T(8,128)(2,1)} %slice.55), channel_id=1, source_target_pairs={{0,1},{1,2},{2,3},{3,0},{4,5},{5,6},{6,7},{7,4},{8,9},{9,10},{10,1... | collective-permute-start | bytes 2359304 | tf_op jit(solution)/shard_map/ppermute | solution.py:290
  169.2 18.2 %collective-permute-start.17 = (bf16[320,1024]{1,0:T(8,128)(2,1)}, bf16[320,1024]{1,0:T(8,128)(2,1)}, u32[]{:S(2)}, u32[]{:S(2)}) collective-permute-start(bf16[320,1024]{1,0:T(8,128)(2,1)} %get-tuple-element.35.refs_0_), channel_id=1, source_target_pairs={{0,8},{4,12},{8,0},{12,4},{1,9},{5,13},{9,1},{13,5},{2,10},{6,14},... | collective-permute-start | bytes 1966088 | tf_op jit(solution)/shard_map/ppermute | solution.py:287
  171.6 17.3 %collective-permute-start.5 = (bf16[128,2048]{1,0:T(8,128)(2,1)S(1)}, bf16[128,2048]{1,0:T(8,128)(2,1)S(1)}, u32[]{:S(2)}, u32[]{:S(2)}) collective-permute-start(bf16[128,2048]{1,0:T(8,128)(2,1)S(1)} %slice.45), channel_id=1, source_target_pairs={{0,1},{1,2},{2,3},{3,0},{4,5},{5,6},{6,7},{7,4},{8,9},{9,10},{10,1... | collective-permute-start | bytes 1572872 | tf_op jit(solution)/shard_map/ppermute | solution.py:290
  176.3 0.9 copy-start.2
  185.7 13.2 %collective-permute-start.20 = (bf16[192,1024]{1,0:T(8,128)(2,1)}, bf16[192,1024]{1,0:T(8,128)(2,1)S(1)}, u32[]{:S(2)}, u32[]{:S(2)}) collective-permute-start(bf16[192,1024]{1,0:T(8,128)(2,1)} %get-tuple-element.36.refs_4_), channel_id=1, source_target_pairs={{0,8},{4,12},{8,0},{12,4},{1,9},{5,13},{9,1},{13,5},{2,10},{6,14},... | collective-permute-start | bytes 1179656 | tf_op jit(solution)/shard_map/ppermute | solution.py:287
  187.0 20.1 %collective-permute-start.19 = (bf16[192,1024]{1,0:T(8,128)(2,1)}, bf16[192,1024]{1,0:T(8,128)(2,1)}, u32[]{:S(2)}, u32[]{:S(2)}) collective-permute-start(bf16[192,1024]{1,0:T(8,128)(2,1)} %get-tuple-element.36.refs_4_), channel_id=1, source_target_pairs={{0,4},{4,0},{8,12},{12,8},{1,5},{5,1},{9,13},{13,9},{2,6},{6,2},{1... | collective-permute-start | bytes 1179656 | tf_op jit(solution)/shard_map/ppermute | solution.py:287
  187.0 22.3 %collective-permute-start.16 = (bf16[320,1024]{1,0:T(8,128)(2,1)}, bf16[320,1024]{1,0:T(8,128)(2,1)}, u32[]{:S(2)}, u32[]{:S(2)}) collective-permute-start(bf16[320,1024]{1,0:T(8,128)(2,1)} %get-tuple-element.35.refs_0_), channel_id=1, source_target_pairs={{0,4},{4,0},{8,12},{12,8},{1,5},{5,1},{9,13},{13,9},{2,6},{6,2},{1... | collective-permute-start | bytes 1966088 | tf_op jit(solution)/shard_map/ppermute | solution.py:287
  187.5 21.8 %collective-permute-start.18 = (bf16[320,1024]{1,0:T(8,128)(2,1)}, bf16[320,1024]{1,0:T(8,128)(2,1)}, u32[]{:S(2)}, u32[]{:S(2)}) collective-permute-start(bf16[320,1024]{1,0:T(8,128)(2,1)} %collective-permute-done.17.refs_2_), channel_id=1, source_target_pairs={{0,4},{4,0},{8,12},{12,8},{1,5},{5,1},{9,13},{13,9},{2,6},{6,2},{1... | collective-permute-start | bytes 1966088 | tf_op jit(solution)/shard_map/ppermute | solution.py:287
  189.0 0.8 copy-start.3
  189.8 9.4 %copy-start.7 = (s32[2560]{0:T(1024)S(1)}, s32[2560]{0:T(1024)}, u32[]{:S(2)}) copy-start(s32[2560]{0:T(1024)} %param.9) | copy-start | bytes 30724
  198.1 9.0 %collective-permute-start.14 = (bf16[128,1024]{1,0:T(8,128)(2,1)}, bf16[128,1024]{1,0:T(8,128)(2,1)S(1)}, u32[]{:S(2)}, u32[]{:S(2)}) collective-permute-start(bf16[128,1024]{1,0:T(8,128)(2,1)} %get-tuple-element.33.refs_0_), channel_id=1, source_target_pairs={{0,8},{4,12},{8,0},{12,4},{1,9},{5,13},{9,1},{13,5},{2,10},{6,14},... | collective-permute-start | bytes 786440 | tf_op jit(solution)/shard_map/ppermute | solution.py:287
  199.0 10.4 %copy-start.8 = (bf16[192,1024]{1,0:T(8,128)(2,1)}, bf16[192,1024]{1,0:T(8,128)(2,1)S(1)}, u32[]{:S(2)}) copy-start(bf16[192,1024]{1,0:T(8,128)(2,1)S(1)} %collective-permute-done.20.refs_6_) | copy-start | bytes 1179652
  199.0 10.3 %collective-permute-start.21 = (bf16[192,1024]{1,0:T(8,128)(2,1)S(1)}, bf16[192,1024]{1,0:T(8,128)(2,1)S(1)}, u32[]{:S(2)}, u32[]{:S(2)}) collective-permute-start(bf16[192,1024]{1,0:T(8,128)(2,1)S(1)} %collective-permute-done.20.refs_6_), channel_id=1, source_target_pairs={{0,4},{4,0},{8,12},{12,8},{1,5},{5,1},{9,13},{13,9},{2,6},{6,2},{1... | collective-permute-start | bytes 1179656 | tf_op jit(solution)/shard_map/ppermute | solution.py:287
  207.1 10.6 %copy-start.4 = (bf16[128,1024]{1,0:T(8,128)(2,1)}, bf16[128,1024]{1,0:T(8,128)(2,1)S(1)}, u32[]{:S(2)}) copy-start(bf16[128,1024]{1,0:T(8,128)(2,1)S(1)} %collective-permute-done.14.refs_2_) | copy-start | bytes 786436
  207.1 10.6 %collective-permute-start.13 = (bf16[128,1024]{1,0:T(8,128)(2,1)}, bf16[128,1024]{1,0:T(8,128)(2,1)S(1)}, u32[]{:S(2)}, u32[]{:S(2)}) collective-permute-start(bf16[128,1024]{1,0:T(8,128)(2,1)} %get-tuple-element.33.refs_0_), channel_id=1, source_target_pairs={{0,4},{4,0},{8,12},{12,8},{1,5},{5,1},{9,13},{13,9},{2,6},{6,2},{1... | collective-permute-start | bytes 786440 | tf_op jit(solution)/shard_map/ppermute | solution.py:287
  207.1 10.6 %collective-permute-start.15 = (bf16[128,1024]{1,0:T(8,128)(2,1)S(1)}, bf16[128,1024]{1,0:T(8,128)(2,1)S(1)}, u32[]{:S(2)}, u32[]{:S(2)}) collective-permute-start(bf16[128,1024]{1,0:T(8,128)(2,1)S(1)} %collective-permute-done.14.refs_2_), channel_id=1, source_target_pairs={{0,4},{4,0},{8,12},{12,8},{1,5},{5,1},{9,13},{13,9},{2,6},{6,2},{1... | collective-permute-start | bytes 786440 | tf_op jit(solution)/shard_map/ppermute | solution.py:287
  209.3 0.8 copy-start.9
  217.7 0.7 copy-start.5
  218.4 0.7 copy-start.6

commit v3 on v2

v3 whole, which is shorter than its diff:
```python
import functools
import math

import jax
import jax.numpy as jnp
from jax import lax
from jax.experimental import pallas as pl
from jax.experimental.pallas import tpu as pltpu
from jax.sharding import PartitionSpec as P

rope_base = 500000.0
BF16 = jnp.bfloat16
F32 = jnp.float32
MIB = 1024 * 1024
PLACE_STEPS = 2
LANES = 128
ROW_CHUNKS = (320, 192, 128)
VMEM = pl.BlockSpec(memory_space=pltpu.VMEM)
SMEM = pl.BlockSpec(memory_space=pltpu.SMEM)
HBM = pl.BlockSpec(memory_space=pl.ANY)


def row_tables(lengths_row, count, head_dim):
    seg_ends = jnp.cumsum(lengths_row)
    seg_starts = seg_ends - lengths_row
    row_index = jnp.arange(count, dtype=jnp.int32)
    segment = jnp.sum((row_index[:, None] >= seg_ends[None, :]).astype(jnp.int32), axis=1)
    picked = segment[:, None] == jnp.arange(lengths_row.shape[0], dtype=jnp.int32)[None, :]
    seg_first = jnp.sum(jnp.where(picked, seg_starts[None, :], 0), axis=1)
    position = row_index - seg_first
    half_dim = head_dim // 2
    exponent = jnp.arange(half_dim, dtype=F32) * (2.0 / head_dim)
    frequency = jnp.power(F32(rope_base), -exponent)
    angle = position.astype(F32)[:, None] * frequency[None, :]
    cosine, sine = jnp.cos(angle), jnp.sin(angle)
    return (
        jnp.broadcast_to(seg_first.astype(jnp.int32)[:, None], (count, LANES)),
        jnp.concatenate([cosine, cosine], axis=1),
        jnp.concatenate([-sine, sine], axis=1),
    )


def home_sources(home_pos, tok_rows, me):
    target = home_pos - me * tok_rows
    hit = target[None, :] == jnp.arange(tok_rows, dtype=jnp.int32)[:, None]
    packed = jnp.arange(home_pos.shape[0], dtype=jnp.int32)
    source = jnp.sum(jnp.where(hit, packed[None, :], 0), axis=1).astype(jnp.int32)
    return jnp.broadcast_to(source[:, None], (tok_rows, LANES))


class Weights:
    def __init__(self, query, keyval):
        self.query, self.keyval = query, keyval
        self.depth = keyval[0].shape[0]
        self.q_cols, self.kv_cols = query[0][0].shape[1], keyval[0].shape[1]
        self.all_cols = self.q_cols + self.kv_cols
        self.width = math.gcd(512, self.q_cols, self.kv_cols)
        self.blocks = self.all_cols // self.width

    def arrays(self):
        return [piece for pieces in self.query for piece in pieces] + self.keyval

    def refs(self, flat):
        flat = list(flat)
        query = [[flat.pop(0) for _ in pieces] for pieces in self.query]
        return query, flat

    def fetch(self, refs, pick, which, block, buf, sem):
        query, keyval = refs
        q_blocks = self.q_cols // self.width
        is_query = block < q_blocks
        span = pl.ds((block if is_query else block - q_blocks) * self.width, self.width)

        def start():
            for j in range(len(keyval)):
                pieces = query[j] if is_query else [keyval[j]]

                @pl.when(pick == j)
                def _(pieces=pieces):
                    if len(pieces) == 1:
                        pltpu.make_async_copy(pieces[0].at[:, span], buf, sem).start()
                    else:
                        half = self.depth // 2
                        for order in range(2):
                            @pl.when(which == order)
                            def _(order=order):
                                for n, piece in enumerate(pieces):
                                    rows = pl.ds((n ^ order) * half, half)
                                    pltpu.make_async_copy(piece.at[:, span], buf.at[rows], sem).start()

        def wait():
            whole = query[0][0] if is_query else keyval[0]
            pltpu.make_async_copy(whole.at[:, span], buf, sem).wait()

        return start, wait


def project_kernel(w, pieces, chunks, ctrl, *refs):
    steps = len(pieces)
    hidden, refs = list(refs[: sum(pieces)]), refs[sum(pieces) :]
    count = len(w.arrays())
    w_refs, refs = w.refs(refs[:count]), refs[count:]
    outs, refs = refs[: len(chunks)], refs[len(chunks) :]
    kept, held, buf, sem, h_sem, kept_sem = refs
    which = ctrl[steps + 1]
    loads = []
    for s, n in enumerate(pieces):
        first, group = 0, []
        for ref in [hidden.pop(0) for _ in range(n)]:
            rows = ref.shape[0]
            group.append(pltpu.make_async_copy(ref, held.at[s, pl.ds(first, rows)], h_sem.at[s, len(group)]))
            first += rows
        loads.append(group)
    todo = [(block, step) for block in range(w.blocks) for step in range(steps)]
    slots = buf.shape[0]
    copies = [
        w.fetch(w_refs, ctrl[step], which, block, buf.at[i % slots], sem.at[i % slots])
        for i, (block, step) in enumerate(todo)
    ]
    keeps = [w.fetch(w_refs, ctrl[steps], which, block, kept.at[block], kept_sem.at[block]) for block in range(w.blocks)]
    for s, group in enumerate(loads):
        for load in group:
            load.start()
        if s < min(slots - 1, len(todo)):
            copies[s][0]()
    for i in range(steps, min(slots - 1, len(todo))):
        copies[i][0]()
    for i, (block, step) in enumerate(todo):
        if i + slots - 1 < len(todo):
            copies[i + slots - 1][0]()
        if step == steps - 1:
            keeps[block][0]()
        if block == 0:
            for load in loads[step]:
                load.wait()
        copies[i][1]()
        span = slice(block * w.width, (block + 1) * w.width)
        first = 0
        for out, rows in zip(outs, chunks):
            part = jnp.dot(held[step, first : first + rows], buf[i % slots], preferred_element_type=F32)
            if step == 0:
                out[:, span] = part
            else:
                out[:, span] += part
            first += rows
    for _, wait in keeps:
        wait()


def project(ctrl, hidden, w, chunks):
    rows, depth = sum(chunks), hidden[0][0].shape[1]
    pieces = [len(h) for h in hidden]
    steps = len(pieces)
    return pl.pallas_call(
        functools.partial(project_kernel, w, pieces, chunks),
        out_shape=[pltpu.VMEM((r, w.all_cols), F32) for r in chunks]
        + [pltpu.VMEM((w.blocks, depth, w.width), BF16)],
        in_specs=[SMEM] + [HBM] * (sum(pieces) + len(w.arrays())),
        out_specs=[VMEM] * (len(chunks) + 1),
        scratch_shapes=[
            pltpu.VMEM((steps, rows, depth), BF16),
            pltpu.VMEM((4, depth, w.width), BF16),
            pltpu.SemaphoreType.DMA((4,)),
            pltpu.SemaphoreType.DMA((steps, max(pieces))),
            pltpu.SemaphoreType.DMA((w.blocks,)),
        ],
        compiler_params=pltpu.CompilerParams(vmem_limit_bytes=24 * MIB),
        cost_estimate=pl.CostEstimate(
            flops=2 * rows * depth * steps * w.all_cols, bytes_accessed=30_000_000, transcendentals=0
        ),
        name="project",
    )(ctrl, *sum(hidden, []), *w.arrays())


def attend_kernel(heads, kv_heads, head_dim, before, part, kept, raw_in, first_ref, cos_ref, sin_ref, *refs):
    kv_before, refs = refs[: len(before)], refs[len(before) :]
    kv_out, mixed_ref, raw, keys_all, values_all = refs
    rows, earlier = part.shape[0], sum(before)
    blocks, _, width = kept.shape
    group = heads // kv_heads
    q_cols = heads * head_dim
    span = earlier + rows
    top = 0
    for ref, n in zip(kv_before, before):
        for g in range(kv_heads):
            keys_all[g, top : top + n] = ref[:, 2 * g * head_dim : (2 * g + 1) * head_dim]
            values_all[g, top : top + n, :head_dim] = ref[:, (2 * g + 1) * head_dim : (2 * g + 2) * head_dim]
        top += n
    for g in range(kv_heads):
        values_all[g, :, head_dim:] = jnp.ones((span, head_dim), BF16)
    cos, sin = cos_ref[...], sin_ref[...]
    for block in range(blocks)[::-1]:
        cols = slice(block * width, (block + 1) * width)
        raw[:, cols] = raw_in[:, cols] + jnp.dot(part[...], kept[block], preferred_element_type=F32)

    def rotated(first):
        u = raw[:, first : first + head_dim]
        return (u * cos + pltpu.roll(u, head_dim // 2, 1) * sin).astype(BF16)

    for g in range(kv_heads):
        first = 2 * g * head_dim
        key = rotated(q_cols + first)
        value = raw[:, q_cols + first + head_dim : q_cols + first + 2 * head_dim].astype(BF16)
        keys_all[g, earlier:span] = key
        values_all[g, earlier:span, :head_dim] = value
        kv_out[:, first : first + head_dim] = key
        kv_out[:, first + head_dim : first + 2 * head_dim] = value
    row_index = earlier + lax.broadcasted_iota(jnp.int32, (rows, span), 0)
    key_index = lax.broadcasted_iota(jnp.int32, (rows, span), 1)
    allowed = (key_index <= row_index) & (key_index >= first_ref[:, :1])
    scale = math.log2(math.e) / math.sqrt(head_dim)
    for g in range(kv_heads):
        mine = range(g * group, (g + 1) * group)
        query = jnp.concatenate([rotated(h * head_dim) for h in mine], axis=0)
        scores = lax.dot_general(query, keys_all[g], (((1,), (1,)), ((), ())), preferred_element_type=F32)
        scores = jnp.where(allowed[None], scores.reshape(group, rows, span) * scale, -jnp.inf)
        weights = jnp.exp2(scores - jnp.max(scores, axis=2, keepdims=True))
        both = jnp.dot(
            weights.astype(BF16).reshape(group * rows, span), values_all[g], preferred_element_type=F32
        )
        mixed = (both[:, :head_dim] / both[:, head_dim:]).astype(BF16)
        for n, h in enumerate(mine):
            mixed_ref[:, h * head_dim : (h + 1) * head_dim] = mixed[n * rows : (n + 1) * rows]


def attend(part, w, kept, raw, tables, kv_before, head_dim):
    rows, depth = part.shape
    heads, kv_heads = w.q_cols // head_dim, w.kv_cols // (2 * head_dim)
    before = [a.shape[0] for a in kv_before]
    count = sum(before) + rows
    return pl.pallas_call(
        functools.partial(attend_kernel, heads, kv_heads, head_dim, before),
        out_shape=[
            jax.ShapeDtypeStruct((rows, w.kv_cols), BF16),
            jax.ShapeDtypeStruct((rows, w.q_cols), BF16),
        ],
        in_specs=[VMEM] * (6 + len(before)),
        out_specs=[VMEM] * 2,
        scratch_shapes=[
            pltpu.VMEM((rows, w.all_cols), F32),
            pltpu.VMEM((kv_heads, count, head_dim), BF16),
            pltpu.VMEM((kv_heads, count, 2 * head_dim), BF16),
        ],
        compiler_params=pltpu.CompilerParams(vmem_limit_bytes=24 * MIB),
        cost_estimate=pl.CostEstimate(
            flops=2 * rows * depth * w.all_cols + 4 * rows * count * w.q_cols,
            bytes_accessed=15_000_000,
            transcendentals=heads * rows * count,
        ),
        name="attend",
    )(part, kept, raw, *tables, *kv_before)


def place_kernel(tops, tok_rows, more, me_ref, source_ref, *refs):
    blocks, out = refs[: len(refs) - 1 - more], refs[-1]
    rows = out.shape[0]
    peers = len(blocks) // len(tops)
    me = me_ref[0]
    total = refs[len(blocks)][...].astype(F32) if more else None
    for n, block in enumerate(blocks):
        chunk, j = divmod(n, peers)
        base = (me ^ j) * tok_rows + tops[chunk]
        index = lax.broadcasted_iota(jnp.int32, (rows, block.shape[0]), 1)
        onehot = (index == source_ref[:, :1] - base).astype(BF16)
        part = jnp.dot(onehot, block[...], preferred_element_type=F32)
        total = part if total is None else total + part
    out[...] = total.astype(BF16)


def place(me, source, blocks, tops, tok_rows, before=None):
    rows, cols = source.shape[0], blocks[0].shape[1]
    more = [] if before is None else [before]
    step = rows // PLACE_STEPS

    def whole(array):
        return pl.BlockSpec(array.shape, lambda i: (0, 0))

    def strip(width):
        return pl.BlockSpec((step, width), lambda i: (i, 0))

    return pl.pallas_call(
        functools.partial(place_kernel, tops, tok_rows, len(more)),
        grid=(PLACE_STEPS,),
        out_shape=jax.ShapeDtypeStruct((rows, cols), BF16),
        in_specs=[SMEM, strip(source.shape[1])] + [whole(b) for b in blocks] + [strip(cols) for _ in more],
        out_specs=strip(cols),
        compiler_params=pltpu.CompilerParams(vmem_limit_bytes=24 * MIB),
        cost_estimate=pl.CostEstimate(
            flops=2 * rows * cols * sum(b.shape[0] for b in blocks),
            bytes_accessed=8 * rows * cols,
            transcendentals=0,
        ),
        name="place",
    )(me, source, *blocks, *more)


def local(hidden, w_query, w_keyval, seg_lengths, home_pos):
    tok_rows = hidden.shape[0]
    w_rows = w_query.shape[0]
    head_dim = w_keyval.shape[2] // 2
    replicas, columns = lax.axis_size("replica"), lax.axis_size("trow")
    me, my_col, my_group = lax.axis_index("replica"), lax.axis_index("trow"), lax.axis_index("groups")
    flat_keyval = w_keyval.reshape(w_rows, -1)
    total = sum(ROW_CHUNKS)
    chunks = [tok_rows * c // total for c in ROW_CHUNKS]
    tops = [sum(chunks[:n]) for n in range(len(chunks))]

    def swap(block, j):
        return lax.ppermute(block, "replica", [(i, i ^ j) for i in range(replicas)])

    def on(block):
        return lax.ppermute(block, "trow", [(i, (i + 1) % columns) for i in range(columns)])

    small = replicas == 4 and columns == 4
    shard_of = [lax.rem(my_col - k + columns, columns) for k in range(columns)]
    picks = [s ^ me for s in shard_of] if small else shard_of
    ctrl = jnp.stack(picks + [my_group]).astype(jnp.int32)
    rows_of = row_tables(seg_lengths[0], tok_rows, head_dim)
    tables = [[t[top : top + rows] for t in rows_of] for top, rows in zip(tops, chunks)]
    source = home_sources(home_pos, tok_rows, me)
    me_array = me.astype(jnp.int32)[None]
    if small:
        half = w_rows // 2
        h1 = on(hidden)
        mine = swap(lax.dynamic_slice_in_dim(w_query, my_group * half, half, 0), 2)
        query_1, keyval_1 = swap(w_query, 1), swap(flat_keyval, 1)
        h1, mine, keyval_later, ctrl, tables, source, me_array = lax.optimization_barrier(
            (h1, mine, flat_keyval, ctrl, tables, source, me_array)
        )
        h2 = on(h1)
        other = lax.ppermute(mine, "groups", [(0, 1), (1, 0)])
        keyval_2 = swap(keyval_later, 2)
        mine_3 = swap(mine, 1)
        h2, other, keyval_2 = lax.optimization_barrier((h2, other, keyval_2))
        hiddens = [[hidden], [h1], [h2]]
        parts = [on(h2[top : top + rows]) for top, rows in zip(tops, chunks)]
        weights = Weights(
            [[w_query], [query_1], [mine, other], [mine_3, swap(other, 1)]],
            [flat_keyval, keyval_1, keyval_2, swap(keyval_2, 1)],
        )
    else:
        hiddens = [[hidden]]
        for _ in range(columns - 2):
            hiddens.append([on(hiddens[-1][0])])
        parts = [on(hiddens[-1][0][top : top + rows]) for top, rows in zip(tops, chunks)]
        depth = hidden.shape[1]
        all_q = lax.all_gather(w_query, "replica", axis=0, tiled=True)
        all_kv = lax.all_gather(flat_keyval, "replica", axis=0, tiled=True)
        spans = [slice(s * depth, (s + 1) * depth) for s in range(columns)]
        weights = Weights([[all_q[s]] for s in spans], [all_kv[s] for s in spans])
    *raws, kept = project(ctrl, hiddens, weights, chunks)
    kv, mixed = [], []
    for part, raw, table in zip(parts, raws, tables):
        kv_new, mixed_new = attend(part, weights, kept, raw, table, kv, head_dim)
        kv, mixed = kv + [kv_new], mixed + [mixed_new]
    blocks = []
    for n, block in enumerate(mixed):
        if small:
            across = swap(block, 2)
            if n + 1 < len(mixed):
                across, _ = lax.optimization_barrier((across, mixed[n + 1]))
                blocks.append([block, swap(block, 1), across, swap(across, 1)])
            else:
                blocks.append([block, swap(block, 1), across])
        else:
            blocks.append([block] + [swap(block, j) for j in range(1, replicas)])
    source_late, _ = lax.optimization_barrier((source, mixed[-1]))
    placed = place(me_array, source_late, sum(blocks[:-1], []), tops[:-1], tok_rows)
    if small:
        across, placed = lax.optimization_barrier((blocks[-1][2], placed))
        blocks[-1] = blocks[-1][:2] + [across, swap(across, 1)]
    return place(me_array, source_late, blocks[-1], tops[-1:], tok_rows, placed)


def solution(mesh):
    placed = (
        P(("groups", "replica"), "trow"),
        P("replica", "trow"),
        P("replica", "trow", None),
        P(("groups", "replica"), None),
        P("groups"),
    )
    return jax.shard_map(
        local,
        mesh=mesh,
        in_specs=placed,
        out_specs=P(("groups", "replica"), "trow"),
        check_vma=False,
    )
```

time: 224 us -> 200 us (0.89)
  Pallas kernels: 57.7 us -> 33.1 us
  waiting for transfers between devices: 131 us -> 142 us
  local copies, waits for them, and re-layouts: 15.9 us -> 7.82 us
    pallas_call x4, Pallas kernels: 45.8 us -> 26 us  [the longest x1 16.6 us: project(): pl.pallas_call(functools.partial(project_kernel, w, pieces, chunks), out_...]
    ppermute x5, waiting for transfers between devices: 33.8 us -> 47 us  [on(): lax.ppermute(block, 'trow', [(i, (i + 1) % columns) for i in range(column...]
    pallas_call x2, Pallas kernels: 12 us -> 7.16 us  [place(): pl.pallas_call(functools.partial(place_kernel, tops, tok_rows, len(more))...]
    slice x3, local copies, waits for them, and re-layouts: 5.7 us -> 1.27 us  [local(): parts = [on(h2[top:top + rows]) for top, rows in zip(tops, chunks)]]
    ppermute x16, waiting for transfers between devices: 53.9 us -> 51.5 us  [swap(): return lax.ppermute(block, 'replica', [(i, i ^ j) for i in range(replicas)])]
    slice x6 -> x4, local copies, waits for them, and re-layouts: 2.35 us -> 0.08 us  [local(): t[top:top + rows]]
  transfers between devices with their start and end apart: 22 -> 22, of which waited for: 8 -> 13; matrix products, arithmetic and copies ran while one was open for 8% -> 5% of each run, Pallas kernels for 24% -> 15%
where the time goes in v3:
time: 200 us
  waiting for transfers between devices  142 us (71%)
  Pallas kernels  33.1 us (17%)
  starting transfers between devices  13.7 us (7%)
  local copies, waits for them, and re-layouts  7.82 us (4%)
  other arithmetic  2.71 us (1%)
    ppermute x16, waiting for transfers between devices, swap(): return lax.ppermute(block, 'replica', [(i, i ^ j) for i in range(replicas)])  51.5 us
    ppermute x5, waiting for transfers between devices, on(): lax.ppermute(block, 'trow', [(i, (i + 1) % columns) for i in range(column...  47 us
    ppermute x1, waiting for transfers between devices, local(): other = lax.ppermute(mine, 'groups', [(0, 1), (1, 0)])  43.5 us
    pallas_call x1, Pallas kernels, project(): pl.pallas_call(functools.partial(project_kernel, w, pieces, chunks), out_...  16.6 us
    pallas_call x3, Pallas kernels, attend(): pl.pallas_call(functools.partial(attend_kernel, heads, kv_heads, head_dim...  9.37 us
    ppermute x16, starting transfers between devices, swap(): return lax.ppermute(block, 'replica', [(i, i ^ j) for i in range(replicas)])  8.69 us
    pallas_call x2, Pallas kernels, place(): pl.pallas_call(functools.partial(place_kernel, tops, tok_rows, len(more))...  7.16 us
  transfers between devices with their start and end apart: 22, of which 13 were waited for; matrix products, arithmetic and copies ran while one was open for 5% of the time, Pallas kernels for 15%

profile of v3, /device:TPU:0, one launch (start us, length us, event | category | flops | bytes accessed | tf_op | source)
XLA Modules:
  0.0 199.6 jit_solution(1310787337288098262)
XLA Ops:
  0.0 3.0 %collective-permute-start = (bf16[640,2048]{1,0:T(8,128)(2,1)}, bf16[640,2048]{1,0:T(8,128)(2,1)}, u32[]{:S(2)}, u32[]{:S(2)}) collective-permute-start(bf16[640,2048]{1,0:T(8,128)(2,1)} %refs_0_.1), channel_id=1, source_target_pairs={{0,1},{1,2},{2,3},{3,0},{4,5},{5,6},{6,7},{7,4},{8,9},{9,10},{10,1... | collective-permute-start | bytes 7864328 | tf_op jit(solution)/shard_map/ppermute | solution.py:312
  3.0 3.1 %constant_dynamic-slice_fusion = bf16[1024,1024]{1,0:T(8,128)(2,1)} fusion(bf16[2048,1024]{1,0:T(8,128)(2,1)} %refs_3_.1, s32[]{:T(128)S(6)} %select_n.11), kind=kLoop, calls=%fused_computation.28 | loop fusion | bytes 4194308 | tf_op jit(solution)/shard_map/dynamic_slice | solution.py:325
  6.2 1.5 collective-permute-start.1
  7.7 0.2 reduce-window.4
  7.8 0.1 fusion.5
  7.9 0.1 fusion.6
  8.0 0.0 copy-start.3
  8.0 0.1 slice.43
  8.1 2.0 %copy.6 = bf16[256,8,2,256]{3,1,2,0:T(8,128)(2,1)S(1)} copy(bf16[256,8,2,256]{3,2,1,0:T(2,128)(2,1)} %bitcast.19) | data formatting | bytes 4194304
  10.2 0.1 stack.23.ctrl
  10.3 0.0 copy-start.4
  10.3 1.2 multiply_sine_fusion
  11.5 0.0 slice-start
  11.5 0.0 copy-start.2
  11.5 0.1 pad_maximum_fusion
  11.6 0.1 fusion.3
  11.8 0.2 fusion
  11.9 0.8 select_reduce_fusion
  12.7 40.9 %collective-permute-done.1.refs_5_ = bf16[1024,1024]{1,0:T(8,128)(2,1)} collective-permute-done((bf16[1024,1024]{1,0:T(8,128)(2,1)}, bf16[1024,1024]{1,0:T(8,128)(2,1)}, u32[]{:S(2)}, u32[]{:S(2)}) %collective-permute-start.1) | collective-permute-done | bytes 2097184 | tf_op jit(solution)/shard_map/ppermute | solution.py:309
  53.6 8.7 %collective-permute-done.refs_1_ = bf16[640,2048]{1,0:T(8,128)(2,1)} collective-permute-done((bf16[640,2048]{1,0:T(8,128)(2,1)}, bf16[640,2048]{1,0:T(8,128)(2,1)}, u32[]{:S(2)}, u32[]{:S(2)}) %collective-permute-start) | collective-permute-done | bytes 2621472 | tf_op jit(solution)/shard_map/ppermute | solution.py:312
  62.2 0.1 broadcast_in_dim.63.source_ref
  62.4 0.1 broadcast_in_dim.58.first_ref
  62.5 0.1 broadcast_in_dim.59.first_ref
  62.6 0.1 broadcast_in_dim.60.first_ref
  62.7 0.0 copy-start
  62.7 0.1 collective-permute-start.2
  62.7 1.6 collective-permute-start.3
  64.3 1.5 collective-permute-start.4
  65.8 0.0 collective-permute-start.6
  65.8 0.5 collective-permute-start.9
  66.3 43.5 %collective-permute-done.3.refs_6_ = bf16[1024,1024]{1,0:T(8,128)(2,1)S(1)} collective-permute-done((bf16[1024,1024]{1,0:T(8,128)(2,1)}, bf16[1024,1024]{1,0:T(8,128)(2,1)S(1)}, u32[]{:S(2)}, u32[]{:S(2)}) %collective-permute-start.3) | collective-permute-done | bytes 2097184 | tf_op jit(solution)/shard_map/ppermute | solution.py:331
  109.8 0.8 collective-permute-done.4.refs_11_
  110.6 12.2 %collective-permute-done.2.refs_2_ = bf16[640,2048]{1,0:T(8,128)(2,1)S(1)} collective-permute-done((bf16[640,2048]{1,0:T(8,128)(2,1)}, bf16[640,2048]{1,0:T(8,128)(2,1)S(1)}, u32[]{:S(2)}, u32[]{:S(2)}) %collective-permute-start.2) | collective-permute-done | bytes 2621472 | tf_op jit(solution)/shard_map/ppermute | solution.py:312
  122.8 0.0 collective-permute-start.10
  122.8 0.5 collective-permute-start.8
  123.3 0.1 slice.50
  123.4 0.1 collective-permute-start.11
  123.5 0.1 slice.51
  123.6 0.8 copy-done.1
  124.4 0.0 collective-permute-done.7.refs_7_
  124.4 2.6 %collective-permute-done.10.refs_12_ = bf16[2048,512]{1,0:T(8,128)(2,1)S(1)} collective-permute-done((bf16[2048,512]{1,0:T(8,128)(2,1)S(1)}, bf16[2048,512]{1,0:T(8,128)(2,1)S(1)}, u32[]{:S(2)}, u32[]{:S(2)}) %collective-permute-start.10) | collective-permute-done | bytes 2097184 | tf_op jit(solution)/shard_map/ppermute | solution.py:309
  126.9 3.0 %collective-permute-done.8.refs_8_ = bf16[1024,1024]{1,0:T(8,128)(2,1)S(1)} collective-permute-done((bf16[1024,1024]{1,0:T(8,128)(2,1)S(1)}, bf16[1024,1024]{1,0:T(8,128)(2,1)S(1)}, u32[]{:S(2)}, u32[]{:S(2)}) %collective-permute-start.8) | collective-permute-done | bytes 2097184 | tf_op jit(solution)/shard_map/ppermute | solution.py:309
  129.9 16.6 %project.1 = (f32[320,1536]{1,0:T(8,128)S(1)}, f32[192,1536]{1,0:T(8,128)S(1)}, f32[128,1536]{1,0:T(8,128)S(1)}, bf16[3,2048,512]{2,1,0:T(8,128)(2,1)S(1)}) custom-call(s32[5]{0:T(128)S(1)} %stack.23.ctrl, bf16[640,2048]{1,0:T(8,128)(2,1)S(1)} %copy-done, bf16[640,2048]{1,0:T(8,128)(2,1)} %collective-permute-done.refs_1_, bf16[640,2048]{1,0:T(8,128)(2,1)} %copy-done.1, ...), custom_call_target="tpu_custom_call" | custom-call | flops 12079595520 | bytes 30000000 | tf_op jit(solution)/shard_map/project/pallas_call | solution.py:154
  146.6 10.4 %collective-permute-done.11.part = bf16[320,2048]{1,0:T(8,128)(2,1)S(1)} collective-permute-done((bf16[320,2048]{1,0:T(8,128)(2,1)S(1)}, bf16[320,2048]{1,0:T(8,128)(2,1)S(1)}, u32[]{:S(2)}, u32[]{:S(2)}) %collective-permute-start.11) | collective-permute-done | bytes 1310752 | tf_op jit(solution)/shard_map/ppermute | solution.py:312
  156.9 3.8 %attend.3 = (bf16[320,512]{1,0:T(8,128)(2,1)S(1)}, bf16[320,1024]{1,0:T(8,128)(2,1)S(1)}) custom-call(bf16[320,2048]{1,0:T(8,128)(2,1)S(1)} %collective-permute-done.11.part, bf16[3,2048,512]{2,1,0:T(8,128)(2,1)S(1)} %get-tuple-element.46.kept, f32[320,1536]{1,0:T(8,128)S(1)} %get-tuple-element.51.raw_in, s32[320,128]{1,0:T(8,128)S(1)} %broadcast_in_dim.58.first_ref, ...), custom_call_target="tpu_custom_call" | custom-call | flops 2432696320 | bytes 15000000 | tf_op jit(solution)/shard_map/attend/pallas_call | solution.py:231
  160.7 1.3 collective-permute-start.16
  162.0 1.1 slice.49
  163.1 0.3 collective-permute-start.5
  163.4 10.4 %collective-permute-done.12.part = bf16[192,2048]{1,0:T(8,128)(2,1)S(1)} collective-permute-done((bf16[192,2048]{1,0:T(8,128)(2,1)S(1)}, bf16[192,2048]{1,0:T(8,128)(2,1)S(1)}, u32[]{:S(2)}, u32[]{:S(2)}) %collective-permute-start.12) | collective-permute-done | bytes 786464 | tf_op jit(solution)/shard_map/ppermute | solution.py:312
  173.8 3.1 %attend.4 = (bf16[192,512]{1,0:T(8,128)(2,1)S(1)}, bf16[192,1024]{1,0:T(8,128)(2,1)S(1)}) custom-call(bf16[192,2048]{1,0:T(8,128)(2,1)S(1)} %collective-permute-done.12.part, bf16[3,2048,512]{2,1,0:T(8,128)(2,1)S(1)} %get-tuple-element.46.kept, f32[192,1536]{1,0:T(8,128)S(1)} %get-tuple-element.56.raw_in, s32[192,128]{1,0:T(8,128)S(1)} %broadcast_in_dim.59.first_ref, ...), custom_call_target="tpu_custom_call" | custom-call | flops 1610612736 | bytes 15000000 | tf_op jit(solution)/shard_map/attend/pallas_call | solution.py:231
  176.9 1.3 collective-permute-start.19
  178.2 0.5 collective-permute-start.17
  178.7 0.0 collective-permute-start.18
  178.7 5.4 %collective-permute-done.5.part = bf16[128,2048]{1,0:T(8,128)(2,1)S(1)} collective-permute-done((bf16[128,2048]{1,0:T(8,128)(2,1)S(1)}, bf16[128,2048]{1,0:T(8,128)(2,1)S(1)}, u32[]{:S(2)}, u32[]{:S(2)}) %collective-permute-start.5) | collective-permute-done | bytes 524320 | tf_op jit(solution)/shard_map/ppermute | solution.py:312
  184.1 2.6 %attend.5 = (bf16[128,512]{1,0:T(8,128)(2,1)}, bf16[128,1024]{1,0:T(8,128)(2,1)S(1)}) custom-call(bf16[128,2048]{1,0:T(8,128)(2,1)S(1)} %collective-permute-done.5.part, bf16[3,2048,512]{2,1,0:T(8,128)(2,1)S(1)} %get-tuple-element.46.kept, f32[128,1536]{1,0:T(8,128)S(1)} %get-tuple-element.47.raw_in, s32[128,128]{1,0:T(8,128)S(1)} %broadcast_in_dim.60.first_ref, ...), custom_call_target="tpu_custom_call" | custom-call | flops 1140850688 | bytes 15000000 | tf_op jit(solution)/shard_map/attend/pallas_call | solution.py:231
  186.6 0.0 collective-permute-done.19.refs_6_
  186.6 0.1 collective-permute-start.20
  186.7 1.3 collective-permute-start.14
  188.0 0.2 collective-permute-start.13
  188.2 0.2 collective-permute-done.20.refs_7_
  188.4 4.5 %place.2.refs_4_ = bf16[640,1024]{1,0:T(8,128)(2,1)S(1)} custom-call(s32[1]{0:T(128)} %bitcast.9.me_ref, s32[640,128]{1,0:T(8,128)S(1)} %broadcast_in_dim.63.source_ref, bf16[320,1024]{1,0:T(8,128)(2,1)S(1)} %get-tuple-element.63.refs_0_, bf16[320,1024]{1,0:T(8,128)(2,1)S(1)} %collective-permute-done.15.refs_1_, ...), custom_call_target="tpu_custom_call" | custom-call | flops 2684354560 | bytes 5242880 | tf_op jit(solution)/shard_map/place/pallas_call | solution.py:281
  193.0 2.5 %collective-permute-done.14.refs_2_ = bf16[128,1024]{1,0:T(8,128)(2,1)S(1)} collective-permute-done((bf16[128,1024]{1,0:T(8,128)(2,1)S(1)}, bf16[128,1024]{1,0:T(8,128)(2,1)S(1)}, u32[]{:S(2)}, u32[]{:S(2)}) %collective-permute-start.14) | collective-permute-done | bytes 262176 | tf_op jit(solution)/shard_map/ppermute | solution.py:309
  195.4 1.5 collective-permute-done.21.refs_3_
  197.0 2.6 %place.3 = bf16[640,1024]{1,0:T(8,128)(2,1)} custom-call(s32[1]{0:T(128)} %bitcast.9.me_ref, s32[640,128]{1,0:T(8,128)S(1)} %broadcast_in_dim.63.source_ref, bf16[128,1024]{1,0:T(8,128)(2,1)S(1)} %get-tuple-element.61.refs_0_, bf16[128,1024]{1,0:T(8,128)(2,1)S(1)} %collective-permute-done.13.refs_1_, bf16[128,1024]{1,0:T(8,128)(2,1)S(1)} %collective-permute-done.14.refs_2_, ...), custom_call_target="tpu_custom_call" | custom-call | flops 671088640 | bytes 5242880 | tf_op jit(solution)/shard_map/place/pallas_call | solution.py:281
  (26 shorter events, 0.1 us)
Async XLA Ops:
  0.0 62.2 %collective-permute-start = (bf16[640,2048]{1,0:T(8,128)(2,1)}, bf16[640,2048]{1,0:T(8,128)(2,1)}, u32[]{:S(2)}, u32[]{:S(2)}) collective-permute-start(bf16[640,2048]{1,0:T(8,128)(2,1)} %refs_0_.1), channel_id=1, source_target_pairs={{0,1},{1,2},{2,3},{3,0},{4,5},{5,6},{6,7},{7,4},{8,9},{9,10},{10,1... | collective-permute-start | bytes 7864328 | tf_op jit(solution)/shard_map/ppermute | solution.py:312
  3.0 4.6 %copy-start.6 = (s32[1,2]{1,0:T(1,128)S(1)}, s32[1,2]{1,0:T(1,128)}, u32[]{:S(2)}) copy-start(s32[1,2]{1,0:T(1,128)} %param.8) | copy-start | bytes 28
  6.2 47.4 %collective-permute-start.1 = (bf16[1024,1024]{1,0:T(8,128)(2,1)}, bf16[1024,1024]{1,0:T(8,128)(2,1)}, u32[]{:S(2)}, u32[]{:S(2)}) collective-permute-start(bf16[1024,1024]{1,0:T(8,128)(2,1)} %constant_dynamic-slice_fusion), channel_id=1, source_target_pairs={{0,8},{4,12},{8,0},{12,4},{1,9},{5,13},{9,1},{13,5},{2,10},{6,14},... | collective-permute-start | bytes 6291464 | tf_op jit(solution)/shard_map/ppermute | solution.py:309
  8.0 2.2 %copy-start.3 = (s32[640]{0:T(1024)}, s32[640]{0:T(1024)S(1)}, u32[]{:S(2)}) copy-start(s32[640]{0:T(1024)S(1)} %fusion.6) | copy-start | bytes 7684
  10.3 1.7 copy-start.4
  11.5 50.9 %slice-start = ((s32[640]{0:T(1024)}), s32[320]{0:T(512)S(1)}, s32[]{:S(2)}) async-start(s32[640]{0:T(1024)} %copy-done.3), calls=%async_computation | async-start | bytes 4096 | tf_op jit(solution)/shard_map/slice | solution.py:319
  11.5 54.3 %copy-start.2 = (bf16[2048,1024]{1,0:T(8,128)(2,1)S(1)}, bf16[2048,1024]{1,0:T(8,128)(2,1)}, u32[]{:S(2)}) copy-start(bf16[2048,1024]{1,0:T(8,128)(2,1)} %refs_3_.1) | copy-start | bytes 12582916
  62.7 67.3 %copy-start = (bf16[640,2048]{1,0:T(8,128)(2,1)S(1)}, bf16[640,2048]{1,0:T(8,128)(2,1)}, u32[]{:S(2)}) copy-start(bf16[640,2048]{1,0:T(8,128)(2,1)} %refs_0_.1) | copy-start | bytes 7864324
  62.7 60.1 %collective-permute-start.2 = (bf16[640,2048]{1,0:T(8,128)(2,1)}, bf16[640,2048]{1,0:T(8,128)(2,1)S(1)}, u32[]{:S(2)}, u32[]{:S(2)}) collective-permute-start(bf16[640,2048]{1,0:T(8,128)(2,1)} %collective-permute-done.refs_1_), channel_id=1, source_target_pairs={{0,1},{1,2},{2,3},{3,0},{4,5},{5,6},{6,7},{7,4},{8,9},{9,10},{10,1... | collective-permute-start | bytes 7864328 | tf_op jit(solution)/shard_map/ppermute | solution.py:312
  62.7 47.1 %collective-permute-start.3 = (bf16[1024,1024]{1,0:T(8,128)(2,1)}, bf16[1024,1024]{1,0:T(8,128)(2,1)S(1)}, u32[]{:S(2)}, u32[]{:S(2)}) collective-permute-start(bf16[1024,1024]{1,0:T(8,128)(2,1)} %collective-permute-done.1.refs_5_), channel_id=1, source_target_pairs={{0,16},{16,0},{1,17},{17,1},{2,18},{18,2},{3,19},{19,3},{4,20},{20... | collective-permute-start | bytes 6291464 | tf_op jit(solution)/shard_map/ppermute | solution.py:331
  64.3 46.3 %collective-permute-start.4 = (bf16[2048,512]{1,0:T(8,128)(2,1)S(1)}, bf16[2048,512]{1,0:T(8,128)(2,1)S(1)}, u32[]{:S(2)}, u32[]{:S(2)}) collective-permute-start(bf16[2048,512]{1,0:T(8,128)(2,1)S(1)} %bitcast.16), channel_id=1, source_target_pairs={{0,8},{4,12},{8,0},{12,4},{1,9},{5,13},{9,1},{13,5},{2,10},{6,14},... | collective-permute-start | bytes 6291464 | tf_op jit(solution)/shard_map/ppermute | solution.py:309
  65.8 58.5 %collective-permute-start.6 = (bf16[2048,1024]{1,0:T(8,128)(2,1)S(1)}, bf16[2048,1024]{1,0:T(8,128)(2,1)S(1)}, u32[]{:S(2)}, u32[]{:S(2)}) collective-permute-start(bf16[2048,1024]{1,0:T(8,128)(2,1)S(1)} %copy-done.2), channel_id=1, source_target_pairs={{0,4},{4,0},{8,12},{12,8},{1,5},{5,1},{9,13},{13,9},{2,6},{6,2},{1... | collective-permute-start | bytes 12582920 | tf_op jit(solution)/shard_map/ppermute | solution.py:309
  65.8 57.6 %collective-permute-start.9 = (bf16[2048,512]{1,0:T(8,128)(2,1)S(1)}, bf16[2048,512]{1,0:T(8,128)(2,1)S(1)}, u32[]{:S(2)}, u32[]{:S(2)}) collective-permute-start(bf16[2048,512]{1,0:T(8,128)(2,1)S(1)} %bitcast.17), channel_id=1, source_target_pairs={{0,4},{4,0},{8,12},{12,8},{1,5},{5,1},{9,13},{13,9},{2,6},{6,2},{1... | collective-permute-start | bytes 6291464 | tf_op jit(solution)/shard_map/ppermute | solution.py:309
  109.8 14.5 %collective-permute-start.7 = (bf16[1024,1024]{1,0:T(8,128)(2,1)}, bf16[1024,1024]{1,0:T(8,128)(2,1)S(1)}, u32[]{:S(2)}, u32[]{:S(2)}) collective-permute-start(bf16[1024,1024]{1,0:T(8,128)(2,1)} %collective-permute-done.1.refs_5_), channel_id=1, source_target_pairs={{0,4},{4,0},{8,12},{12,8},{1,5},{5,1},{9,13},{13,9},{2,6},{6,2},{1... | collective-permute-start | bytes 6291464 | tf_op jit(solution)/shard_map/ppermute | solution.py:309
  122.8 1.6 copy-start.1
  122.8 4.2 %collective-permute-start.10 = (bf16[2048,512]{1,0:T(8,128)(2,1)S(1)}, bf16[2048,512]{1,0:T(8,128)(2,1)S(1)}, u32[]{:S(2)}, u32[]{:S(2)}) collective-permute-start(bf16[2048,512]{1,0:T(8,128)(2,1)S(1)} %collective-permute-done.4.refs_11_), channel_id=1, source_target_pairs={{0,4},{4,0},{8,12},{12,8},{1,5},{5,1},{9,13},{13,9},{2,6},{6,2},{1... | collective-permute-start | bytes 6291464 | tf_op jit(solution)/shard_map/ppermute | solution.py:309
  122.8 7.2 %collective-permute-start.8 = (bf16[1024,1024]{1,0:T(8,128)(2,1)S(1)}, bf16[1024,1024]{1,0:T(8,128)(2,1)S(1)}, u32[]{:S(2)}, u32[]{:S(2)}) collective-permute-start(bf16[1024,1024]{1,0:T(8,128)(2,1)S(1)} %collective-permute-done.3.refs_6_), channel_id=1, source_target_pairs={{0,4},{4,0},{8,12},{12,8},{1,5},{5,1},{9,13},{13,9},{2,6},{6,2},{1... | collective-permute-start | bytes 6291464 | tf_op jit(solution)/shard_map/ppermute | solution.py:309
  123.4 33.5 %collective-permute-start.11 = (bf16[320,2048]{1,0:T(8,128)(2,1)S(1)}, bf16[320,2048]{1,0:T(8,128)(2,1)S(1)}, u32[]{:S(2)}, u32[]{:S(2)}) collective-permute-start(bf16[320,2048]{1,0:T(8,128)(2,1)S(1)} %slice.50), channel_id=1, source_target_pairs={{0,1},{1,2},{2,3},{3,0},{4,5},{5,6},{6,7},{7,4},{8,9},{9,10},{10,1... | collective-permute-start | bytes 3932168 | tf_op jit(solution)/shard_map/ppermute | solution.py:312
  124.4 2.6 %copy-start.5 = (bf16[2048,1024]{1,0:T(8,128)(2,1)}, bf16[2048,1024]{1,0:T(8,128)(2,1)S(1)}, u32[]{:S(2)}) copy-start(bf16[2048,1024]{1,0:T(8,128)(2,1)S(1)} %collective-permute-done.6.refs_4_) | copy-start | bytes 12582916
  124.4 49.4 %collective-permute-start.12 = (bf16[192,2048]{1,0:T(8,128)(2,1)S(1)}, bf16[192,2048]{1,0:T(8,128)(2,1)S(1)}, u32[]{:S(2)}, u32[]{:S(2)}) collective-permute-start(bf16[192,2048]{1,0:T(8,128)(2,1)S(1)} %slice.51), channel_id=1, source_target_pairs={{0,1},{1,2},{2,3},{3,0},{4,5},{5,6},{6,7},{7,4},{8,9},{9,10},{10,1... | collective-permute-start | bytes 2359304 | tf_op jit(solution)/shard_map/ppermute | solution.py:312
  160.7 17.5 %collective-permute-start.16 = (bf16[320,1024]{1,0:T(8,128)(2,1)S(1)}, bf16[320,1024]{1,0:T(8,128)(2,1)S(1)}, u32[]{:S(2)}, u32[]{:S(2)}) collective-permute-start(bf16[320,1024]{1,0:T(8,128)(2,1)S(1)} %get-tuple-element.63.refs_0_), channel_id=1, source_target_pairs={{0,8},{4,12},{8,0},{12,4},{1,9},{5,13},{9,1},{13,5},{2,10},{6,14},... | collective-permute-start | bytes 1966088 | tf_op jit(solution)/shard_map/ppermute | solution.py:309
  163.1 21.0 %collective-permute-start.5 = (bf16[128,2048]{1,0:T(8,128)(2,1)S(1)}, bf16[128,2048]{1,0:T(8,128)(2,1)S(1)}, u32[]{:S(2)}, u32[]{:S(2)}) collective-permute-start(bf16[128,2048]{1,0:T(8,128)(2,1)S(1)} %slice.49), channel_id=1, source_target_pairs={{0,1},{1,2},{2,3},{3,0},{4,5},{5,6},{6,7},{7,4},{8,9},{9,10},{10,1... | collective-permute-start | bytes 1572872 | tf_op jit(solution)/shard_map/ppermute | solution.py:312
  176.9 9.8 %collective-permute-start.19 = (bf16[192,1024]{1,0:T(8,128)(2,1)S(1)}, bf16[192,1024]{1,0:T(8,128)(2,1)S(1)}, u32[]{:S(2)}, u32[]{:S(2)}) collective-permute-start(bf16[192,1024]{1,0:T(8,128)(2,1)S(1)} %get-tuple-element.64.refs_4_), channel_id=1, source_target_pairs={{0,8},{4,12},{8,0},{12,4},{1,9},{5,13},{9,1},{13,5},{2,10},{6,14},... | collective-permute-start | bytes 1179656 | tf_op jit(solution)/shard_map/ppermute | solution.py:309
  178.2 10.0 %collective-permute-start.15 = (bf16[320,1024]{1,0:T(8,128)(2,1)S(1)}, bf16[320,1024]{1,0:T(8,128)(2,1)S(1)}, u32[]{:S(2)}, u32[]{:S(2)}) collective-permute-start(bf16[320,1024]{1,0:T(8,128)(2,1)S(1)} %get-tuple-element.63.refs_0_), channel_id=1, source_target_pairs={{0,4},{4,0},{8,12},{12,8},{1,5},{5,1},{9,13},{13,9},{2,6},{6,2},{1... | collective-permute-start | bytes 1966088 | tf_op jit(solution)/shard_map/ppermute | solution.py:309
  178.2 10.2 %collective-permute-start.17 = (bf16[320,1024]{1,0:T(8,128)(2,1)S(1)}, bf16[320,1024]{1,0:T(8,128)(2,1)S(1)}, u32[]{:S(2)}, u32[]{:S(2)}) collective-permute-start(bf16[320,1024]{1,0:T(8,128)(2,1)S(1)} %collective-permute-done.16.refs_2_), channel_id=1, source_target_pairs={{0,4},{4,0},{8,12},{12,8},{1,5},{5,1},{9,13},{13,9},{2,6},{6,2},{1... | collective-permute-start | bytes 1966088 | tf_op jit(solution)/shard_map/ppermute | solution.py:309
  178.7 9.3 %collective-permute-start.18 = (bf16[192,1024]{1,0:T(8,128)(2,1)S(1)}, bf16[192,1024]{1,0:T(8,128)(2,1)S(1)}, u32[]{:S(2)}, u32[]{:S(2)}) collective-permute-start(bf16[192,1024]{1,0:T(8,128)(2,1)S(1)} %get-tuple-element.64.refs_4_), channel_id=1, source_target_pairs={{0,4},{4,0},{8,12},{12,8},{1,5},{5,1},{9,13},{13,9},{2,6},{6,2},{1... | collective-permute-start | bytes 1179656 | tf_op jit(solution)/shard_map/ppermute | solution.py:309
  186.6 1.8 collective-permute-start.20
  186.7 8.7 %collective-permute-start.14 = (bf16[128,1024]{1,0:T(8,128)(2,1)S(1)}, bf16[128,1024]{1,0:T(8,128)(2,1)S(1)}, u32[]{:S(2)}, u32[]{:S(2)}) collective-permute-start(bf16[128,1024]{1,0:T(8,128)(2,1)S(1)} %get-tuple-element.61.refs_0_), channel_id=1, source_target_pairs={{0,8},{4,12},{8,0},{12,4},{1,9},{5,13},{9,1},{13,5},{2,10},{6,14},... | collective-permute-start | bytes 786440 | tf_op jit(solution)/shard_map/ppermute | solution.py:309
  188.0 7.4 %collective-permute-start.13 = (bf16[128,1024]{1,0:T(8,128)(2,1)S(1)}, bf16[128,1024]{1,0:T(8,128)(2,1)S(1)}, u32[]{:S(2)}, u32[]{:S(2)}) collective-permute-start(bf16[128,1024]{1,0:T(8,128)(2,1)S(1)} %get-tuple-element.61.refs_0_), channel_id=1, source_target_pairs={{0,4},{4,0},{8,12},{12,8},{1,5},{5,1},{9,13},{13,9},{2,6},{6,2},{1... | collective-permute-start | bytes 786440 | tf_op jit(solution)/shard_map/ppermute | solution.py:309
  195.4 1.5 collective-permute-start.21

commit v4 on v3

--- a/solution.py
+++ b/solution.py
@@ -12,7 +12,7 @@
 BF16 = jnp.bfloat16
 F32 = jnp.float32
 MIB = 1024 * 1024
-PLACE_STEPS = 2
+PLACE_STEPS = 5
 LANES = 128
 ROW_CHUNKS = (320, 192, 128)
 VMEM = pl.BlockSpec(memory_space=pltpu.VMEM)
@@ -251,39 +251,48 @@
     )(part, kept, raw, *tables, *kv_before)
 
 
-def place_kernel(tops, tok_rows, more, me_ref, source_ref, *refs):
-    blocks, out = refs[: len(refs) - 1 - more], refs[-1]
-    rows = out.shape[0]
-    peers = len(blocks) // len(tops)
+def place_kernel(spans, tok_rows, more, final, me_ref, source_ref, *refs):
+    blocks, refs = refs[: len(spans)], refs[len(spans) :]
+    before, refs = refs[:more], refs[more:]
+    out = refs[0]
+    rows = source_ref.shape[0]
+    step = rows // PLACE_STEPS
     me = me_ref[0]
-    total = refs[len(blocks)][...].astype(F32) if more else None
-    for n, block in enumerate(blocks):
-        chunk, j = divmod(n, peers)
-        base = (me ^ j) * tok_rows + tops[chunk]
-        index = lax.broadcasted_iota(jnp.int32, (rows, block.shape[0]), 1)
-        onehot = (index == source_ref[:, :1] - base).astype(BF16)
-        part = jnp.dot(onehot, block[...], preferred_element_type=F32)
-        total = part if total is None else total + part
-    out[...] = total.astype(BF16)
-
-
-def place(me, source, blocks, tops, tok_rows, before=None):
+    writes = []
+    for i in range(PLACE_STEPS):
+        strip = slice(i * step, (i + 1) * step)
+        total = before[0][strip].astype(F32) if more else None
+        for block, parts in zip(blocks, spans):
+            for first, count, j, top in parts:
+                base = (me ^ j) * tok_rows + top
+                index = lax.broadcasted_iota(jnp.int32, (step, count), 1)
+                onehot = (index == source_ref[strip, :1] - base).astype(BF16)
+                part = jnp.dot(onehot, block[first : first + count], preferred_element_type=F32)
+                total = part if total is None else total + part
+        if final:
+            held, sem = refs[1:]
+            held[strip] = total.astype(BF16)
+            span = pl.ds(i * step, step)
+            writes.append(pltpu.make_async_copy(held.at[span], out.at[span], sem.at[i]))
+            writes[-1].start()
+        else:
+            out[strip] = total.astype(BF16)
+    for write in writes:
+        write.wait()
+
+
+def place(me, source, arrived, tok_rows, before=None):
+    blocks, spans = [a for a, _ in arrived], [p for _, p in arrived]
     rows, cols = source.shape[0], blocks[0].shape[1]
     more = [] if before is None else [before]
-    step = rows // PLACE_STEPS
-
-    def whole(array):
-        return pl.BlockSpec(array.shape, lambda i: (0, 0))
-
-    def strip(width):
-        return pl.BlockSpec((step, width), lambda i: (i, 0))
-
+    final = len(more)
+    scratch = [pltpu.VMEM((rows, cols), BF16), pltpu.SemaphoreType.DMA((PLACE_STEPS,))]
     return pl.pallas_call(
-        functools.partial(place_kernel, tops, tok_rows, len(more)),
-        grid=(PLACE_STEPS,),
+        functools.partial(place_kernel, spans, tok_rows, len(more), final),
         out_shape=jax.ShapeDtypeStruct((rows, cols), BF16),
-        in_specs=[SMEM, strip(source.shape[1])] + [whole(b) for b in blocks] + [strip(cols) for _ in more],
-        out_specs=strip(cols),
+        in_specs=[SMEM] + [VMEM] * (1 + len(blocks) + len(more)),
+        out_specs=HBM if final else VMEM,
+        scratch_shapes=scratch if final else [],
         compiler_params=pltpu.CompilerParams(vmem_limit_bytes=24 * MIB),
         cost_estimate=pl.CostEstimate(
             flops=2 * rows * cols * sum(b.shape[0] for b in blocks),
@@ -307,6 +316,9 @@
 
     def swap(block, j):
         return lax.ppermute(block, "replica", [(i, i ^ j) for i in range(replicas)])
+
+    def after(block, *others):
+        return lax.optimization_barrier((block, *others))[0]
 
     def on(block):
         return lax.ppermute(block, "trow", [(i, (i + 1) % columns) for i in range(columns)])
@@ -324,14 +336,12 @@
         h1 = on(hidden)
         mine = swap(lax.dynamic_slice_in_dim(w_query, my_group * half, half, 0), 2)
         query_1, keyval_1 = swap(w_query, 1), swap(flat_keyval, 1)
-        h1, mine, keyval_later, ctrl, tables, source, me_array = lax.optimization_barrier(
-            (h1, mine, flat_keyval, ctrl, tables, source, me_array)
-        )
+        mine, ctrl, tables, source, me_array = lax.optimization_barrier((mine, ctrl, tables, source, me_array))
+        h1, mine, keyval_later = lax.optimization_barrier((h1, mine, flat_keyval))
         h2 = on(h1)
         other = lax.ppermute(mine, "groups", [(0, 1), (1, 0)])
         keyval_2 = swap(keyval_later, 2)
         mine_3 = swap(mine, 1)
-        h2, other, keyval_2 = lax.optimization_barrier((h2, other, keyval_2))
         hiddens = [[hidden], [h1], [h2]]
         parts = [on(h2[top : top + rows]) for top, rows in zip(tops, chunks)]
         weights = Weights(
@@ -353,23 +363,25 @@
     for part, raw, table in zip(parts, raws, tables):
         kv_new, mixed_new = attend(part, weights, kept, raw, table, kv, head_dim)
         kv, mixed = kv + [kv_new], mixed + [mixed_new]
-    blocks = []
-    for n, block in enumerate(mixed):
-        if small:
+    last = len(mixed) - 1
+    early, late = [], []
+    for n, (block, top, rows) in enumerate(zip(mixed, tops, chunks)):
+        if not small:
+            arrived = [swap(block, j) if j else block for j in range(replicas)]
+        else:
             across = swap(block, 2)
-            if n + 1 < len(mixed):
-                across, _ = lax.optimization_barrier((across, mixed[n + 1]))
-                blocks.append([block, swap(block, 1), across, swap(across, 1)])
-            else:
-                blocks.append([block, swap(block, 1), across])
-        else:
-            blocks.append([block] + [swap(block, j) for j in range(1, replicas)])
-    source_late, _ = lax.optimization_barrier((source, mixed[-1]))
-    placed = place(me_array, source_late, sum(blocks[:-1], []), tops[:-1], tok_rows)
+            arrived = [block, swap(block, 1), across]
+            if n < last:
+                arrived[2] = after(across, mixed[n + 1])
+                arrived.append(swap(arrived[2], 1))
+        (late if n == last else early).extend((a, [(0, rows, j, top)]) for j, a in enumerate(arrived))
+    source_late = after(source, mixed[last])
+    placed = place(me_array, source_late, early, tok_rows)
     if small:
-        across, placed = lax.optimization_barrier((blocks[-1][2], placed))
-        blocks[-1] = blocks[-1][:2] + [across, swap(across, 1)]
-    return place(me_array, source_late, blocks[-1], tops[-1:], tok_rows, placed)
+        final, placed = lax.optimization_barrier((late[2][0], placed))
+        late[2] = (final, late[2][1])
+        late.append((swap(final, 1), [(0, chunks[last], 3, tops[last])]))
+    return place(me_array, source_late, late, tok_rows, placed)
 
 
 def solution(mesh):

time: 200 us -> 199 us (level)
  local copies, waits for them, and re-layouts: 7.82 us -> 10.2 us
  waiting for transfers between devices: 142 us -> 140 us
    ppermute x1, waiting for transfers between devices: 43.5 us -> 1.42 us  [local(): other = lax.ppermute(mine, 'groups', [(0, 1), (1, 0)])]
    ppermute x16, waiting for transfers between devices: 51.5 us -> 91.1 us  [swap(): return lax.ppermute(block, 'replica', [(i, i ^ j) for i in range(replicas)])]
    unnamed x15, local copies, waits for them, and re-layouts: 2.85 us -> 5.26 us
where the time goes in v4:
time: 199 us
  waiting for transfers between devices  140 us (70%)
  Pallas kernels  32.6 us (16%)
  starting transfers between devices  12.6 us (6%)
  local copies, waits for them, and re-layouts  10.2 us (5%)
  other arithmetic  2.71 us (1%)
    ppermute x16, waiting for transfers between devices, swap(): return lax.ppermute(block, 'replica', [(i, i ^ j) for i in range(replicas)])  91.1 us
    ppermute x5, waiting for transfers between devices, on(): lax.ppermute(block, 'trow', [(i, (i + 1) % columns) for i in range(column...  47.9 us
    pallas_call x1, Pallas kernels, project(): pl.pallas_call(functools.partial(project_kernel, w, pieces, chunks), out_...  16.6 us
    pallas_call x3, Pallas kernels, attend(): pl.pallas_call(functools.partial(attend_kernel, heads, kv_heads, head_dim...  9.38 us
    ppermute x16, starting transfers between devices, swap(): return lax.ppermute(block, 'replica', [(i, i ^ j) for i in range(replicas)])  7.74 us
    pallas_call x2, Pallas kernels, place(): pl.pallas_call(functools.partial(place_kernel, spans, tok_rows, len(more)...  6.6 us
    unnamed x15, local copies, waits for them, and re-layouts  5.26 us
  transfers between devices with their start and end apart: 22, of which 13 were waited for; matrix products, arithmetic and copies ran while one was open for 5% of the time, Pallas kernels for 15%

profile of v4, /device:TPU:0, one launch (start us, length us, event | category | flops | bytes accessed | tf_op | source)
XLA Modules:
  0.0 199.0 jit_solution(17857678243781217599)
XLA Ops:
  0.0 3.0 %collective-permute-start.1 = (bf16[640,2048]{1,0:T(8,128)(2,1)}, bf16[640,2048]{1,0:T(8,128)(2,1)}, u32[]{:S(2)}, u32[]{:S(2)}) collective-permute-start(bf16[640,2048]{1,0:T(8,128)(2,1)} %refs_0_.1), channel_id=1, source_target_pairs={{0,1},{1,2},{2,3},{3,0},{4,5},{5,6},{6,7},{7,4},{8,9},{9,10},{10,1... | collective-permute-start | bytes 7864328 | tf_op jit(solution)/shard_map/ppermute | solution.py:324
  3.0 3.1 %constant_dynamic-slice_fusion = bf16[1024,1024]{1,0:T(8,128)(2,1)} fusion(bf16[2048,1024]{1,0:T(8,128)(2,1)} %refs_3_.1, s32[]{:T(128)S(6)} %select_n.11), kind=kLoop, calls=%fused_computation.28 | loop fusion | bytes 4194308 | tf_op jit(solution)/shard_map/dynamic_slice | solution.py:337
  6.2 1.5 collective-permute-start
  7.7 0.2 reduce-window.4
  7.8 0.1 fusion.5
  7.9 0.1 fusion.6
  8.0 0.0 copy-start.3
  8.0 0.1 slice.43
  8.1 2.0 %copy.6 = bf16[256,8,2,256]{3,1,2,0:T(8,128)(2,1)S(1)} copy(bf16[256,8,2,256]{3,2,1,0:T(2,128)(2,1)} %bitcast.19) | data formatting | bytes 4194304
  10.2 0.1 stack.23.ctrl
  10.3 0.0 copy-start.4
  10.3 1.2 multiply_sine_fusion
  11.5 0.0 slice-start
  11.5 0.0 copy-start.2
  11.5 0.1 pad_maximum_fusion
  11.6 0.1 fusion.3
  11.8 0.2 fusion
  11.9 0.8 select_reduce_fusion
  12.7 40.9 %collective-permute-done.refs_5_ = bf16[1024,1024]{1,0:T(8,128)(2,1)} collective-permute-done((bf16[1024,1024]{1,0:T(8,128)(2,1)}, bf16[1024,1024]{1,0:T(8,128)(2,1)}, u32[]{:S(2)}, u32[]{:S(2)}) %collective-permute-start) | collective-permute-done | bytes 2097184 | tf_op jit(solution)/shard_map/ppermute | solution.py:318
  53.6 0.1 broadcast_in_dim.63.source_ref
  53.7 0.1 broadcast_in_dim.58.first_ref
  53.8 0.1 broadcast_in_dim.59.first_ref
  53.9 0.1 broadcast_in_dim.60.first_ref
  54.0 8.2 %collective-permute-done.1.refs_1_ = bf16[640,2048]{1,0:T(8,128)(2,1)} collective-permute-done((bf16[640,2048]{1,0:T(8,128)(2,1)}, bf16[640,2048]{1,0:T(8,128)(2,1)}, u32[]{:S(2)}, u32[]{:S(2)}) %collective-permute-start.1) | collective-permute-done | bytes 2621472 | tf_op jit(solution)/shard_map/ppermute | solution.py:324
  62.2 0.0 collective-permute-start.2
  62.2 0.1 collective-permute-start.4
  62.3 1.6 collective-permute-start.9
  63.9 1.5 collective-permute-start.5
  65.4 45.0 %collective-permute-done.9.refs_11_ = bf16[2048,512]{1,0:T(8,128)(2,1)S(1)} collective-permute-done((bf16[2048,512]{1,0:T(8,128)(2,1)S(1)}, bf16[2048,512]{1,0:T(8,128)(2,1)S(1)}, u32[]{:S(2)}, u32[]{:S(2)}) %collective-permute-start.9) | collective-permute-done | bytes 2097184 | tf_op jit(solution)/shard_map/ppermute | solution.py:318
  110.4 0.0 collective-permute-start.6
  110.4 1.4 collective-permute-done.5.refs_6_
  111.8 10.5 %collective-permute-done.2.refs_2_ = bf16[640,2048]{1,0:T(8,128)(2,1)S(1)} collective-permute-done((bf16[640,2048]{1,0:T(8,128)(2,1)}, bf16[640,2048]{1,0:T(8,128)(2,1)S(1)}, u32[]{:S(2)}, u32[]{:S(2)}) %collective-permute-start.2) | collective-permute-done | bytes 2621472 | tf_op jit(solution)/shard_map/ppermute | solution.py:324
  122.3 0.1 slice.61
  122.4 0.0 collective-permute-done.8.refs_10_
  122.4 0.1 collective-permute-start.11
  122.5 0.1 slice.62
  122.6 1.3 copy-done.1
  123.9 0.0 collective-permute-done.4.refs_4_
  123.9 0.0 collective-permute-done.6.refs_7_
  123.9 0.0 collective-permute-done.10.refs_12_
  123.9 1.9 copy-done.5
  125.8 0.6 collective-permute-done.7.refs_8_
  126.5 16.6 %project.1 = (f32[320,1536]{1,0:T(8,128)S(1)}, f32[192,1536]{1,0:T(8,128)S(1)}, f32[128,1536]{1,0:T(8,128)S(1)}, bf16[3,2048,512]{2,1,0:T(8,128)(2,1)S(1)}) custom-call(s32[5]{0:T(128)S(1)} %stack.23.ctrl, bf16[640,2048]{1,0:T(8,128)(2,1)S(1)} %copy-done, bf16[640,2048]{1,0:T(8,128)(2,1)} %collective-permute-done.1.refs_1_, bf16[640,2048]{1,0:T(8,128)(2,1)} %copy-done.1, ...), custom_call_target="tpu_custom_call" | custom-call | flops 12079595520 | bytes 30000000 | tf_op jit(solution)/shard_map/project/pallas_call | solution.py:154
  143.1 12.8 %collective-permute-done.11.part = bf16[320,2048]{1,0:T(8,128)(2,1)S(1)} collective-permute-done((bf16[320,2048]{1,0:T(8,128)(2,1)S(1)}, bf16[320,2048]{1,0:T(8,128)(2,1)S(1)}, u32[]{:S(2)}, u32[]{:S(2)}) %collective-permute-start.11) | collective-permute-done | bytes 1310752 | tf_op jit(solution)/shard_map/ppermute | solution.py:324
  155.9 3.8 %attend.3 = (bf16[320,512]{1,0:T(8,128)(2,1)S(1)}, bf16[320,1024]{1,0:T(8,128)(2,1)S(1)}) custom-call(bf16[320,2048]{1,0:T(8,128)(2,1)S(1)} %collective-permute-done.11.part, bf16[3,2048,512]{2,1,0:T(8,128)(2,1)S(1)} %get-tuple-element.42.kept, f32[320,1536]{1,0:T(8,128)S(1)} %get-tuple-element.47.raw_in, s32[320,128]{1,0:T(8,128)S(1)} %broadcast_in_dim.58.first_ref, ...), custom_call_target="tpu_custom_call" | custom-call | flops 2432696320 | bytes 15000000 | tf_op jit(solution)/shard_map/attend/pallas_call | solution.py:231
  159.6 1.3 collective-permute-start.16
  160.9 1.1 slice.60
  162.0 0.3 collective-permute-start.3
  162.3 10.4 %collective-permute-done.12.part = bf16[192,2048]{1,0:T(8,128)(2,1)S(1)} collective-permute-done((bf16[192,2048]{1,0:T(8,128)(2,1)S(1)}, bf16[192,2048]{1,0:T(8,128)(2,1)S(1)}, u32[]{:S(2)}, u32[]{:S(2)}) %collective-permute-start.12) | collective-permute-done | bytes 786464 | tf_op jit(solution)/shard_map/ppermute | solution.py:324
  172.7 3.1 %attend.4 = (bf16[192,512]{1,0:T(8,128)(2,1)S(1)}, bf16[192,1024]{1,0:T(8,128)(2,1)S(1)}) custom-call(bf16[192,2048]{1,0:T(8,128)(2,1)S(1)} %collective-permute-done.12.part, bf16[3,2048,512]{2,1,0:T(8,128)(2,1)S(1)} %get-tuple-element.42.kept, f32[192,1536]{1,0:T(8,128)S(1)} %get-tuple-element.52.raw_in, s32[192,128]{1,0:T(8,128)S(1)} %broadcast_in_dim.59.first_ref, ...), custom_call_target="tpu_custom_call" | custom-call | flops 1610612736 | bytes 15000000 | tf_op jit(solution)/shard_map/attend/pallas_call | solution.py:231
  175.8 1.3 collective-permute-start.19
  177.1 0.0 collective-permute-start.15
  177.1 0.5 collective-permute-start.17
  177.6 0.0 collective-permute-start.18
  177.6 5.9 %collective-permute-done.3.part = bf16[128,2048]{1,0:T(8,128)(2,1)S(1)} collective-permute-done((bf16[128,2048]{1,0:T(8,128)(2,1)S(1)}, bf16[128,2048]{1,0:T(8,128)(2,1)S(1)}, u32[]{:S(2)}, u32[]{:S(2)}) %collective-permute-start.3) | collective-permute-done | bytes 524320 | tf_op jit(solution)/shard_map/ppermute | solution.py:324
  183.6 2.5 %attend.5 = (bf16[128,512]{1,0:T(8,128)(2,1)}, bf16[128,1024]{1,0:T(8,128)(2,1)S(1)}) custom-call(bf16[128,2048]{1,0:T(8,128)(2,1)S(1)} %collective-permute-done.3.part, bf16[3,2048,512]{2,1,0:T(8,128)(2,1)S(1)} %get-tuple-element.42.kept, f32[128,1536]{1,0:T(8,128)S(1)} %get-tuple-element.43.raw_in, s32[128,128]{1,0:T(8,128)S(1)} %broadcast_in_dim.60.first_ref, ...), custom_call_target="tpu_custom_call" | custom-call | flops 1140850688 | bytes 15000000 | tf_op jit(solution)/shard_map/attend/pallas_call | solution.py:231
  186.1 0.1 collective-permute-done.19.refs_6_
  186.2 1.3 collective-permute-start.14
  187.5 0.2 collective-permute-start.13
  187.7 0.2 collective-permute-done.20.refs_7_
  187.9 4.3 %place.2.refs_4_ = bf16[640,1024]{1,0:T(8,128)(2,1)S(1)} custom-call(s32[1]{0:T(128)} %bitcast.9.me_ref, s32[640,128]{1,0:T(8,128)S(1)} %broadcast_in_dim.63.source_ref, bf16[320,1024]{1,0:T(8,128)(2,1)S(1)} %get-tuple-element.59.refs_0_, bf16[320,1024]{1,0:T(8,128)(2,1)S(1)} %collective-permute-done.15.refs_1_, ...), custom_call_target="tpu_custom_call" | custom-call | flops 2684354560 | bytes 5242880 | tf_op jit(solution)/shard_map/place/pallas_call | solution.py:290
  192.2 2.7 %collective-permute-done.14.refs_2_ = bf16[128,1024]{1,0:T(8,128)(2,1)S(1)} collective-permute-done((bf16[128,1024]{1,0:T(8,128)(2,1)S(1)}, bf16[128,1024]{1,0:T(8,128)(2,1)S(1)}, u32[]{:S(2)}, u32[]{:S(2)}) %collective-permute-start.14) | collective-permute-done | bytes 262176 | tf_op jit(solution)/shard_map/ppermute | solution.py:318
  195.0 1.5 collective-permute-done.21.refs_3_
  196.5 2.3 %place.3 = bf16[640,1024]{1,0:T(8,128)(2,1)} custom-call(s32[1]{0:T(128)} %bitcast.9.me_ref, s32[640,128]{1,0:T(8,128)S(1)} %broadcast_in_dim.63.source_ref, bf16[128,1024]{1,0:T(8,128)(2,1)S(1)} %get-tuple-element.57.refs_0_, bf16[128,1024]{1,0:T(8,128)(2,1)S(1)} %collective-permute-done.13.refs_1_, bf16[128,1024]{1,0:T(8,128)(2,1)S(1)} %collective-permute-done.14.refs_2_, ...), custom_call_target="tpu_custom_call" | custom-call | flops 671088640 | bytes 5242880 | tf_op jit(solution)/shard_map/place/pallas_call | solution.py:290
  (26 shorter events, 0.1 us)
Async XLA Ops:
  0.0 62.2 %collective-permute-start.1 = (bf16[640,2048]{1,0:T(8,128)(2,1)}, bf16[640,2048]{1,0:T(8,128)(2,1)}, u32[]{:S(2)}, u32[]{:S(2)}) collective-permute-start(bf16[640,2048]{1,0:T(8,128)(2,1)} %refs_0_.1), channel_id=1, source_target_pairs={{0,1},{1,2},{2,3},{3,0},{4,5},{5,6},{6,7},{7,4},{8,9},{9,10},{10,1... | collective-permute-start | bytes 7864328 | tf_op jit(solution)/shard_map/ppermute | solution.py:324
  3.0 4.6 %copy-start.6 = (s32[1,2]{1,0:T(1,128)S(1)}, s32[1,2]{1,0:T(1,128)}, u32[]{:S(2)}) copy-start(s32[1,2]{1,0:T(1,128)} %param.8) | copy-start | bytes 28
  6.2 47.4 %collective-permute-start = (bf16[1024,1024]{1,0:T(8,128)(2,1)}, bf16[1024,1024]{1,0:T(8,128)(2,1)}, u32[]{:S(2)}, u32[]{:S(2)}) collective-permute-start(bf16[1024,1024]{1,0:T(8,128)(2,1)} %constant_dynamic-slice_fusion), channel_id=1, source_target_pairs={{0,8},{4,12},{8,0},{12,4},{1,9},{5,13},{9,1},{13,5},{2,10},{6,14},... | collective-permute-start | bytes 6291464 | tf_op jit(solution)/shard_map/ppermute | solution.py:318
  8.0 2.2 %copy-start.3 = (s32[640]{0:T(1024)}, s32[640]{0:T(1024)S(1)}, u32[]{:S(2)}) copy-start(s32[640]{0:T(1024)S(1)} %fusion.6) | copy-start | bytes 7684
  10.3 1.7 copy-start.4
  11.5 42.2 %slice-start = ((s32[640]{0:T(1024)}), s32[320]{0:T(512)S(1)}, s32[]{:S(2)}) async-start(s32[640]{0:T(1024)} %copy-done.3), calls=%async_computation | async-start | bytes 4096 | tf_op jit(solution)/shard_map/slice | solution.py:331
  11.5 50.7 %copy-start.2 = (bf16[2048,1024]{1,0:T(8,128)(2,1)S(1)}, bf16[2048,1024]{1,0:T(8,128)(2,1)}, u32[]{:S(2)}) copy-start(bf16[2048,1024]{1,0:T(8,128)(2,1)} %refs_3_.1) | copy-start | bytes 12582916
  62.2 64.2 %copy-start = (bf16[640,2048]{1,0:T(8,128)(2,1)S(1)}, bf16[640,2048]{1,0:T(8,128)(2,1)}, u32[]{:S(2)}) copy-start(bf16[640,2048]{1,0:T(8,128)(2,1)} %refs_0_.1) | copy-start | bytes 7864324
  62.2 60.1 %collective-permute-start.2 = (bf16[640,2048]{1,0:T(8,128)(2,1)}, bf16[640,2048]{1,0:T(8,128)(2,1)S(1)}, u32[]{:S(2)}, u32[]{:S(2)}) collective-permute-start(bf16[640,2048]{1,0:T(8,128)(2,1)} %collective-permute-done.1.refs_1_), channel_id=1, source_target_pairs={{0,1},{1,2},{2,3},{3,0},{4,5},{5,6},{6,7},{7,4},{8,9},{9,10},{10,1... | collective-permute-start | bytes 7864328 | tf_op jit(solution)/shard_map/ppermute | solution.py:324
  62.2 61.6 %collective-permute-start.4 = (bf16[2048,1024]{1,0:T(8,128)(2,1)S(1)}, bf16[2048,1024]{1,0:T(8,128)(2,1)S(1)}, u32[]{:S(2)}, u32[]{:S(2)}) collective-permute-start(bf16[2048,1024]{1,0:T(8,128)(2,1)S(1)} %copy-done.2), channel_id=1, source_target_pairs={{0,4},{4,0},{8,12},{12,8},{1,5},{5,1},{9,13},{13,9},{2,6},{6,2},{1... | collective-permute-start | bytes 12582920 | tf_op jit(solution)/shard_map/ppermute | solution.py:318
  62.3 48.0 %collective-permute-start.9 = (bf16[2048,512]{1,0:T(8,128)(2,1)S(1)}, bf16[2048,512]{1,0:T(8,128)(2,1)S(1)}, u32[]{:S(2)}, u32[]{:S(2)}) collective-permute-start(bf16[2048,512]{1,0:T(8,128)(2,1)S(1)} %bitcast.16), channel_id=1, source_target_pairs={{0,8},{4,12},{8,0},{12,4},{1,9},{5,13},{9,1},{13,5},{2,10},{6,14},... | collective-permute-start | bytes 6291464 | tf_op jit(solution)/shard_map/ppermute | solution.py:318
  63.9 47.9 %collective-permute-start.5 = (bf16[1024,1024]{1,0:T(8,128)(2,1)}, bf16[1024,1024]{1,0:T(8,128)(2,1)S(1)}, u32[]{:S(2)}, u32[]{:S(2)}) collective-permute-start(bf16[1024,1024]{1,0:T(8,128)(2,1)} %collective-permute-done.refs_5_), channel_id=1, source_target_pairs={{0,16},{16,0},{1,17},{17,1},{2,18},{18,2},{3,19},{19,3},{4,20},{20... | collective-permute-start | bytes 6291464 | tf_op jit(solution)/shard_map/ppermute | solution.py:342
  65.4 57.0 %collective-permute-start.8 = (bf16[2048,512]{1,0:T(8,128)(2,1)S(1)}, bf16[2048,512]{1,0:T(8,128)(2,1)S(1)}, u32[]{:S(2)}, u32[]{:S(2)}) collective-permute-start(bf16[2048,512]{1,0:T(8,128)(2,1)S(1)} %bitcast.17), channel_id=1, source_target_pairs={{0,4},{4,0},{8,12},{12,8},{1,5},{5,1},{9,13},{13,9},{2,6},{6,2},{1... | collective-permute-start | bytes 6291464 | tf_op jit(solution)/shard_map/ppermute | solution.py:318
  110.4 13.5 %collective-permute-start.6 = (bf16[1024,1024]{1,0:T(8,128)(2,1)}, bf16[1024,1024]{1,0:T(8,128)(2,1)S(1)}, u32[]{:S(2)}, u32[]{:S(2)}) collective-permute-start(bf16[1024,1024]{1,0:T(8,128)(2,1)} %collective-permute-done.refs_5_), channel_id=1, source_target_pairs={{0,4},{4,0},{8,12},{12,8},{1,5},{5,1},{9,13},{13,9},{2,6},{6,2},{1... | collective-permute-start | bytes 6291464 | tf_op jit(solution)/shard_map/ppermute | solution.py:318
  111.8 12.1 %collective-permute-start.10 = (bf16[2048,512]{1,0:T(8,128)(2,1)S(1)}, bf16[2048,512]{1,0:T(8,128)(2,1)S(1)}, u32[]{:S(2)}, u32[]{:S(2)}) collective-permute-start(bf16[2048,512]{1,0:T(8,128)(2,1)S(1)} %collective-permute-done.9.refs_11_), channel_id=1, source_target_pairs={{0,4},{4,0},{8,12},{12,8},{1,5},{5,1},{9,13},{13,9},{2,6},{6,2},{1... | collective-permute-start | bytes 6291464 | tf_op jit(solution)/shard_map/ppermute | solution.py:318
  122.3 1.6 copy-start.1
  122.3 4.2 %collective-permute-start.7 = (bf16[1024,1024]{1,0:T(8,128)(2,1)S(1)}, bf16[1024,1024]{1,0:T(8,128)(2,1)S(1)}, u32[]{:S(2)}, u32[]{:S(2)}) collective-permute-start(bf16[1024,1024]{1,0:T(8,128)(2,1)S(1)} %collective-permute-done.5.refs_6_), channel_id=1, source_target_pairs={{0,4},{4,0},{8,12},{12,8},{1,5},{5,1},{9,13},{13,9},{2,6},{6,2},{1... | collective-permute-start | bytes 6291464 | tf_op jit(solution)/shard_map/ppermute | solution.py:318
  122.4 33.4 %collective-permute-start.11 = (bf16[320,2048]{1,0:T(8,128)(2,1)S(1)}, bf16[320,2048]{1,0:T(8,128)(2,1)S(1)}, u32[]{:S(2)}, u32[]{:S(2)}) collective-permute-start(bf16[320,2048]{1,0:T(8,128)(2,1)S(1)} %slice.61), channel_id=1, source_target_pairs={{0,1},{1,2},{2,3},{3,0},{4,5},{5,6},{6,7},{7,4},{8,9},{9,10},{10,1... | collective-permute-start | bytes 3932168 | tf_op jit(solution)/shard_map/ppermute | solution.py:324
  123.9 2.0 copy-start.5
  123.9 48.9 %collective-permute-start.12 = (bf16[192,2048]{1,0:T(8,128)(2,1)S(1)}, bf16[192,2048]{1,0:T(8,128)(2,1)S(1)}, u32[]{:S(2)}, u32[]{:S(2)}) collective-permute-start(bf16[192,2048]{1,0:T(8,128)(2,1)S(1)} %slice.62), channel_id=1, source_target_pairs={{0,1},{1,2},{2,3},{3,0},{4,5},{5,6},{6,7},{7,4},{8,9},{9,10},{10,1... | collective-permute-start | bytes 2359304 | tf_op jit(solution)/shard_map/ppermute | solution.py:324
  159.6 17.5 %collective-permute-start.16 = (bf16[320,1024]{1,0:T(8,128)(2,1)S(1)}, bf16[320,1024]{1,0:T(8,128)(2,1)S(1)}, u32[]{:S(2)}, u32[]{:S(2)}) collective-permute-start(bf16[320,1024]{1,0:T(8,128)(2,1)S(1)} %get-tuple-element.59.refs_0_), channel_id=1, source_target_pairs={{0,8},{4,12},{8,0},{12,4},{1,9},{5,13},{9,1},{13,5},{2,10},{6,14},... | collective-permute-start | bytes 1966088 | tf_op jit(solution)/shard_map/ppermute | solution.py:318
  162.0 21.5 %collective-permute-start.3 = (bf16[128,2048]{1,0:T(8,128)(2,1)S(1)}, bf16[128,2048]{1,0:T(8,128)(2,1)S(1)}, u32[]{:S(2)}, u32[]{:S(2)}) collective-permute-start(bf16[128,2048]{1,0:T(8,128)(2,1)S(1)} %slice.60), channel_id=1, source_target_pairs={{0,1},{1,2},{2,3},{3,0},{4,5},{5,6},{6,7},{7,4},{8,9},{9,10},{10,1... | collective-permute-start | bytes 1572872 | tf_op jit(solution)/shard_map/ppermute | solution.py:324
  175.8 10.4 %collective-permute-start.19 = (bf16[192,1024]{1,0:T(8,128)(2,1)S(1)}, bf16[192,1024]{1,0:T(8,128)(2,1)S(1)}, u32[]{:S(2)}, u32[]{:S(2)}) collective-permute-start(bf16[192,1024]{1,0:T(8,128)(2,1)S(1)} %get-tuple-element.60.refs_4_), channel_id=1, source_target_pairs={{0,8},{4,12},{8,0},{12,4},{1,9},{5,13},{9,1},{13,5},{2,10},{6,14},... | collective-permute-start | bytes 1179656 | tf_op jit(solution)/shard_map/ppermute | solution.py:318
  177.1 10.6 %collective-permute-start.15 = (bf16[320,1024]{1,0:T(8,128)(2,1)S(1)}, bf16[320,1024]{1,0:T(8,128)(2,1)S(1)}, u32[]{:S(2)}, u32[]{:S(2)}) collective-permute-start(bf16[320,1024]{1,0:T(8,128)(2,1)S(1)} %get-tuple-element.59.refs_0_), channel_id=1, source_target_pairs={{0,4},{4,0},{8,12},{12,8},{1,5},{5,1},{9,13},{13,9},{2,6},{6,2},{1... | collective-permute-start | bytes 1966088 | tf_op jit(solution)/shard_map/ppermute | solution.py:318
  177.1 10.8 %collective-permute-start.17 = (bf16[320,1024]{1,0:T(8,128)(2,1)S(1)}, bf16[320,1024]{1,0:T(8,128)(2,1)S(1)}, u32[]{:S(2)}, u32[]{:S(2)}) collective-permute-start(bf16[320,1024]{1,0:T(8,128)(2,1)S(1)} %collective-permute-done.16.refs_2_), channel_id=1, source_target_pairs={{0,4},{4,0},{8,12},{12,8},{1,5},{5,1},{9,13},{13,9},{2,6},{6,2},{1... | collective-permute-start | bytes 1966088 | tf_op jit(solution)/shard_map/ppermute | solution.py:318
  177.6 9.9 %collective-permute-start.18 = (bf16[192,1024]{1,0:T(8,128)(2,1)S(1)}, bf16[192,1024]{1,0:T(8,128)(2,1)S(1)}, u32[]{:S(2)}, u32[]{:S(2)}) collective-permute-start(bf16[192,1024]{1,0:T(8,128)(2,1)S(1)} %get-tuple-element.60.refs_4_), channel_id=1, source_target_pairs={{0,4},{4,0},{8,12},{12,8},{1,5},{5,1},{9,13},{13,9},{2,6},{6,2},{1... | collective-permute-start | bytes 1179656 | tf_op jit(solution)/shard_map/ppermute | solution.py:318
  186.2 1.7 collective-permute-start.20
  186.2 8.7 %collective-permute-start.14 = (bf16[128,1024]{1,0:T(8,128)(2,1)S(1)}, bf16[128,1024]{1,0:T(8,128)(2,1)S(1)}, u32[]{:S(2)}, u32[]{:S(2)}) collective-permute-start(bf16[128,1024]{1,0:T(8,128)(2,1)S(1)} %get-tuple-element.57.refs_0_), channel_id=1, source_target_pairs={{0,8},{4,12},{8,0},{12,4},{1,9},{5,13},{9,1},{13,5},{2,10},{6,14},... | collective-permute-start | bytes 786440 | tf_op jit(solution)/shard_map/ppermute | solution.py:318
  187.5 7.4 %collective-permute-start.13 = (bf16[128,1024]{1,0:T(8,128)(2,1)S(1)}, bf16[128,1024]{1,0:T(8,128)(2,1)S(1)}, u32[]{:S(2)}, u32[]{:S(2)}) collective-permute-start(bf16[128,1024]{1,0:T(8,128)(2,1)S(1)} %get-tuple-element.57.refs_0_), channel_id=1, source_target_pairs={{0,4},{4,0},{8,12},{12,8},{1,5},{5,1},{9,13},{13,9},{2,6},{6,2},{1... | collective-permute-start | bytes 786440 | tf_op jit(solution)/shard_map/ppermute | solution.py:318
  194.9 1.5 collective-permute-start.21

commit v5 on v4

--- a/solution.py
+++ b/solution.py
@@ -364,7 +364,7 @@
         kv_new, mixed_new = attend(part, weights, kept, raw, table, kv, head_dim)
         kv, mixed = kv + [kv_new], mixed + [mixed_new]
     last = len(mixed) - 1
-    early, late = [], []
+    early = []
     for n, (block, top, rows) in enumerate(zip(mixed, tops, chunks)):
         if not small:
             arrived = [swap(block, j) if j else block for j in range(replicas)]
@@ -374,13 +374,14 @@
             if n < last:
                 arrived[2] = after(across, mixed[n + 1])
                 arrived.append(swap(arrived[2], 1))
-        (late if n == last else early).extend((a, [(0, rows, j, top)]) for j, a in enumerate(arrived))
+        arrived = [(a, [(0, rows, j, top)]) for j, a in enumerate(arrived)]
+        early += arrived if n < last else arrived[:1]
+        late = arrived[1:]
     source_late = after(source, mixed[last])
     placed = place(me_array, source_late, early, tok_rows)
     if small:
-        final, placed = lax.optimization_barrier((late[2][0], placed))
-        late[2] = (final, late[2][1])
-        late.append((swap(final, 1), [(0, chunks[last], 3, tops[last])]))
+        final, placed = lax.optimization_barrier((late[1][0], placed))
+        late = [late[0], (final, late[1][1]), (swap(final, 1), [(0, chunks[last], 3, tops[last])])]
     return place(me_array, source_late, late, tok_rows, placed)
 
 

time: 199 us -> 199 us (level)
  no operation moved by 1% of the time
where the time goes in v5:
time: 199 us
  waiting for transfers between devices  140 us (70%)
  Pallas kernels  32.6 us (16%)
  starting transfers between devices  12.6 us (6%)
  local copies, waits for them, and re-layouts  10.2 us (5%)
  other arithmetic  2.71 us (1%)
    ppermute x16, waiting for transfers between devices, swap(): return lax.ppermute(block, 'replica', [(i, i ^ j) for i in range(replicas)])  90.7 us
    ppermute x5, waiting for transfers between devices, on(): lax.ppermute(block, 'trow', [(i, (i + 1) % columns) for i in range(column...  47.9 us
    pallas_call x1, Pallas kernels, project(): pl.pallas_call(functools.partial(project_kernel, w, pieces, chunks), out_...  16.6 us
    pallas_call x3, Pallas kernels, attend(): pl.pallas_call(functools.partial(attend_kernel, heads, kv_heads, head_dim...  9.38 us
    ppermute x16, starting transfers between devices, swap(): return lax.ppermute(block, 'replica', [(i, i ^ j) for i in range(replicas)])  7.74 us
    pallas_call x2, Pallas kernels, place(): pl.pallas_call(functools.partial(place_kernel, spans, tok_rows, len(more)...  6.6 us
    unnamed x15, local copies, waits for them, and re-layouts  5.26 us
  transfers between devices with their start and end apart: 22, of which 13 were waited for; matrix products, arithmetic and copies ran while one was open for 5% of the time, Pallas kernels for 15%

profile of v5, /device:TPU:0, one launch (start us, length us, event | category | flops | bytes accessed | tf_op | source)
XLA Modules:
  0.0 198.7 jit_solution(284739827433458308)
XLA Ops:
  0.0 3.0 %collective-permute-start.1 = (bf16[640,2048]{1,0:T(8,128)(2,1)}, bf16[640,2048]{1,0:T(8,128)(2,1)}, u32[]{:S(2)}, u32[]{:S(2)}) collective-permute-start(bf16[640,2048]{1,0:T(8,128)(2,1)} %refs_0_.1), channel_id=1, source_target_pairs={{0,1},{1,2},{2,3},{3,0},{4,5},{5,6},{6,7},{7,4},{8,9},{9,10},{10,1... | collective-permute-start | bytes 7864328 | tf_op jit(solution)/shard_map/ppermute | solution.py:324
  3.0 3.1 %constant_dynamic-slice_fusion = bf16[1024,1024]{1,0:T(8,128)(2,1)} fusion(bf16[2048,1024]{1,0:T(8,128)(2,1)} %refs_3_.1, s32[]{:T(128)S(6)} %select_n.11), kind=kLoop, calls=%fused_computation.28 | loop fusion | bytes 4194308 | tf_op jit(solution)/shard_map/dynamic_slice | solution.py:337
  6.2 1.5 collective-permute-start
  7.7 0.2 reduce-window.4
  7.8 0.1 fusion.5
  7.9 0.1 fusion.6
  8.0 0.0 copy-start.3
  8.0 0.1 slice.43
  8.1 2.0 %copy.6 = bf16[256,8,2,256]{3,1,2,0:T(8,128)(2,1)S(1)} copy(bf16[256,8,2,256]{3,2,1,0:T(2,128)(2,1)} %bitcast.19) | data formatting | bytes 4194304
  10.2 0.1 stack.23.ctrl
  10.3 0.0 copy-start.4
  10.3 1.2 multiply_sine_fusion
  11.5 0.0 slice-start
  11.5 0.0 copy-start.2
  11.5 0.1 pad_maximum_fusion
  11.6 0.1 fusion.3
  11.8 0.2 fusion
  11.9 0.8 select_reduce_fusion
  12.7 40.9 %collective-permute-done.refs_5_ = bf16[1024,1024]{1,0:T(8,128)(2,1)} collective-permute-done((bf16[1024,1024]{1,0:T(8,128)(2,1)}, bf16[1024,1024]{1,0:T(8,128)(2,1)}, u32[]{:S(2)}, u32[]{:S(2)}) %collective-permute-start) | collective-permute-done | bytes 2097184 | tf_op jit(solution)/shard_map/ppermute | solution.py:318
  53.6 0.1 broadcast_in_dim.63.source_ref
  53.7 0.1 broadcast_in_dim.58.first_ref
  53.8 0.1 broadcast_in_dim.59.first_ref
  53.9 0.1 broadcast_in_dim.60.first_ref
  54.0 8.2 %collective-permute-done.1.refs_1_ = bf16[640,2048]{1,0:T(8,128)(2,1)} collective-permute-done((bf16[640,2048]{1,0:T(8,128)(2,1)}, bf16[640,2048]{1,0:T(8,128)(2,1)}, u32[]{:S(2)}, u32[]{:S(2)}) %collective-permute-start.1) | collective-permute-done | bytes 2621472 | tf_op jit(solution)/shard_map/ppermute | solution.py:324
  62.2 0.0 collective-permute-start.2
  62.2 0.1 collective-permute-start.4
  62.3 1.6 collective-permute-start.9
  63.9 1.5 collective-permute-start.5
  65.4 0.0 collective-permute-start.8
  65.4 45.0 %collective-permute-done.9.refs_11_ = bf16[2048,512]{1,0:T(8,128)(2,1)S(1)} collective-permute-done((bf16[2048,512]{1,0:T(8,128)(2,1)S(1)}, bf16[2048,512]{1,0:T(8,128)(2,1)S(1)}, u32[]{:S(2)}, u32[]{:S(2)}) %collective-permute-start.9) | collective-permute-done | bytes 2097184 | tf_op jit(solution)/shard_map/ppermute | solution.py:318
  110.4 1.4 collective-permute-done.5.refs_6_
  111.8 0.0 collective-permute-start.10
  111.8 10.5 %collective-permute-done.2.refs_2_ = bf16[640,2048]{1,0:T(8,128)(2,1)S(1)} collective-permute-done((bf16[640,2048]{1,0:T(8,128)(2,1)}, bf16[640,2048]{1,0:T(8,128)(2,1)S(1)}, u32[]{:S(2)}, u32[]{:S(2)}) %collective-permute-start.2) | collective-permute-done | bytes 2621472 | tf_op jit(solution)/shard_map/ppermute | solution.py:324
  122.3 0.0 collective-permute-start.7
  122.3 0.1 slice.61
  122.4 0.1 collective-permute-start.11
  122.5 0.1 slice.62
  122.6 1.3 copy-done.1
  123.9 0.0 collective-permute-start.12
  123.9 0.0 collective-permute-done.6.refs_7_
  123.9 1.9 copy-done.5
  125.8 0.6 collective-permute-done.7.refs_8_
  126.5 16.6 %project.1 = (f32[320,1536]{1,0:T(8,128)S(1)}, f32[192,1536]{1,0:T(8,128)S(1)}, f32[128,1536]{1,0:T(8,128)S(1)}, bf16[3,2048,512]{2,1,0:T(8,128)(2,1)S(1)}) custom-call(s32[5]{0:T(128)S(1)} %stack.23.ctrl, bf16[640,2048]{1,0:T(8,128)(2,1)S(1)} %copy-done, bf16[640,2048]{1,0:T(8,128)(2,1)} %collective-permute-done.1.refs_1_, bf16[640,2048]{1,0:T(8,128)(2,1)} %copy-done.1, ...), custom_call_target="tpu_custom_call" | custom-call | flops 12079595520 | bytes 30000000 | tf_op jit(solution)/shard_map/project/pallas_call | solution.py:154
  143.1 12.8 %collective-permute-done.11.part = bf16[320,2048]{1,0:T(8,128)(2,1)S(1)} collective-permute-done((bf16[320,2048]{1,0:T(8,128)(2,1)S(1)}, bf16[320,2048]{1,0:T(8,128)(2,1)S(1)}, u32[]{:S(2)}, u32[]{:S(2)}) %collective-permute-start.11) | collective-permute-done | bytes 1310752 | tf_op jit(solution)/shard_map/ppermute | solution.py:324
  155.9 3.8 %attend.3 = (bf16[320,512]{1,0:T(8,128)(2,1)S(1)}, bf16[320,1024]{1,0:T(8,128)(2,1)S(1)}) custom-call(bf16[320,2048]{1,0:T(8,128)(2,1)S(1)} %collective-permute-done.11.part, bf16[3,2048,512]{2,1,0:T(8,128)(2,1)S(1)} %get-tuple-element.42.kept, f32[320,1536]{1,0:T(8,128)S(1)} %get-tuple-element.47.raw_in, s32[320,128]{1,0:T(8,128)S(1)} %broadcast_in_dim.58.first_ref, ...), custom_call_target="tpu_custom_call" | custom-call | flops 2432696320 | bytes 15000000 | tf_op jit(solution)/shard_map/attend/pallas_call | solution.py:231
  159.6 1.3 collective-permute-start.16
  160.9 1.1 slice.60
  162.0 0.3 collective-permute-start.3
  162.3 10.4 %collective-permute-done.12.part = bf16[192,2048]{1,0:T(8,128)(2,1)S(1)} collective-permute-done((bf16[192,2048]{1,0:T(8,128)(2,1)S(1)}, bf16[192,2048]{1,0:T(8,128)(2,1)S(1)}, u32[]{:S(2)}, u32[]{:S(2)}) %collective-permute-start.12) | collective-permute-done | bytes 786464 | tf_op jit(solution)/shard_map/ppermute | solution.py:324
  172.7 3.1 %attend.4 = (bf16[192,512]{1,0:T(8,128)(2,1)S(1)}, bf16[192,1024]{1,0:T(8,128)(2,1)S(1)}) custom-call(bf16[192,2048]{1,0:T(8,128)(2,1)S(1)} %collective-permute-done.12.part, bf16[3,2048,512]{2,1,0:T(8,128)(2,1)S(1)} %get-tuple-element.42.kept, f32[192,1536]{1,0:T(8,128)S(1)} %get-tuple-element.52.raw_in, s32[192,128]{1,0:T(8,128)S(1)} %broadcast_in_dim.59.first_ref, ...), custom_call_target="tpu_custom_call" | custom-call | flops 1610612736 | bytes 15000000 | tf_op jit(solution)/shard_map/attend/pallas_call | solution.py:231
  175.8 1.3 collective-permute-start.19
  177.1 0.5 collective-permute-start.17
  177.6 0.0 collective-permute-start.18
  177.6 5.9 %collective-permute-done.3.part = bf16[128,2048]{1,0:T(8,128)(2,1)S(1)} collective-permute-done((bf16[128,2048]{1,0:T(8,128)(2,1)S(1)}, bf16[128,2048]{1,0:T(8,128)(2,1)S(1)}, u32[]{:S(2)}, u32[]{:S(2)}) %collective-permute-start.3) | collective-permute-done | bytes 524320 | tf_op jit(solution)/shard_map/ppermute | solution.py:324
  183.6 2.5 %attend.5 = (bf16[128,512]{1,0:T(8,128)(2,1)}, bf16[128,1024]{1,0:T(8,128)(2,1)S(1)}) custom-call(bf16[128,2048]{1,0:T(8,128)(2,1)S(1)} %collective-permute-done.3.part, bf16[3,2048,512]{2,1,0:T(8,128)(2,1)S(1)} %get-tuple-element.42.kept, f32[128,1536]{1,0:T(8,128)S(1)} %get-tuple-element.43.raw_in, s32[128,128]{1,0:T(8,128)S(1)} %broadcast_in_dim.60.first_ref, ...), custom_call_target="tpu_custom_call" | custom-call | flops 1140850688 | bytes 15000000 | tf_op jit(solution)/shard_map/attend/pallas_call | solution.py:231
  186.1 0.1 collective-permute-done.19.refs_6_
  186.2 0.0 collective-permute-start.20
  186.2 1.3 collective-permute-start.14
  187.5 0.2 collective-permute-start.13
  187.7 0.2 collective-permute-done.20.refs_7_
  187.9 4.6 %place.2.refs_3_ = bf16[640,1024]{1,0:T(8,128)(2,1)S(1)} custom-call(s32[1]{0:T(128)} %bitcast.9.me_ref, s32[640,128]{1,0:T(8,128)S(1)} %broadcast_in_dim.63.source_ref, bf16[320,1024]{1,0:T(8,128)(2,1)S(1)} %get-tuple-element.59.refs_0_, bf16[320,1024]{1,0:T(8,128)(2,1)S(1)} %collective-permute-done.15.refs_1_, ...), custom_call_target="tpu_custom_call" | custom-call | flops 2852126720 | bytes 5242880 | tf_op jit(solution)/shard_map/place/pallas_call | solution.py:290
  192.6 2.4 %collective-permute-done.14.refs_1_ = bf16[128,1024]{1,0:T(8,128)(2,1)S(1)} collective-permute-done((bf16[128,1024]{1,0:T(8,128)(2,1)S(1)}, bf16[128,1024]{1,0:T(8,128)(2,1)S(1)}, u32[]{:S(2)}, u32[]{:S(2)}) %collective-permute-start.14) | collective-permute-done | bytes 262176 | tf_op jit(solution)/shard_map/ppermute | solution.py:318
  195.0 1.5 collective-permute-done.21.refs_2_
  196.5 2.0 %place.3 = bf16[640,1024]{1,0:T(8,128)(2,1)} custom-call(s32[1]{0:T(128)} %bitcast.9.me_ref, s32[640,128]{1,0:T(8,128)S(1)} %broadcast_in_dim.63.source_ref, bf16[128,1024]{1,0:T(8,128)(2,1)S(1)} %collective-permute-done.13.refs_0_, bf16[128,1024]{1,0:T(8,128)(2,1)S(1)} %collective-permute-done.14.refs_1_, ...), custom_call_target="tpu_custom_call" | custom-call | flops 503316480 | bytes 5242880 | tf_op jit(solution)/shard_map/place/pallas_call | solution.py:290
  (26 shorter events, 0.1 us)
Async XLA Ops:
  0.0 62.2 %collective-permute-start.1 = (bf16[640,2048]{1,0:T(8,128)(2,1)}, bf16[640,2048]{1,0:T(8,128)(2,1)}, u32[]{:S(2)}, u32[]{:S(2)}) collective-permute-start(bf16[640,2048]{1,0:T(8,128)(2,1)} %refs_0_.1), channel_id=1, source_target_pairs={{0,1},{1,2},{2,3},{3,0},{4,5},{5,6},{6,7},{7,4},{8,9},{9,10},{10,1... | collective-permute-start | bytes 7864328 | tf_op jit(solution)/shard_map/ppermute | solution.py:324
  3.0 4.6 %copy-start.6 = (s32[1,2]{1,0:T(1,128)S(1)}, s32[1,2]{1,0:T(1,128)}, u32[]{:S(2)}) copy-start(s32[1,2]{1,0:T(1,128)} %param.8) | copy-start | bytes 28
  6.2 47.4 %collective-permute-start = (bf16[1024,1024]{1,0:T(8,128)(2,1)}, bf16[1024,1024]{1,0:T(8,128)(2,1)}, u32[]{:S(2)}, u32[]{:S(2)}) collective-permute-start(bf16[1024,1024]{1,0:T(8,128)(2,1)} %constant_dynamic-slice_fusion), channel_id=1, source_target_pairs={{0,8},{4,12},{8,0},{12,4},{1,9},{5,13},{9,1},{13,5},{2,10},{6,14},... | collective-permute-start | bytes 6291464 | tf_op jit(solution)/shard_map/ppermute | solution.py:318
  8.0 2.2 %copy-start.3 = (s32[640]{0:T(1024)}, s32[640]{0:T(1024)S(1)}, u32[]{:S(2)}) copy-start(s32[640]{0:T(1024)S(1)} %fusion.6) | copy-start | bytes 7684
  10.3 1.7 copy-start.4
  11.5 42.2 %slice-start = ((s32[640]{0:T(1024)}), s32[320]{0:T(512)S(1)}, s32[]{:S(2)}) async-start(s32[640]{0:T(1024)} %copy-done.3), calls=%async_computation | async-start | bytes 4096 | tf_op jit(solution)/shard_map/slice | solution.py:331
  11.5 50.7 %copy-start.2 = (bf16[2048,1024]{1,0:T(8,128)(2,1)S(1)}, bf16[2048,1024]{1,0:T(8,128)(2,1)}, u32[]{:S(2)}) copy-start(bf16[2048,1024]{1,0:T(8,128)(2,1)} %refs_3_.1) | copy-start | bytes 12582916
  62.2 64.2 %copy-start = (bf16[640,2048]{1,0:T(8,128)(2,1)S(1)}, bf16[640,2048]{1,0:T(8,128)(2,1)}, u32[]{:S(2)}) copy-start(bf16[640,2048]{1,0:T(8,128)(2,1)} %refs_0_.1) | copy-start | bytes 7864324
  62.2 60.1 %collective-permute-start.2 = (bf16[640,2048]{1,0:T(8,128)(2,1)}, bf16[640,2048]{1,0:T(8,128)(2,1)S(1)}, u32[]{:S(2)}, u32[]{:S(2)}) collective-permute-start(bf16[640,2048]{1,0:T(8,128)(2,1)} %collective-permute-done.1.refs_1_), channel_id=1, source_target_pairs={{0,1},{1,2},{2,3},{3,0},{4,5},{5,6},{6,7},{7,4},{8,9},{9,10},{10,1... | collective-permute-start | bytes 7864328 | tf_op jit(solution)/shard_map/ppermute | solution.py:324
  62.2 61.6 %collective-permute-start.4 = (bf16[2048,1024]{1,0:T(8,128)(2,1)S(1)}, bf16[2048,1024]{1,0:T(8,128)(2,1)S(1)}, u32[]{:S(2)}, u32[]{:S(2)}) collective-permute-start(bf16[2048,1024]{1,0:T(8,128)(2,1)S(1)} %copy-done.2), channel_id=1, source_target_pairs={{0,4},{4,0},{8,12},{12,8},{1,5},{5,1},{9,13},{13,9},{2,6},{6,2},{1... | collective-permute-start | bytes 12582920 | tf_op jit(solution)/shard_map/ppermute | solution.py:318
  62.3 48.0 %collective-permute-start.9 = (bf16[2048,512]{1,0:T(8,128)(2,1)S(1)}, bf16[2048,512]{1,0:T(8,128)(2,1)S(1)}, u32[]{:S(2)}, u32[]{:S(2)}) collective-permute-start(bf16[2048,512]{1,0:T(8,128)(2,1)S(1)} %bitcast.16), channel_id=1, source_target_pairs={{0,8},{4,12},{8,0},{12,4},{1,9},{5,13},{9,1},{13,5},{2,10},{6,14},... | collective-permute-start | bytes 6291464 | tf_op jit(solution)/shard_map/ppermute | solution.py:318
  63.9 47.9 %collective-permute-start.5 = (bf16[1024,1024]{1,0:T(8,128)(2,1)}, bf16[1024,1024]{1,0:T(8,128)(2,1)S(1)}, u32[]{:S(2)}, u32[]{:S(2)}) collective-permute-start(bf16[1024,1024]{1,0:T(8,128)(2,1)} %collective-permute-done.refs_5_), channel_id=1, source_target_pairs={{0,16},{16,0},{1,17},{17,1},{2,18},{18,2},{3,19},{19,3},{4,20},{20... | collective-permute-start | bytes 6291464 | tf_op jit(solution)/shard_map/ppermute | solution.py:342
  65.4 57.0 %collective-permute-start.8 = (bf16[2048,512]{1,0:T(8,128)(2,1)S(1)}, bf16[2048,512]{1,0:T(8,128)(2,1)S(1)}, u32[]{:S(2)}, u32[]{:S(2)}) collective-permute-start(bf16[2048,512]{1,0:T(8,128)(2,1)S(1)} %bitcast.17), channel_id=1, source_target_pairs={{0,4},{4,0},{8,12},{12,8},{1,5},{5,1},{9,13},{13,9},{2,6},{6,2},{1... | collective-permute-start | bytes 6291464 | tf_op jit(solution)/shard_map/ppermute | solution.py:318
  110.4 13.5 %collective-permute-start.6 = (bf16[1024,1024]{1,0:T(8,128)(2,1)}, bf16[1024,1024]{1,0:T(8,128)(2,1)S(1)}, u32[]{:S(2)}, u32[]{:S(2)}) collective-permute-start(bf16[1024,1024]{1,0:T(8,128)(2,1)} %collective-permute-done.refs_5_), channel_id=1, source_target_pairs={{0,4},{4,0},{8,12},{12,8},{1,5},{5,1},{9,13},{13,9},{2,6},{6,2},{1... | collective-permute-start | bytes 6291464 | tf_op jit(solution)/shard_map/ppermute | solution.py:318
  111.8 12.1 %collective-permute-start.10 = (bf16[2048,512]{1,0:T(8,128)(2,1)S(1)}, bf16[2048,512]{1,0:T(8,128)(2,1)S(1)}, u32[]{:S(2)}, u32[]{:S(2)}) collective-permute-start(bf16[2048,512]{1,0:T(8,128)(2,1)S(1)} %collective-permute-done.9.refs_11_), channel_id=1, source_target_pairs={{0,4},{4,0},{8,12},{12,8},{1,5},{5,1},{9,13},{13,9},{2,6},{6,2},{1... | collective-permute-start | bytes 6291464 | tf_op jit(solution)/shard_map/ppermute | solution.py:318
  122.3 1.6 copy-start.1
  122.3 4.2 %collective-permute-start.7 = (bf16[1024,1024]{1,0:T(8,128)(2,1)S(1)}, bf16[1024,1024]{1,0:T(8,128)(2,1)S(1)}, u32[]{:S(2)}, u32[]{:S(2)}) collective-permute-start(bf16[1024,1024]{1,0:T(8,128)(2,1)S(1)} %collective-permute-done.5.refs_6_), channel_id=1, source_target_pairs={{0,4},{4,0},{8,12},{12,8},{1,5},{5,1},{9,13},{13,9},{2,6},{6,2},{1... | collective-permute-start | bytes 6291464 | tf_op jit(solution)/shard_map/ppermute | solution.py:318
  122.4 33.4 %collective-permute-start.11 = (bf16[320,2048]{1,0:T(8,128)(2,1)S(1)}, bf16[320,2048]{1,0:T(8,128)(2,1)S(1)}, u32[]{:S(2)}, u32[]{:S(2)}) collective-permute-start(bf16[320,2048]{1,0:T(8,128)(2,1)S(1)} %slice.61), channel_id=1, source_target_pairs={{0,1},{1,2},{2,3},{3,0},{4,5},{5,6},{6,7},{7,4},{8,9},{9,10},{10,1... | collective-permute-start | bytes 3932168 | tf_op jit(solution)/shard_map/ppermute | solution.py:324
  123.9 2.0 copy-start.5
  123.9 48.9 %collective-permute-start.12 = (bf16[192,2048]{1,0:T(8,128)(2,1)S(1)}, bf16[192,2048]{1,0:T(8,128)(2,1)S(1)}, u32[]{:S(2)}, u32[]{:S(2)}) collective-permute-start(bf16[192,2048]{1,0:T(8,128)(2,1)S(1)} %slice.62), channel_id=1, source_target_pairs={{0,1},{1,2},{2,3},{3,0},{4,5},{5,6},{6,7},{7,4},{8,9},{9,10},{10,1... | collective-permute-start | bytes 2359304 | tf_op jit(solution)/shard_map/ppermute | solution.py:324
  159.6 17.5 %collective-permute-start.16 = (bf16[320,1024]{1,0:T(8,128)(2,1)S(1)}, bf16[320,1024]{1,0:T(8,128)(2,1)S(1)}, u32[]{:S(2)}, u32[]{:S(2)}) collective-permute-start(bf16[320,1024]{1,0:T(8,128)(2,1)S(1)} %get-tuple-element.59.refs_0_), channel_id=1, source_target_pairs={{0,8},{4,12},{8,0},{12,4},{1,9},{5,13},{9,1},{13,5},{2,10},{6,14},... | collective-permute-start | bytes 1966088 | tf_op jit(solution)/shard_map/ppermute | solution.py:318
  162.0 21.5 %collective-permute-start.3 = (bf16[128,2048]{1,0:T(8,128)(2,1)S(1)}, bf16[128,2048]{1,0:T(8,128)(2,1)S(1)}, u32[]{:S(2)}, u32[]{:S(2)}) collective-permute-start(bf16[128,2048]{1,0:T(8,128)(2,1)S(1)} %slice.60), channel_id=1, source_target_pairs={{0,1},{1,2},{2,3},{3,0},{4,5},{5,6},{6,7},{7,4},{8,9},{9,10},{10,1... | collective-permute-start | bytes 1572872 | tf_op jit(solution)/shard_map/ppermute | solution.py:324
  175.8 10.4 %collective-permute-start.19 = (bf16[192,1024]{1,0:T(8,128)(2,1)S(1)}, bf16[192,1024]{1,0:T(8,128)(2,1)S(1)}, u32[]{:S(2)}, u32[]{:S(2)}) collective-permute-start(bf16[192,1024]{1,0:T(8,128)(2,1)S(1)} %get-tuple-element.60.refs_4_), channel_id=1, source_target_pairs={{0,8},{4,12},{8,0},{12,4},{1,9},{5,13},{9,1},{13,5},{2,10},{6,14},... | collective-permute-start | bytes 1179656 | tf_op jit(solution)/shard_map/ppermute | solution.py:318
  177.1 10.6 %collective-permute-start.15 = (bf16[320,1024]{1,0:T(8,128)(2,1)S(1)}, bf16[320,1024]{1,0:T(8,128)(2,1)S(1)}, u32[]{:S(2)}, u32[]{:S(2)}) collective-permute-start(bf16[320,1024]{1,0:T(8,128)(2,1)S(1)} %get-tuple-element.59.refs_0_), channel_id=1, source_target_pairs={{0,4},{4,0},{8,12},{12,8},{1,5},{5,1},{9,13},{13,9},{2,6},{6,2},{1... | collective-permute-start | bytes 1966088 | tf_op jit(solution)/shard_map/ppermute | solution.py:318
  177.1 10.8 %collective-permute-start.17 = (bf16[320,1024]{1,0:T(8,128)(2,1)S(1)}, bf16[320,1024]{1,0:T(8,128)(2,1)S(1)}, u32[]{:S(2)}, u32[]{:S(2)}) collective-permute-start(bf16[320,1024]{1,0:T(8,128)(2,1)S(1)} %collective-permute-done.16.refs_2_), channel_id=1, source_target_pairs={{0,4},{4,0},{8,12},{12,8},{1,5},{5,1},{9,13},{13,9},{2,6},{6,2},{1... | collective-permute-start | bytes 1966088 | tf_op jit(solution)/shard_map/ppermute | solution.py:318
  177.6 9.9 %collective-permute-start.18 = (bf16[192,1024]{1,0:T(8,128)(2,1)S(1)}, bf16[192,1024]{1,0:T(8,128)(2,1)S(1)}, u32[]{:S(2)}, u32[]{:S(2)}) collective-permute-start(bf16[192,1024]{1,0:T(8,128)(2,1)S(1)} %get-tuple-element.60.refs_4_), channel_id=1, source_target_pairs={{0,4},{4,0},{8,12},{12,8},{1,5},{5,1},{9,13},{13,9},{2,6},{6,2},{1... | collective-permute-start | bytes 1179656 | tf_op jit(solution)/shard_map/ppermute | solution.py:318
  186.2 1.7 collective-permute-start.20
  186.2 8.7 %collective-permute-start.14 = (bf16[128,1024]{1,0:T(8,128)(2,1)S(1)}, bf16[128,1024]{1,0:T(8,128)(2,1)S(1)}, u32[]{:S(2)}, u32[]{:S(2)}) collective-permute-start(bf16[128,1024]{1,0:T(8,128)(2,1)S(1)} %get-tuple-element.57.refs_8_), channel_id=1, source_target_pairs={{0,8},{4,12},{8,0},{12,4},{1,9},{5,13},{9,1},{13,5},{2,10},{6,14},... | collective-permute-start | bytes 786440 | tf_op jit(solution)/shard_map/ppermute | solution.py:318
  187.5 7.4 %collective-permute-start.13 = (bf16[128,1024]{1,0:T(8,128)(2,1)S(1)}, bf16[128,1024]{1,0:T(8,128)(2,1)S(1)}, u32[]{:S(2)}, u32[]{:S(2)}) collective-permute-start(bf16[128,1024]{1,0:T(8,128)(2,1)S(1)} %get-tuple-element.57.refs_8_), channel_id=1, source_target_pairs={{0,4},{4,0},{8,12},{12,8},{1,5},{5,1},{9,13},{13,9},{2,6},{6,2},{1... | collective-permute-start | bytes 786440 | tf_op jit(solution)/shard_map/ppermute | solution.py:318
  194.9 1.5 collective-permute-start.21
